TPU v7x, 128 devices: a whole 4x4x4 slice. The times are simulated.
128 devices in a mesh: branch: 16 (over z_hi, x, core), seq: 8 (over z_lo, y).
Axes of the slice: x: 4, y: 4, z: 4 (z_hi: 2, z_lo: 2; z = z_hi * 2 + z_lo), core: 2. Of those that a mesh axis runs over, the one named last changes fastest.
Arguments:
- frame_tokens: bfloat16 [32, 256, 5120], P('branch', 'seq'), may hold values from -6 to 6
- actions: int32 [32], P('branch'), may hold values from 0 to 15
- visible_from: int32 [32], P('branch'), may hold values from 0 to 16
- action_modulation_table: bfloat16 [16, 3, 5120], replicated, may hold values from -3 to 3
- w_qkv: bfloat16 [5120, 3, 3072], P(None, None, 'seq'), may hold values from -0.078125 to 0.078125
- w_out: bfloat16 [3072, 5120], P('seq'), may hold values from -0.109375 to 0.109375
- ctx_kv: bfloat16 [2, 8192, 3072], P(None, 'branch', 'seq'), may hold values from -400 to 400
Outputs:
- layer_out: bfloat16 [32, 256, 5120], P('branch', 'seq')
Inputs may be any that keep to these rules, and one draw needn't show every extreme that they name: Branch b attends to the context frames visible_from[b] to 31 and always to its own frame.
All inputs are finite; a program needn't handle non-finite values.
Results may differ from a plain program's by a relative error of at most 0.0085.
Values may be sent and summed in bfloat16 or wider, within the bound.
No kernel may reach another device: no remote copies, remote signals or barrier semaphores. Data moves between devices by JAX's collectives and lax.ppermute only.
A program may use at most 128 MiB of HBM per device.

v0:
```python
import jax
import jax.numpy as jnp
from jax import lax
from jax.sharding import PartitionSpec as P

HDIM = 128
ACTIONS = 16
FRAME_TOK = 256


def layer_norm(value_rows):
    value_rows = value_rows.astype(jnp.float32)
    mean = jnp.mean(value_rows, axis=-1, keepdims=True)
    centred = value_rows - mean
    variance = jnp.mean(centred * centred, axis=-1, keepdims=True)
    return centred / jnp.sqrt(variance + 1e-06)


def attend(carry, queries, keys, vals, valid):
    top, total, accum = carry
    attention_logits = jnp.einsum(
        "bqhd,khd->bhqk", queries, keys, preferred_element_type=jnp.float32
    ) * HDIM ** (-0.5)
    mask = valid[:, None, None, :]
    attention_logits = jnp.where(mask, attention_logits, -1e30)
    updated_running_max = jnp.maximum(top, jnp.max(attention_logits, axis=-1))
    expo = jnp.where(mask, jnp.exp(attention_logits - updated_running_max[..., None]), 0.0)
    factor = jnp.exp(top - updated_running_max)
    total = total * factor + jnp.sum(expo, axis=-1)
    accum = accum * factor[..., None] + jnp.einsum(
        "bhqk,khd->bhqd", expo.astype(jnp.bfloat16), vals, preferred_element_type=jnp.float32
    )
    return (updated_running_max, total, accum)


def shards(frame_tokens, actions, visible_from, action_modulation_table, w_qkv, w_out, ctx_kv):
    branches = frame_tokens.shape[0]
    local_width = w_qkv.shape[2]
    heads_here = local_width // HDIM
    action_indicator = (actions[:, None] == jnp.arange(ACTIONS, dtype=jnp.int32)[None, :]).astype(
        jnp.bfloat16
    )
    action_shift_scale = jnp.einsum(
        "wn,nlg->wlg", action_indicator, action_modulation_table, preferred_element_type=jnp.float32
    )
    hidden = (
        layer_norm(frame_tokens) * (1.0 + action_shift_scale[:, 1][:, None, :])
        + action_shift_scale[:, 0][:, None, :]
    ).astype(jnp.bfloat16)
    qkv = jnp.einsum(
        "btd,dkh->btkh",
        lax.all_gather(hidden, "seq", axis=1, tiled=True),
        w_qkv,
        preferred_element_type=jnp.float32,
    ).astype(jnp.bfloat16)
    frame_len = qkv.shape[1]
    queries = qkv[:, :, 0].reshape(branches, frame_len, heads_here, HDIM)
    own_keys = qkv[:, :, 1].reshape(branches, frame_len, heads_here, HDIM)
    own_vals = qkv[:, :, 2].reshape(branches, frame_len, heads_here, HDIM)
    attention_logits = jnp.einsum(
        "bqhd,bkhd->bhqk", queries, own_keys, preferred_element_type=jnp.float32
    ) * HDIM ** (-0.5)
    top = jnp.max(attention_logits, axis=-1)
    expo = jnp.exp(attention_logits - top[..., None])
    total = jnp.sum(expo, axis=-1)
    accum = jnp.einsum(
        "bhqk,bkhd->bhqd", expo.astype(jnp.bfloat16), own_vals, preferred_element_type=jnp.float32
    )
    carry = (top, total, accum)
    context = lax.all_gather(ctx_kv, "branch", axis=1, tiled=True)
    length = context.shape[1]
    block = 512
    count = length // block

    def advance(index, inner):
        part_kv = lax.dynamic_slice_in_dim(context, index * block, block, 1)
        keys = part_kv[0].reshape(block, heads_here, HDIM)
        vals = part_kv[1].reshape(block, heads_here, HDIM)
        frame = (index * block + jnp.arange(block, dtype=jnp.int32)) // FRAME_TOK
        valid = frame[None, :] >= visible_from[:, None]
        return attend(inner, queries, keys, vals, valid)

    carry = lax.fori_loop(0, count, advance, carry)
    top, total, accum = carry
    attended = (accum / total[..., None]).astype(jnp.bfloat16)
    attended = jnp.transpose(attended, (2, 0, 1, 3)).reshape(frame_len, branches, local_width)
    projected = lax.psum_scatter(
        jnp.einsum("tbh,hd->tbd", attended, w_out, preferred_element_type=jnp.float32).astype(
            jnp.bfloat16
        ),
        "seq",
        scatter_dimension=0,
        tiled=True,
    ).astype(jnp.float32)
    projected = jnp.transpose(projected, (1, 0, 2))
    result = frame_tokens.astype(jnp.float32) + action_shift_scale[:, 2][:, None, :] * projected
    return result.astype(jnp.bfloat16)


def solution(mesh):
    in_specs = (
        P("branch", "seq", None),
        P("branch"),
        P("branch"),
        P(),
        P(None, None, "seq"),
        P("seq", None),
        P(None, "branch", "seq"),
    )
    out_specs = P("branch", "seq", None)
    return jax.shard_map(shards, mesh=mesh, in_specs=in_specs, out_specs=out_specs, check_vma=False)
```

profile of v0, /device:TPU:28, one launch (start us, length us, event | category | flops | bytes accessed | tf_op | source)
XLA Modules:
  0.0 325.7 jit_solution(13895122458595489936)
XLA Ops:
  6.5 1.4 convert_reduce_fusion
  7.9 1.4 fusion.31
  10.3 2.2 fusion.34
  12.6 1.2 copy.42
  13.9 61.1 %all-gather.3.cloned.1.call-done = bf16[2,256,5120]{2,1,0:T(8,128)(2,1)} async-done(((bf16[2,32,5120]{2,1,0:T(8,128)(2,1)}), bf16[2,256,5120]{2,1,0:T(8,128)(2,1)}) %all-gather.3.cloned.1.call-update) | async-done | bytes 5242896 | tf_op jit(solution)/shard_map/all_gather | solution.py:52
  75.0 10.7 %fusion.24 = bf16[2,256,3,384]{3,1,2,0:T(8,128)(2,1)S(1)} fusion(bf16[5120,3,384]{2,0,1:T(8,128)(2,1)} %param.13, bf16[2,256,5120]{2,1,0:T(8,128)(2,1)} %all-gather.3.cloned.1.call-done), kind=kOutput, calls=%fused_computation.37 | convolution fusion | flops 6040387584 | bytes 18219008 | tf_op jit(solution)/shard_map/btd,dkh->btkh/dot_general | solution.py:50
  87.7 90.3 %all-gather.5.cloned.1.call-done = bf16[2,8192,384]{1,2,0:T(8,128)(2,1)} async-done(((bf16[2,512,384]{1,2,0:T(8,128)(2,1)}), bf16[2,8192,384]{1,2,0:T(8,128)(2,1)}) %all-gather.5.cloned.1.call-update) | async-done | bytes 12582928 | tf_op jit(solution)/shard_map/all_gather | solution.py:70
  178.0 70.9 %while.19 = (s32[]{:T(128)}, f32[2,3,256]{2,0,1:T(2,128)S(1)}, f32[2,3,256]{2,0,1:T(2,128)S(1)}, f32[2,3,256,128]{2,3,0,1:T(8,128)S(1)}, s32[2]{0:T(128)S(1)}, /...) while((s32[]{:T(128)}, f32[2,3,256]{2,0,1:T(2,128)S(1)}, ...), condition=%wide.region_7.8_spmd, body=%wide.region_4.7_spmd.sunk | while | flops 413282304 | bytes 13869251 | solution.py:83
  178.1 1.2 constant_dynamic-slice_fusion.3
  181.1 1.3 fusion.68
  185.6 1.3 fusion.68
  187.0 1.2 constant_dynamic-slice_fusion.3
  190.0 1.3 fusion.68
  194.4 1.3 fusion.68
  195.9 1.2 constant_dynamic-slice_fusion.3
  198.9 1.3 fusion.68
  203.3 1.3 fusion.68
  207.7 1.3 fusion.68
  212.2 1.3 fusion.68
  213.6 1.2 constant_dynamic-slice_fusion.3
  216.6 1.3 fusion.68
  218.0 1.2 constant_dynamic-slice_fusion.3
  221.0 1.3 fusion.68
  225.5 1.3 fusion.68
  229.9 1.3 fusion.68
  234.3 1.3 fusion.68
  238.8 1.3 fusion.68
  243.2 1.3 fusion.68
  247.6 1.3 fusion.68
  249.0 6.8 %convolution_convert_fusion = bf16[256,2,5120]{2,0,1:T(8,128)(2,1)} fusion(bf16[256,2,384]{0,2,1:T(8,128)(2,1)S(1)} %bitcast.90, bf16[384,5120]{1,0:T(8,128)(2,1)} %param.14), kind=kOutput, calls=%fused_computation.28 | convolution fusion | flops 2015887360 | bytes 9568256 | tf_op jit(solution)/shard_map/tbh,hd->tbd/dot_general | solution.py:88
  255.9 61.1 %reduce-scatter.2.cloned.1.call-done = bf16[32,2,5120]{2,0,1:T(8,128)(2,1)} async-done(((bf16[256,2,5120]{2,0,1:T(8,128)(2,1)}), bf16[32,2,5120]{2,0,1:T(8,128)(2,1)}) %reduce-scatter.2.cloned.1.call-update) | async-done | bytes 655376 | tf_op jit(solution)/shard_map/reduce_scatter | solution.py:87
  317.0 2.2 fusion.35
  (153 shorter events, 46.5 us)
Async XLA Ops:
  6.5 2.8 copy-start
  6.5 6.1 %copy-start.2 = (bf16[2,512,384]{2,1,0:T(8,128)(2,1)S(1)}, bf16[2,512,384]{2,1,0:T(8,128)(2,1)}, u32[]{:S(2)}) copy-start(bf16[2,512,384]{2,1,0:T(8,128)(2,1)} %param.15) | copy-start | bytes 2359300
  6.5 68.5 %all-gather.3.cloned.1.call-start = ((), (), s32[]{:S(2)}) async-start(), calls=%async_computation.1 | async-start | bytes 5898240 | tf_op jit(solution)/shard_map/all_gather | solution.py:52
  12.6 165.5 %all-gather.5.cloned.1.call-start = ((), (), s32[]{:S(2)}) async-start(), calls=%async_computation.2 | async-start | bytes 13369344 | tf_op jit(solution)/shard_map/all_gather | solution.py:70
  13.9 303.1 %reduce-scatter.2.cloned.1.call-start = ((), (), s32[]{:S(2)}) async-start(), calls=%async_computation.3 | async-start | bytes 5898240 | tf_op jit(solution)/shard_map/reduce_scatter | solution.py:87
  86.7 91.3 %copy-start.3 = (s32[2]{0:T(128)S(1)}, s32[2]{0:T(128)}, u32[]{:S(2)}) copy-start(s32[2]{0:T(128)} %param.11) | copy-start | bytes 28
  255.9 61.1 %copy-start.1 = (bf16[2,32,5120]{2,1,0:T(8,128)(2,1)S(1)}, bf16[2,32,5120]{2,1,0:T(8,128)(2,1)}, u32[]{:S(2)}) copy-start(bf16[2,32,5120]{2,1,0:T(8,128)(2,1)} %param.9) | copy-start | bytes 1966084
Sparse Core Ops, SparseCore 0:
  12.7 62.2 all-gather.2
  77.3 100.6 all-gather.4
  256.0 60.9 reduce-scatter.1
where the time goes:
time: 330 us; the launch traced here: 326 us
  waiting for transfers between devices  213 us (65%)
  matrix products  55.3 us (17%)
  other arithmetic  22.6 us (7%)
  local copies, waits for them, and re-layouts  20.9 us (6%)
  between operations  13.2 us (4%)
    all_gather x1, waiting for transfers between devices, shards(): context = lax.all_gather(ctx_kv, 'branch', axis=1, tiled=True)  90.3 us
    reduce_scatter x1, waiting for transfers between devices, shards(): lax.psum_scatter(jnp.einsum('tbh,hd->tbd', attended, w_out, preferred_ele...  61.1 us
    all_gather x1, waiting for transfers between devices, shards(): lax.all_gather(hidden, 'seq', axis=1, tiled=True)  61.1 us
    dot_general x16, matrix products, attend(): jnp.einsum('bhqk,khd->bhqd', expo.astype(jnp.bfloat16), vals, preferred_e...  20.6 us
    slice x16, local copies, waits for them, and re-layouts, advance(): vals = part_kv[1].reshape(block, heads_here, HDIM)  18.7 us
    dot_general x16, matrix products, attend(): jnp.einsum('bqhd,khd->bhqk', queries, keys, preferred_element_type=jnp.fl...  15.5 us
    reduce_sum x16, other arithmetic, attend(): total = total * factor + jnp.sum(expo, axis=-1)  13.2 us
    dot_general x1, matrix products, shards(): jnp.einsum('btd,dkh->btkh', lax.all_gather(hidden, 'seq', axis=1, tiled=T...  10.7 us
  transfers between devices with their start and end apart: 3, of which 3 were waited for; matrix products, arithmetic and copies ran while one was open for 4% of the time, Pallas kernels for 0%

commit v1 on v0

v1 whole, which is shorter than its diff:
```python
import functools
import math

import jax
import jax.numpy as jnp
from jax import lax
from jax.experimental import pallas as pl
from jax.experimental.pallas import tpu as pltpu
from jax.sharding import PartitionSpec as P

HDIM = 128
ACTIONS = 16
FRAME_TOK = 256
HERE = 3
WIDTH = HERE * HDIM
SCALE2 = math.log2(math.e) * HDIM ** (-0.5)
MASKED = -1e30
VMEM = pl.BlockSpec(memory_space=pltpu.VMEM)
SMEM = pl.BlockSpec(memory_space=pltpu.SMEM)
ANY = pl.BlockSpec(memory_space=pl.ANY)


def along_seq(a, dy=0, dz=0):
    perm = [
        (z * 4 + y, (z + dz) % 2 * 4 + (y + dy) % 4) for z in range(2) for y in range(4)
    ]
    return lax.ppermute(a, "seq", perm)


def along_branch(a, dx=0, dz=0, dc=0):
    perm = [
        ((z * 4 + x) * 2 + c, ((z + dz) % 2 * 4 + (x + dx) % 4) * 2 + (c + dc) % 2)
        for z in range(2)
        for x in range(4)
        for c in range(2)
    ]
    return lax.ppermute(a, "branch", perm)


def across_z(a):
    perm = []
    for b in range(16):
        for s in range(8):
            perm.append((b * 8 + s, (b + 8) % 16 * 8 + (s + 4) % 8))
    return lax.ppermute(a, ("branch", "seq"), perm)


def norm_kernel(actions, x_ref, table_ref, hidden_ref, gate_ref):
    rows = lax.broadcasted_iota(jnp.int32, (ACTIONS, 1), 0)
    for b in range(x_ref.shape[0]):
        pick = rows == actions[b]
        shift, scale, gate = (
            jnp.sum(
                jnp.where(pick, table_ref[c].astype(jnp.float32), 0.0), axis=0, keepdims=True
            )
            for c in range(3)
        )
        gate_ref[b] = gate
        x = x_ref[b].astype(jnp.float32)
        centred = x - jnp.mean(x, axis=-1, keepdims=True)
        variance = jnp.mean(centred * centred, axis=-1, keepdims=True)
        normed = centred * (1.0 / jnp.sqrt(variance + 1e-06))
        hidden_ref[b] = (normed * (1.0 + scale) + shift).astype(jnp.bfloat16)


def norm(actions, x, table):
    return pl.pallas_call(
        norm_kernel,
        out_shape=(
            jax.ShapeDtypeStruct(x.shape, jnp.bfloat16),
            jax.ShapeDtypeStruct((x.shape[0], 1, x.shape[2]), jnp.float32),
        ),
        in_specs=[SMEM, VMEM, VMEM],
        out_specs=(VMEM, VMEM),
        compiler_params=pltpu.CompilerParams(vmem_limit_bytes=24 << 20),
    )(actions, x, table)


def qkv_kernel(count, *refs):
    shards, w_ref, outs, acc = refs[:count], refs[count], refs[count + 1 : count + 4], refs[-1]
    step = pl.program_id(0)
    x = jnp.concatenate([s[b] for b in range(2) for s in shards], axis=0)

    @pl.when(step == 0)
    def _():
        acc[...] = jnp.zeros_like(acc)

    for c in range(3):
        acc[c] += jnp.dot(x, w_ref[c], preferred_element_type=jnp.float32)

    @pl.when(step == pl.num_programs(0) - 1)
    def _():
        rows = count * 32
        for c in range(3):
            for b in range(2):
                outs[c][b] = acc[c, b * rows : (b + 1) * rows].astype(jnp.bfloat16)


def project_qkv(shards, w):
    count, depth, block = len(shards), w.shape[1], 1024
    rows = count * 32
    out = jax.ShapeDtypeStruct((2, rows, WIDTH), jnp.bfloat16)
    return pl.pallas_call(
        functools.partial(qkv_kernel, count),
        grid=(depth // block,),
        out_shape=(out,) * 3,
        in_specs=[pl.BlockSpec((2, 32, block), lambda i: (0, 0, i))] * count
        + [pl.BlockSpec((3, block, WIDTH), lambda i: (0, i, 0))],
        out_specs=(pl.BlockSpec((2, rows, WIDTH), lambda i: (0, 0, 0)),) * 3,
        scratch_shapes=[pltpu.VMEM((3, 2 * rows, WIDTH), jnp.float32)],
        compiler_params=pltpu.CompilerParams(vmem_limit_bytes=32 << 20),
        cost_estimate=pl.CostEstimate(
            flops=2 * 2 * rows * depth * 3 * WIDTH,
            bytes_accessed=depth * 3 * WIDTH * 2 + 2 * rows * depth * 2,
            transcendentals=0,
        ),
    )(*shards, w)


def attend_kernel(branches, chunk, blocks, own, start_ref, q_ref, frame_ref, *rest):
    if own:
        own_k, own_v, rest = rest[0], rest[1], rest[2:]
    parts, o_ref, stat_ref, kv, top_s, sum_s, acc_s, sems = rest[:blocks], *rest[blocks:]
    copies = [
        pltpu.make_async_copy(parts[i], kv.at[:, pl.ds(i * 512, 512)], sems.at[i])
        for i in range(blocks)
    ]
    for copy in copies:
        copy.start()

    def block_step(b, h, k, v, bias, first):
        q = q_ref[b, :, h * HDIM : (h + 1) * HDIM]
        s = lax.dot_general(q, k, (((1,), (1,)), ((), ())), preferred_element_type=jnp.float32)
        s = s * SCALE2
        if bias is not None:
            s = s + bias
        top = jnp.max(s, axis=1, keepdims=True)
        if first:
            new = jnp.broadcast_to(top, (FRAME_TOK, HDIM))
        else:
            old = top_s[b, h]
            new = jnp.maximum(old, top)
        p = jnp.exp2(s - new[:, :1])
        sums = p[:, :HDIM]
        for j in range(1, p.shape[1] // HDIM):
            sums = sums + p[:, j * HDIM : (j + 1) * HDIM]
        pv = jnp.dot(p.astype(jnp.bfloat16), v, preferred_element_type=jnp.float32)
        if first:
            sum_s[b, h] = sums
            acc_s[b, h] = pv
        else:
            factor = jnp.exp2(old - new)
            sum_s[b, h] = sum_s[b, h] * factor + sums
            acc_s[b, h] = acc_s[b, h] * factor + pv
        top_s[b, h] = new

    if own:
        for b in range(branches):
            for h in range(HERE):
                cols = slice(h * HDIM, (h + 1) * HDIM)
                block_step(b, h, own_k[b, :, cols], own_v[b, :, cols], None, True)
    else:
        top_s[...] = jnp.full_like(top_s[...], 2 * MASKED)
        sum_s[...] = jnp.zeros_like(sum_s[...])
        acc_s[...] = jnp.zeros_like(acc_s[...])
    for copy in copies:
        copy.wait()

    def loop(i, _):
        rows = pl.ds(pl.multiple_of(i * chunk, chunk), chunk)
        for b in range(branches):
            bias = jnp.where(frame_ref[pl.ds(i, 1), :] >= start_ref[b], 0.0, MASKED)
            for h in range(HERE):
                cols = slice(h * HDIM, (h + 1) * HDIM)
                block_step(b, h, kv[0, rows, cols], kv[1, rows, cols], bias, False)
        return 0

    lax.fori_loop(0, blocks * 512 // chunk, loop, 0)
    lane = lax.broadcasted_iota(jnp.int32, (FRAME_TOK, HDIM), 1)
    for b in range(branches):
        stats = jnp.zeros((FRAME_TOK, HDIM), jnp.float32)
        for h in range(HERE):
            total = jnp.sum(sum_s[b, h], axis=1, keepdims=True)
            o_ref[b, :, h * HDIM : (h + 1) * HDIM] = (acc_s[b, h] / total).astype(o_ref.dtype)
            left = top_s[b, h] + jnp.log2(total)
            for part in range(3):
                piece = left.astype(jnp.bfloat16).astype(jnp.float32)
                stats = jnp.where(lane == h * 3 + part, piece, stats)
                left = left - piece
        stat_ref[b] = stats.astype(jnp.bfloat16)


def attend(start, q, frames, parts, own=None, dtype=jnp.bfloat16):
    branches, blocks, chunk = q.shape[0], len(parts), 2048
    state = pltpu.VMEM((branches, HERE, FRAME_TOK, HDIM), jnp.float32)
    return pl.pallas_call(
        functools.partial(attend_kernel, branches, chunk, blocks, own is not None),
        out_shape=(
            jax.ShapeDtypeStruct((branches, FRAME_TOK, WIDTH), dtype),
            jax.ShapeDtypeStruct((branches, FRAME_TOK, HDIM), jnp.bfloat16),
        ),
        in_specs=[SMEM, VMEM, VMEM] + ([VMEM, VMEM] if own else []) + [ANY] * blocks,
        out_specs=(VMEM, VMEM),
        scratch_shapes=[
            pltpu.VMEM((2, blocks * 512, WIDTH), jnp.bfloat16),
            state,
            state,
            state,
            pltpu.SemaphoreType.DMA((blocks,)),
        ],
        compiler_params=pltpu.CompilerParams(vmem_limit_bytes=40 << 20),
        cost_estimate=pl.CostEstimate(
            flops=8 * branches * FRAME_TOK * blocks * 512 * WIDTH,
            bytes_accessed=blocks * 512 * WIDTH * 4,
            transcendentals=branches * FRAME_TOK * blocks * 512 * HERE,
        ),
    )(start, q, frames.reshape(-1, chunk), *(own or ()), *parts)


def log_sums(stats):
    s = stats[..., : 3 * HERE].astype(jnp.float32)
    return s.reshape(s.shape[:-1] + (HERE, 3)).sum(-1)


def out_kernel(a_ref, b_ref, wa_ref, wb_ref, o_ref):
    rows = a_ref.shape[1]
    for b in range(2):
        o_ref[b] = (
            jnp.dot(a_ref[b], wa_ref[...], preferred_element_type=jnp.float32)
            + jnp.dot(b_ref[b], wb_ref[...], preferred_element_type=jnp.float32)
        ).astype(jnp.bfloat16)


def project_out(a, b, wa, wb):
    rows, width, block = a.shape[1], wa.shape[1], 512
    return pl.pallas_call(
        out_kernel,
        grid=(width // block,),
        out_shape=jax.ShapeDtypeStruct((2, rows, width), jnp.bfloat16),
        in_specs=[
            pl.BlockSpec((2, rows, WIDTH), lambda i: (0, 0, 0)),
            pl.BlockSpec((2, rows, WIDTH), lambda i: (0, 0, 0)),
            pl.BlockSpec((WIDTH, block), lambda i: (0, i)),
            pl.BlockSpec((WIDTH, block), lambda i: (0, i)),
        ],
        out_specs=pl.BlockSpec((2, rows, block), lambda i: (0, 0, i)),
        compiler_params=pltpu.CompilerParams(vmem_limit_bytes=24 << 20),
        cost_estimate=pl.CostEstimate(
            flops=8 * rows * WIDTH * width,
            bytes_accessed=4 * WIDTH * width + 4 * rows * width,
            transcendentals=0,
        ),
    )(a, b, wa, wb)


def shards(x, actions, visible_from, table, w_qkv, w_out, ctx):
    branch = lax.axis_index("branch")
    core, base = branch % 2, branch // 8 * 8
    hidden, gate = norm(actions, x, jnp.transpose(table, (1, 0, 2)))
    w = jnp.transpose(w_qkv, (1, 0, 2))

    a0 = hidden
    a1, a3, b0 = along_seq(a0, 1), along_seq(a0, -1), along_seq(a0, 0, 1)
    a2 = jnp.concatenate([along_seq(a1[:1], 1), along_seq(a3[1:], -1)], axis=0)
    b1, b3 = along_seq(b0, 1), along_seq(b0, -1)
    b2 = along_seq(a2, 0, 1)

    ctx, _ = lax.optimization_barrier((ctx, hidden))
    mine = [ctx, along_branch(ctx, 1), along_branch(ctx, -1), along_branch(ctx, 2)]
    parts = mine + [along_branch(part, 0, 0, 1) for part in mine]
    at = branch // 2 % 4
    order = [base + (at + d) % 4 * 2 + c for c in (core, 1 - core) for d in (0, 3, 1, 2)]
    frames = jnp.stack(order)[:, None] * 2 + jnp.arange(512, dtype=jnp.int32) // FRAME_TOK
    far_start = along_branch(visible_from, 0, 1)

    half = w_out.shape[1] // 2
    near = across_z(lax.dynamic_slice_in_dim(w_out, core * half, half, 1))
    far = along_branch(near, 0, 0, 1)
    w_other = jnp.where(
        core == 0, jnp.concatenate([near, far], 1), jnp.concatenate([far, near], 1)
    )

    first = project_qkv([a0, a1, a3, b0], w)
    second = project_qkv([a2, b1, b3, b2], w)
    q, k, v = (
        jnp.concatenate([f[:, :96], s[:, :32], f[:, 96:], s[:, 32:]], axis=1)
        for f, s in zip(first, second)
    )
    far_q = along_branch(q, 0, 1)
    o_0, s_0 = attend(visible_from[:1], q[:1], frames, parts, (k[:1], v[:1]), jnp.float32)
    far_q, _ = lax.optimization_barrier((far_q, s_0))
    far_o = attend(far_start, far_q, frames, parts)
    packed = along_branch(jnp.concatenate(far_o, axis=2), 0, 1)
    o_1, s_1 = attend(visible_from[1:], q[1:], frames, parts, (k[1:], v[1:]), jnp.float32)
    own_o, own_l = jnp.concatenate([o_0, o_1]), log_sums(jnp.concatenate([s_0, s_1]))
    far_l = log_sums(packed[..., WIDTH:])
    top = jnp.maximum(own_l, far_l)
    own_w, far_w = jnp.exp2(own_l - top), jnp.exp2(far_l - top)
    total = own_w + far_w
    spread = lambda u: jnp.repeat(u / total, HDIM, axis=2)
    attended = (
        own_o * spread(own_w) + packed[..., :WIDTH].astype(jnp.float32) * spread(far_w)
    ).astype(jnp.bfloat16)

    here, there = attended[:, :128], attended[:, 128:]
    other = along_seq(there, 0, 1)
    p2 = project_out(here[:, 96:], other[:, 96:], w_out, w_other)
    down, up = along_seq(p2[:1], -1), along_seq(p2[1:], 1)
    rest = project_out(here[:, :96], other[:, :96], w_out, w_other).astype(jnp.float32)
    p0, p1, p3 = rest[:, :32], rest[:, 32:64], rest[:, 64:]
    p1 = jnp.concatenate([p1[:1] + down.astype(jnp.float32), p1[1:]]).astype(jnp.bfloat16)
    p3 = jnp.concatenate([p3[:1], p3[1:] + up.astype(jnp.float32)]).astype(jnp.bfloat16)
    t1, t3 = along_seq(p1, -1), along_seq(p3, 1)
    projected = p0 + t1.astype(jnp.float32) + t3.astype(jnp.float32)
    return (x.astype(jnp.float32) + gate * projected).astype(jnp.bfloat16)


def solution(mesh):
    in_specs = (
        P("branch", "seq", None),
        P("branch"),
        P("branch"),
        P(),
        P(None, None, "seq"),
        P("seq", None),
        P(None, "branch", "seq"),
    )
    out_specs = P("branch", "seq", None)
    return jax.shard_map(shards, mesh=mesh, in_specs=in_specs, out_specs=out_specs, check_vma=False)
```

time: 330 us -> 166 us (0.50); the launches traced: 326 us -> 166 us
  waiting for transfers between devices: 213 us -> 52.3 us
  Pallas kernels: 0 us -> 56.4 us
  matrix products: 55.3 us -> 0 us
  starting transfers between devices: 0.09 us -> 33.5 us
  other arithmetic: 22.6 us -> 7.78 us
  between operations: 13.2 us -> 0.54 us
  local copies, waits for them, and re-layouts: 20.9 us -> 15.1 us
    all_gather x2 -> x0, waiting for transfers between devices: 151 us -> none  [the longest x1 90.3 us: shards(): context = lax.all_gather(ctx_kv, 'branch', axis=1, tiled=True)]
    reduce_scatter x1 -> x0, waiting for transfers between devices: 61.1 us -> none  [shards(): lax.psum_scatter(jnp.einsum('tbh,hd->tbd', attended, w_out, preferred_ele...]
    pallas_call x0 -> x8, Pallas kernels: none -> 56.4 us  [the longest x3 30.5 us: attend(): pl.pallas_call(functools.partial(attend_kernel, branches, chunk, blocks,...]
    dot_general x37 -> x0, matrix products: 55.3 us -> none  [the longest x16 20.6 us: attend(): jnp.einsum('bhqk,khd->bhqd', expo.astype(jnp.bfloat16), vals, preferred_e...]
    ppermute x0 -> x25, waiting for transfers between devices: none -> 52.3 us  [the longest x13 42.3 us: along_seq(): return lax.ppermute(a, 'seq', perm)]
    ppermute x0 -> x25, starting transfers between devices: none -> 33.5 us  [the longest x13 19.7 us: along_seq(): return lax.ppermute(a, 'seq', perm)]
    slice x20 -> x24, local copies, waits for them, and re-layouts: 19.4 us -> 2.96 us  [the longest x2 1.99 us: shards(): a2 = jnp.concatenate([along_seq(a1[:1], 1), along_seq(a3[1:], -1)], axis=0)]
    reduce_sum x18 -> x2, other arithmetic: 16 us -> 0.05 us  [log_sums(): return s.reshape(s.shape[:-1] + (HERE, 3)).sum(-1)]
  transfers between devices with their start and end apart: 3 -> 25, of which waited for: 3 -> 11; matrix products, arithmetic and copies ran while one was open for 4% -> 6% of each run, Pallas kernels for 0% -> 30%
where the time goes in v1:
time: 166 us
  Pallas kernels  56.4 us (34%)
  waiting for transfers between devices  52.3 us (32%)
  starting transfers between devices  33.5 us (20%)
  local copies, waits for them, and re-layouts  15.1 us (9%)
  other arithmetic  7.78 us (5%)
    ppermute x13, waiting for transfers between devices, along_seq(): return lax.ppermute(a, 'seq', perm)  42.3 us
    pallas_call x3, Pallas kernels, attend(): pl.pallas_call(functools.partial(attend_kernel, branches, chunk, blocks,...  30.5 us
    ppermute x13, starting transfers between devices, along_seq(): return lax.ppermute(a, 'seq', perm)  19.7 us
    pallas_call x2, Pallas kernels, project_qkv(): pl.pallas_call(functools.partial(qkv_kernel, count), grid=(depth // block...  14 us
    ppermute x11, starting transfers between devices, along_branch(): return lax.ppermute(a, 'branch', perm)  11.2 us
    pallas_call x2, Pallas kernels, project_out(): pl.pallas_call(out_kernel, grid=(width // block,), out_shape=jax.ShapeDty...  9.41 us
    unnamed x30, local copies, waits for them, and re-layouts  7.87 us
    ppermute x11, waiting for transfers between devices, along_branch(): return lax.ppermute(a, 'branch', perm)  5.03 us
  transfers between devices with their start and end apart: 25, of which 11 were waited for; matrix products, arithmetic and copies ran while one was open for 6% of the time, Pallas kernels for 30%

profile of v1, /device:TPU:28, one launch (start us, length us, event | category | flops | bytes accessed | tf_op | source)
XLA Modules:
  0.0 165.7 jit_solution(17818480784416607093)
XLA Ops:
  2.8 2.4 %shard_map.73 = (bf16[2,32,5120]{2,1,0:T(8,128)(2,1)}, f32[2,1,5120]{2,1,0:T(1,128)S(1)}) custom-call(s32[2]{0:T(128)S(1)} %copy-done.5, bf16[2,32,5120]{2,1,0:T(8,128)(2,1)S(1)} %copy-done.2, bf16[3,16,5120]{2,1,0:T(8,128)(2,1)S(1)} %bitcast.27), custom_call_target="tpu_custom_call" | custom-call | tf_op jit(solution)/shard_map/pallas_call | solution.py:67
  5.2 1.9 %collective-permute-start.2 = (bf16[2,32,5120]{2,1,0:T(8,128)(2,1)}, bf16[2,32,5120]{2,1,0:T(8,128)(2,1)}, u32[]{:S(2)}, u32[]{:S(2)}) collective-permute-start(bf16[2,32,5120]{2,1,0:T(8,128)(2,1)} %get-tuple-element.22.refs_0_), channel_id=1, source_target_pairs={{0,4},{1,5},{2,6},{3,7},{4,0},{5,1},{6,2},{7,3},{8,12},{9,13},{10,... | collective-permute-start | bytes 1966088 | tf_op jit(solution)/shard_map/ppermute | solution.py:27
  7.9 2.5 %collective-permute-start = (bf16[2,32,5120]{2,1,0:T(8,128)(2,1)}, bf16[2,32,5120]{2,1,0:T(8,128)(2,1)}, u32[]{:S(2)}, u32[]{:S(2)}) collective-permute-start(bf16[2,32,5120]{2,1,0:T(8,128)(2,1)} %get-tuple-element.22.refs_0_), channel_id=1, source_target_pairs={{0,1},{1,2},{2,3},{3,0},{4,5},{5,6},{6,7},{7,4},{8,9},{9,10},{10,1... | collective-permute-start | bytes 1966088 | tf_op jit(solution)/shard_map/ppermute | solution.py:27
  10.9 2.2 %collective-permute-start.9 = (bf16[2,512,384]{2,1,0:T(8,128)(2,1)}, bf16[2,512,384]{2,1,0:T(8,128)(2,1)}, u32[]{:S(2)}, u32[]{:S(2)}) collective-permute-start(bf16[2,512,384]{2,1,0:T(8,128)(2,1)} %rest_0_), channel_id=1, source_target_pairs={{0,48},{8,56},{16,0},{24,8},{32,16},{40,24},{48,32},{56,40},{64,11... | collective-permute-start | bytes 2359304 | tf_op jit(solution)/shard_map/ppermute | solution.py:37
  13.3 3.1 %constant_dynamic-slice_fusion = bf16[384,2560]{1,0:T(8,128)(2,1)} fusion(bf16[384,5120]{1,0:T(8,128)(2,1)} %wa_ref.3, s32[]{:T(128)S(6)} %select_n.72), kind=kLoop, calls=%fused_computation.44 | loop fusion | bytes 3932164 | tf_op jit(solution)/shard_map/dynamic_slice | solution.py:277
  16.5 7.7 %collective-permute-done.refs_1_ = bf16[2,32,5120]{2,1,0:T(8,128)(2,1)} collective-permute-done((bf16[2,32,5120]{2,1,0:T(8,128)(2,1)}, bf16[2,32,5120]{2,1,0:T(8,128)(2,1)}, u32[]{:S(2)}, u32[]{:S(2)}) %collective-permute-start) | collective-permute-done | bytes 655392 | tf_op jit(solution)/shard_map/ppermute | solution.py:27
  25.1 3.8 %collective-permute-start.3 = (bf16[1,32,5120]{2,1,0:T(8,128)(2,1)S(1)}, bf16[1,32,5120]{2,1,0:T(8,128)(2,1)S(1)}, u32[]{:S(2)}, u32[]{:S(2)}) collective-permute-start(bf16[1,32,5120]{2,1,0:T(8,128)(2,1)S(1)} %slice.161), channel_id=1, source_target_pairs={{0,1},{1,2},{2,3},{3,0},{4,5},{5,6},{6,7},{7,4},{8,9},{9,10},{10,1... | collective-permute-start | bytes 983048 | tf_op jit(solution)/shard_map/ppermute | solution.py:27
  28.9 1.3 collective-permute-start.8
  31.2 3.2 %collective-permute-done.3 = bf16[1,32,5120]{2,1,0:T(8,128)(2,1)S(1)} collective-permute-done((bf16[1,32,5120]{2,1,0:T(8,128)(2,1)S(1)}, bf16[1,32,5120]{2,1,0:T(8,128)(2,1)S(1)}, u32[]{:S(2)}, u32[]{:S(2)}) %collective-permute-start.3) | collective-permute-done | bytes 327712 | tf_op jit(solution)/shard_map/ppermute | solution.py:27
  34.4 2.6 %collective-permute-start.19 = (bf16[384,2560]{1,0:T(8,128)(2,1)}, bf16[384,2560]{1,0:T(8,128)(2,1)}, u32[]{:S(2)}, u32[]{:S(2)}) collective-permute-start(bf16[384,2560]{1,0:T(8,128)(2,1)} %constant_dynamic-slice_fusion), channel_id=1, source_target_pairs={{0,68},{1,69},{2,70},{3,71},{4,64},{5,65},{6,66},{7,67},{8,76},{9,... | collective-permute-start | bytes 5898248 | tf_op jit(solution)/shard_map/ppermute | solution.py:45
  37.0 6.3 %collective-permute-done.4 = bf16[1,32,5120]{2,1,0:T(8,128)(2,1)S(1)} collective-permute-done((bf16[1,32,5120]{2,1,0:T(8,128)(2,1)S(1)}, bf16[1,32,5120]{2,1,0:T(8,128)(2,1)S(1)}, u32[]{:S(2)}, u32[]{:S(2)}) %collective-permute-start.4) | collective-permute-done | bytes 327712 | tf_op jit(solution)/shard_map/ppermute | solution.py:27
  43.4 3.3 %collective-permute-start.5 = (bf16[2,32,5120]{2,1,0:T(8,128)(2,1)}, bf16[2,32,5120]{2,1,0:T(8,128)(2,1)S(1)}, u32[]{:S(2)}, u32[]{:S(2)}) collective-permute-start(bf16[2,32,5120]{2,1,0:T(8,128)(2,1)} %collective-permute-done.2.refs_3_), channel_id=1, source_target_pairs={{0,1},{1,2},{2,3},{3,0},{4,5},{5,6},{6,7},{7,4},{8,9},{9,10},{10,1... | collective-permute-start | bytes 1966088 | tf_op jit(solution)/shard_map/ppermute | solution.py:27
  47.9 4.3 %copy-done = bf16[5120,3,384]{2,0,1:T(8,128)(2,1)S(1)} copy-done((bf16[5120,3,384]{2,0,1:T(8,128)(2,1)S(1)}, bf16[5120,3,384]{2,0,1:T(8,128)(2,1)}, u32[]{:S(2)}) %copy-start) | copy-done | bytes 11796504
  52.3 7.4 %shard_map.74 = (bf16[2,128,384]{2,1,0:T(8,128)(2,1)S(1)}, bf16[2,128,384]{2,1,0:T(8,128)(2,1)S(1)}, bf16[2,128,384]{2,1,0:T(8,128)(2,1)S(1)}) custom-call(bf16[2,32,5120]{2,1,0:T(8,128)(2,1)} %get-tuple-element.22.refs_0_, bf16[2,32,5120]{2,1,0:T(8,128)(2,1)} %collective-permute-done.refs_1_, bf16[2,32,5120]{2,1,0:T(8,128)(2,1)} %collective-permute-done.1.refs_2_, ...), custom_call_target="tpu_custom_call" | custom-call | flops 3019898880 | bytes 14417920 | tf_op jit(solution)/shard_map/pallas_call | solution.py:103
  60.5 1.7 %collective-permute-done.7.refs_3_ = bf16[2,32,5120]{2,1,0:T(8,128)(2,1)S(1)} collective-permute-done((bf16[2,32,5120]{2,1,0:T(8,128)(2,1)S(1)}, bf16[2,32,5120]{2,1,0:T(8,128)(2,1)S(1)}, u32[]{:S(2)}, u32[]{:S(2)}) %collective-permute-start.7) | collective-permute-done | bytes 655392 | tf_op jit(solution)/shard_map/ppermute | solution.py:27
  62.2 6.7 %shard_map.75 = (bf16[2,128,384]{2,1,0:T(8,128)(2,1)S(1)}, bf16[2,128,384]{2,1,0:T(8,128)(2,1)S(1)}, bf16[2,128,384]{2,1,0:T(8,128)(2,1)S(1)}) custom-call(bf16[2,32,5120]{2,1,0:T(8,128)(2,1)S(1)} %constant_dynamic-update-slice_fusion.refs_0_, bf16[2,32,5120]{2,1,0:T(8,128)(2,1)S(1)} %collective-permute-done.5.refs_1_, ...), custom_call_target="tpu_custom_call" | custom-call | flops 3019898880 | bytes 14417920 | tf_op jit(solution)/shard_map/pallas_call | solution.py:103
  69.3 3.7 %collective-permute-start.16 = (bf16[2,256,384]{2,1,0:T(8,128)(2,1)S(1)}, bf16[2,256,384]{2,1,0:T(8,128)(2,1)S(1)}, u32[]{:S(2)}, u32[]{:S(2)}) collective-permute-start(bf16[2,256,384]{2,1,0:T(8,128)(2,1)S(1)} %pad_maximum_fusion.3), channel_id=1, source_target_pairs={{0,64},{8,72},{16,80},{24,88},{32,96},{40,104},{48,112},{56,120},{... | collective-permute-start | bytes 1179656 | tf_op jit(solution)/shard_map/ppermute | solution.py:37
  73.3 8.3 %shard_map.76 = (f32[1,256,384]{2,1,0:T(8,128)S(1)}, bf16[1,256,128]{2,1,0:T(8,128)(2,1)S(1)}) custom-call(s32[1]{0:T(128)} %get-tuple-element.52.start_ref, bf16[1,256,384]{2,1,0:T(8,128)(2,1)S(1)} %get-tuple-element.48.q_ref, s32[2,2048]{1,0:T(2,128)S(1)} %broadcast_add_fusion.frame_ref, bf16[1,256,384]{2,1,0:T(8,128)(2,1)S(1)} %get-tuple-element.53.rest_0_, ...), custom_call_target="tpu_custom_call" | custom-call | flops 3221225472 | bytes 6291456 | tf_op jit(solution)/shard_map/pallas_call | solution.py:196
  81.6 5.0 %collective-permute-done.19 = bf16[384,2560]{1,0:T(8,128)(2,1)} collective-permute-done((bf16[384,2560]{1,0:T(8,128)(2,1)}, bf16[384,2560]{1,0:T(8,128)(2,1)}, u32[]{:S(2)}, u32[]{:S(2)}) %collective-permute-start.19) | collective-permute-done | bytes 1966112 | tf_op jit(solution)/shard_map/ppermute | solution.py:45
  86.6 14.0 %shard_map.78 = (bf16[2,256,384]{2,1,0:T(8,128)(2,1)S(1)}, bf16[2,256,128]{2,1,0:T(8,128)(2,1)S(1)}) custom-call(s32[2]{0:T(128)S(1)} %collective-permute-done.15.start_ref, bf16[2,256,384]{2,1,0:T(8,128)(2,1)S(1)} %collective-permute-done.16.q_ref, s32[2,2048]{1,0:T(2,128)S(1)} %broadcast_add_fusion.frame_ref, bf16[2,512,384]{2,1,0:T(8,128)(2,1)S(1)} %copy-done.6, ...), custom_call_target="tpu_custom_call" | custom-call | flops 6442450944 | bytes 6291456 | tf_op jit(solution)/shard_map/pallas_call | solution.py:196
  100.7 2.7 %collective-permute-start.17 = (bf16[2,256,512]{2,1,0:T(8,128)(2,1)S(1)}, bf16[2,256,512]{2,1,0:T(8,128)(2,1)S(1)}, u32[]{:S(2)}, u32[]{:S(2)}) collective-permute-start(bf16[2,256,512]{2,1,0:T(8,128)(2,1)S(1)} %pad_maximum_fusion.2), channel_id=1, source_target_pairs={{0,64},{8,72},{16,80},{24,88},{32,96},{40,104},{48,112},{56,120},{... | collective-permute-start | bytes 1572872 | tf_op jit(solution)/shard_map/ppermute | solution.py:37
  103.3 8.3 %shard_map.77 = (f32[1,256,384]{2,1,0:T(8,128)S(1)}, bf16[1,256,128]{2,1,0:T(8,128)(2,1)S(1)}) custom-call(s32[1]{0:T(128)} %get-tuple-element.51.start_ref, bf16[1,256,384]{2,1,0:T(8,128)(2,1)S(1)} %get-tuple-element.47.q_ref, s32[2,2048]{1,0:T(2,128)S(1)} %broadcast_add_fusion.frame_ref, bf16[1,256,384]{2,1,0:T(8,128)(2,1)S(1)} %get-tuple-element.54.rest_0_, ...), custom_call_target="tpu_custom_call" | custom-call | flops 3221225472 | bytes 6291456 | tf_op jit(solution)/shard_map/pallas_call | solution.py:196
  111.8 5.0 %collective-permute-done.17 = bf16[2,256,512]{2,1,0:T(8,128)(2,1)S(1)} collective-permute-done((bf16[2,256,512]{2,1,0:T(8,128)(2,1)S(1)}, bf16[2,256,512]{2,1,0:T(8,128)(2,1)S(1)}, u32[]{:S(2)}, u32[]{:S(2)}) %collective-permute-start.17) | collective-permute-done | bytes 524320 | tf_op jit(solution)/shard_map/ppermute | solution.py:37
  120.1 5.9 %collective-permute-done.18 = bf16[2,128,384]{2,1,0:T(8,128)(2,1)S(1)} collective-permute-done((bf16[2,128,384]{2,1,0:T(8,128)(2,1)S(1)}, bf16[2,128,384]{2,1,0:T(8,128)(2,1)S(1)}, u32[]{:S(2)}, u32[]{:S(2)}) %collective-permute-start.18) | collective-permute-done | bytes 196640 | tf_op jit(solution)/shard_map/ppermute | solution.py:27
  126.1 4.5 %maximum_select_fusion.wb_ref = bf16[384,5120]{1,0:T(8,128)(2,1)S(1)} fusion(bf16[384,2560]{1,0:T(8,128)(2,1)} %collective-permute-done.20, bf16[384,2560]{1,0:T(8,128)(2,1)} %collective-permute-done.19, pred[]{:T(512)S(6)} %eq.14), kind=kLoop, calls=%fused_computation | loop fusion | flops 17694720 | bytes 7864321 | tf_op jit(solution)/shard_map/jit(_where)/select_n | solution.py:279
  130.6 4.5 %shard_map.80 = bf16[2,32,5120]{2,1,0:T(8,128)(2,1)S(1)} custom-call(bf16[2,32,384]{2,1,0:T(8,128)(2,1)S(1)} %slice.176.a_ref, bf16[2,32,384]{2,1,0:T(8,128)(2,1)S(1)} %slice.177.b_ref, bf16[384,5120]{1,0:T(8,128)(2,1)S(1)} %copy-done.1, bf16[384,5120]{1,0:T(8,128)(2,1)S(1)} %maximum_select_fusion.wb_ref), custom_call_target="tpu_custom_call" | custom-call | flops 503316480 | bytes 8519680 | tf_op jit(solution)/shard_map/pallas_call | solution.py:236
  135.1 2.3 %collective-permute-start.21 = (bf16[1,32,5120]{2,1,0:T(8,128)(2,1)S(1)}, bf16[1,32,5120]{2,1,0:T(8,128)(2,1)S(1)}, u32[]{:S(2)}, u32[]{:S(2)}) collective-permute-start(bf16[1,32,5120]{2,1,0:T(8,128)(2,1)S(1)} %get-tuple-element.41), channel_id=1, source_target_pairs={{0,3},{1,0},{2,1},{3,2},{4,7},{5,4},{6,5},{7,6},{8,11},{9,8},{10,9... | collective-permute-start | bytes 983048 | tf_op jit(solution)/shard_map/ppermute | solution.py:27
  137.4 1.5 collective-permute-start.23
  138.9 4.9 %shard_map.79 = bf16[2,96,5120]{2,1,0:T(8,128)(2,1)S(1)} custom-call(bf16[2,96,384]{2,1,0:T(8,128)(2,1)S(1)} %slice.171.a_ref, bf16[2,96,384]{2,1,0:T(8,128)(2,1)S(1)} %slice.173.b_ref, bf16[384,5120]{1,0:T(8,128)(2,1)S(1)} %copy-done.1, bf16[384,5120]{1,0:T(8,128)(2,1)S(1)} %maximum_select_fusion.wb_ref), custom_call_target="tpu_custom_call" | custom-call | flops 1509949440 | bytes 9830400 | tf_op jit(solution)/shard_map/pallas_call | solution.py:236
  146.6 2.3 %collective-permute-start.24 = (bf16[2,32,5120]{2,1,0:T(8,128)(2,1)S(1)}, bf16[2,32,5120]{2,1,0:T(8,128)(2,1)S(1)}, u32[]{:S(2)}, u32[]{:S(2)}) collective-permute-start(bf16[2,32,5120]{2,1,0:T(8,128)(2,1)S(1)} %pad_maximum_fusion.1), channel_id=1, source_target_pairs={{0,1},{1,2},{2,3},{3,0},{4,5},{5,6},{6,7},{7,4},{8,9},{9,10},{10,1... | collective-permute-start | bytes 1966088 | tf_op jit(solution)/shard_map/ppermute | solution.py:27
  149.0 12.2 %collective-permute-done.24 = bf16[2,32,5120]{2,1,0:T(8,128)(2,1)S(1)} collective-permute-done((bf16[2,32,5120]{2,1,0:T(8,128)(2,1)S(1)}, bf16[2,32,5120]{2,1,0:T(8,128)(2,1)S(1)}, u32[]{:S(2)}, u32[]{:S(2)}) %collective-permute-start.24) | collective-permute-done | bytes 655392 | tf_op jit(solution)/shard_map/ppermute | solution.py:27
  161.2 3.3 %collective-permute-done.22 = bf16[2,32,5120]{2,1,0:T(8,128)(2,1)S(1)} collective-permute-done((bf16[2,32,5120]{2,1,0:T(8,128)(2,1)S(1)}, bf16[2,32,5120]{2,1,0:T(8,128)(2,1)S(1)}, u32[]{:S(2)}, u32[]{:S(2)}) %collective-permute-start.22) | collective-permute-done | bytes 655392 | tf_op jit(solution)/shard_map/ppermute | solution.py:27
  (112 shorter events, 16.5 us)
Async XLA Ops:
  2.8 44.6 %copy-start.8 = (s32[2]{0:T(128)S(1)}, s32[2]{0:T(128)}, u32[]{:S(2)}) copy-start(s32[2]{0:T(128)} %param.9) | copy-start | bytes 28
  5.2 29.2 %collective-permute-start.2 = (bf16[2,32,5120]{2,1,0:T(8,128)(2,1)}, bf16[2,32,5120]{2,1,0:T(8,128)(2,1)}, u32[]{:S(2)}, u32[]{:S(2)}) collective-permute-start(bf16[2,32,5120]{2,1,0:T(8,128)(2,1)} %get-tuple-element.22.refs_0_), channel_id=1, source_target_pairs={{0,4},{1,5},{2,6},{3,7},{4,0},{5,1},{6,2},{7,3},{8,12},{9,13},{10,... | collective-permute-start | bytes 1966088 | tf_op jit(solution)/shard_map/ppermute | solution.py:27
  7.1 21.8 %collective-permute-start.1 = (bf16[2,32,5120]{2,1,0:T(8,128)(2,1)}, bf16[2,32,5120]{2,1,0:T(8,128)(2,1)}, u32[]{:S(2)}, u32[]{:S(2)}) collective-permute-start(bf16[2,32,5120]{2,1,0:T(8,128)(2,1)} %get-tuple-element.22.refs_0_), channel_id=1, source_target_pairs={{0,3},{1,0},{2,1},{3,2},{4,7},{5,4},{6,5},{7,6},{8,11},{9,8},{10,9... | collective-permute-start | bytes 1966088 | tf_op jit(solution)/shard_map/ppermute | solution.py:27
  7.9 16.2 %collective-permute-start = (bf16[2,32,5120]{2,1,0:T(8,128)(2,1)}, bf16[2,32,5120]{2,1,0:T(8,128)(2,1)}, u32[]{:S(2)}, u32[]{:S(2)}) collective-permute-start(bf16[2,32,5120]{2,1,0:T(8,128)(2,1)} %get-tuple-element.22.refs_0_), channel_id=1, source_target_pairs={{0,1},{1,2},{2,3},{3,0},{4,5},{5,6},{6,7},{7,4},{8,9},{9,10},{10,1... | collective-permute-start | bytes 1966088 | tf_op jit(solution)/shard_map/ppermute | solution.py:27
  10.4 33.0 %collective-permute-start.10 = (bf16[2,512,384]{2,1,0:T(8,128)(2,1)}, bf16[2,512,384]{2,1,0:T(8,128)(2,1)}, u32[]{:S(2)}, u32[]{:S(2)}) collective-permute-start(bf16[2,512,384]{2,1,0:T(8,128)(2,1)} %rest_0_), channel_id=1, source_target_pairs={{0,32},{8,40},{16,48},{24,56},{32,0},{40,8},{48,16},{56,24},{64,96... | collective-permute-start | bytes 2359304 | tf_op jit(solution)/shard_map/ppermute | solution.py:37
  10.9 35.8 %collective-permute-start.9 = (bf16[2,512,384]{2,1,0:T(8,128)(2,1)}, bf16[2,512,384]{2,1,0:T(8,128)(2,1)}, u32[]{:S(2)}, u32[]{:S(2)}) collective-permute-start(bf16[2,512,384]{2,1,0:T(8,128)(2,1)} %rest_0_), channel_id=1, source_target_pairs={{0,48},{8,56},{16,0},{24,8},{32,16},{40,24},{48,32},{56,40},{64,11... | collective-permute-start | bytes 2359304 | tf_op jit(solution)/shard_map/ppermute | solution.py:37
  13.0 49.2 %slice-start = ((s8[11796480]{0:T(1024)(128)(4,1)}), s8[3407872]{0:T(1024)(128)(4,1)S(1)}, s32[]{:S(2)}) async-start(s8[11796480]{0:T(1024)(128)(4,1)} %bitcast.24), calls=%async_computation | async-start | bytes 6815744
  13.3 15.7 %copy-start.6 = (bf16[2,512,384]{2,1,0:T(8,128)(2,1)S(1)}, bf16[2,512,384]{2,1,0:T(8,128)(2,1)}, u32[]{:S(2)}) copy-start(bf16[2,512,384]{2,1,0:T(8,128)(2,1)} %rest_0_) | copy-start | bytes 2359300
  25.1 9.2 %collective-permute-start.3 = (bf16[1,32,5120]{2,1,0:T(8,128)(2,1)S(1)}, bf16[1,32,5120]{2,1,0:T(8,128)(2,1)S(1)}, u32[]{:S(2)}, u32[]{:S(2)}) collective-permute-start(bf16[1,32,5120]{2,1,0:T(8,128)(2,1)S(1)} %slice.161), channel_id=1, source_target_pairs={{0,1},{1,2},{2,3},{3,0},{4,5},{5,6},{6,7},{7,4},{8,9},{9,10},{10,1... | collective-permute-start | bytes 983048 | tf_op jit(solution)/shard_map/ppermute | solution.py:27
  28.9 30.8 %collective-permute-start.8 = (bf16[2,512,384]{2,1,0:T(8,128)(2,1)S(1)}, bf16[2,512,384]{2,1,0:T(8,128)(2,1)S(1)}, u32[]{:S(2)}, u32[]{:S(2)}) collective-permute-start(bf16[2,512,384]{2,1,0:T(8,128)(2,1)S(1)} %copy-done.6), channel_id=1, source_target_pairs={{0,16},{8,24},{16,32},{24,40},{32,48},{40,56},{48,0},{56,8},{64,80... | collective-permute-start | bytes 2359304 | tf_op jit(solution)/shard_map/ppermute | solution.py:37
  34.4 9.0 %collective-permute-start.4 = (bf16[1,32,5120]{2,1,0:T(8,128)(2,1)S(1)}, bf16[1,32,5120]{2,1,0:T(8,128)(2,1)S(1)}, u32[]{:S(2)}, u32[]{:S(2)}) collective-permute-start(bf16[1,32,5120]{2,1,0:T(8,128)(2,1)S(1)} %slice.162), channel_id=1, source_target_pairs={{0,3},{1,0},{2,1},{3,2},{4,7},{5,4},{6,5},{7,6},{8,11},{9,8},{10,9... | collective-permute-start | bytes 983048 | tf_op jit(solution)/shard_map/ppermute | solution.py:27
  34.4 52.2 %collective-permute-start.19 = (bf16[384,2560]{1,0:T(8,128)(2,1)}, bf16[384,2560]{1,0:T(8,128)(2,1)}, u32[]{:S(2)}, u32[]{:S(2)}) collective-permute-start(bf16[384,2560]{1,0:T(8,128)(2,1)} %constant_dynamic-slice_fusion), channel_id=1, source_target_pairs={{0,68},{1,69},{2,70},{3,71},{4,64},{5,65},{6,66},{7,67},{8,76},{9,... | collective-permute-start | bytes 5898248 | tf_op jit(solution)/shard_map/ppermute | solution.py:45
  43.4 16.5 %collective-permute-start.6 = (bf16[2,32,5120]{2,1,0:T(8,128)(2,1)}, bf16[2,32,5120]{2,1,0:T(8,128)(2,1)S(1)}, u32[]{:S(2)}, u32[]{:S(2)}) collective-permute-start(bf16[2,32,5120]{2,1,0:T(8,128)(2,1)} %collective-permute-done.2.refs_3_), channel_id=1, source_target_pairs={{0,3},{1,0},{2,1},{3,2},{4,7},{5,4},{6,5},{7,6},{8,11},{9,8},{10,9... | collective-permute-start | bytes 1966088 | tf_op jit(solution)/shard_map/ppermute | solution.py:27
  43.4 17.0 %collective-permute-start.5 = (bf16[2,32,5120]{2,1,0:T(8,128)(2,1)}, bf16[2,32,5120]{2,1,0:T(8,128)(2,1)S(1)}, u32[]{:S(2)}, u32[]{:S(2)}) collective-permute-start(bf16[2,32,5120]{2,1,0:T(8,128)(2,1)} %collective-permute-done.2.refs_3_), channel_id=1, source_target_pairs={{0,1},{1,2},{2,3},{3,0},{4,5},{5,6},{6,7},{7,4},{8,9},{9,10},{10,1... | collective-permute-start | bytes 1966088 | tf_op jit(solution)/shard_map/ppermute | solution.py:27
  46.7 15.5 %collective-permute-start.7 = (bf16[2,32,5120]{2,1,0:T(8,128)(2,1)S(1)}, bf16[2,32,5120]{2,1,0:T(8,128)(2,1)S(1)}, u32[]{:S(2)}, u32[]{:S(2)}) collective-permute-start(bf16[2,32,5120]{2,1,0:T(8,128)(2,1)S(1)} %constant_dynamic-update-slice_fusion.refs_0_), channel_id=1, source_target_pairs={{0,4},{1,5},{2,6},{3,7},{4,0},{5,1},{6,2},{7,3},{8,12},{9,13},{10,... | collective-permute-start | bytes 1966088 | tf_op jit(solution)/shard_map/ppermute | solution.py:27
  52.3 9.9 %slice-start.1 = ((s8[11796480]{0:T(1024)(128)(4,1)}), s8[4194304]{0:T(1024)(128)(4,1)S(1)}, s32[]{:S(2)}) async-start(s8[11796480]{0:T(1024)(128)(4,1)} %bitcast.24), calls=%async_computation.1 | async-start | bytes 8388608
  52.3 9.9 %slice-start.2 = ((s8[11796480]{0:T(1024)(128)(4,1)}), s8[4194304]{0:T(1024)(128)(4,1)S(1)}, s32[]{:S(2)}) async-start(s8[11796480]{0:T(1024)(128)(4,1)} %bitcast.24), calls=%async_computation.2 | async-start | bytes 8388608
  59.8 9.5 %collective-permute-start.11 = (bf16[2,512,384]{2,1,0:T(8,128)(2,1)S(1)}, bf16[2,512,384]{2,1,0:T(8,128)(2,1)S(1)}, u32[]{:S(2)}, u32[]{:S(2)}) collective-permute-start(bf16[2,512,384]{2,1,0:T(8,128)(2,1)S(1)} %copy-done.6), channel_id=1, source_target_pairs={{0,8},{8,0},{16,24},{24,16},{32,40},{40,32},{48,56},{56,48},{64,72... | collective-permute-start | bytes 2359304 | tf_op jit(solution)/shard_map/ppermute | solution.py:37
  59.9 13.1 %collective-permute-start.14 = (bf16[2,512,384]{2,1,0:T(8,128)(2,1)}, bf16[2,512,384]{2,1,0:T(8,128)(2,1)S(1)}, u32[]{:S(2)}, u32[]{:S(2)}) collective-permute-start(bf16[2,512,384]{2,1,0:T(8,128)(2,1)} %collective-permute-done.10.rest_5_.rest_3_), channel_id=1, source_target_pairs={{0,8},{8,0},{16,24},{24,16},{32,40},{40,32},{48,56},{56,48},{64,72... | collective-permute-start | bytes 2359304 | tf_op jit(solution)/shard_map/ppermute | solution.py:37
  60.4 12.9 %collective-permute-start.13 = (bf16[2,512,384]{2,1,0:T(8,128)(2,1)}, bf16[2,512,384]{2,1,0:T(8,128)(2,1)S(1)}, u32[]{:S(2)}, u32[]{:S(2)}) collective-permute-start(bf16[2,512,384]{2,1,0:T(8,128)(2,1)} %collective-permute-done.9.rest_4_.rest_2_), channel_id=1, source_target_pairs={{0,8},{8,0},{16,24},{24,16},{32,40},{40,32},{48,56},{56,48},{64,72... | collective-permute-start | bytes 2359304 | tf_op jit(solution)/shard_map/ppermute | solution.py:37
  62.2 11.1 %collective-permute-start.12 = (bf16[2,512,384]{2,1,0:T(8,128)(2,1)S(1)}, bf16[2,512,384]{2,1,0:T(8,128)(2,1)S(1)}, u32[]{:S(2)}, u32[]{:S(2)}) collective-permute-start(bf16[2,512,384]{2,1,0:T(8,128)(2,1)S(1)} %collective-permute-done.8.rest_3_.rest_1_), channel_id=1, source_target_pairs={{0,8},{8,0},{16,24},{24,16},{32,40},{40,32},{48,56},{56,48},{64,72... | collective-permute-start | bytes 2359304 | tf_op jit(solution)/shard_map/ppermute | solution.py:37
  69.3 17.3 %collective-permute-start.16 = (bf16[2,256,384]{2,1,0:T(8,128)(2,1)S(1)}, bf16[2,256,384]{2,1,0:T(8,128)(2,1)S(1)}, u32[]{:S(2)}, u32[]{:S(2)}) collective-permute-start(bf16[2,256,384]{2,1,0:T(8,128)(2,1)S(1)} %pad_maximum_fusion.3), channel_id=1, source_target_pairs={{0,64},{8,72},{16,80},{24,88},{32,96},{40,104},{48,112},{56,120},{... | collective-permute-start | bytes 1179656 | tf_op jit(solution)/shard_map/ppermute | solution.py:37
  73.0 13.6 %collective-permute-start.15 = (s32[2]{0:T(128)S(1)}, s32[2]{0:T(128)S(1)}, u32[]{:S(2)}, u32[]{:S(2)}) collective-permute-start(s32[2]{0:T(128)S(1)} %copy-done.8), channel_id=1, source_target_pairs={{0,64},{8,72},{16,80},{24,88},{32,96},{40,104},{48,112},{56,120},{... | collective-permute-start | bytes 32 | tf_op jit(solution)/shard_map/ppermute | solution.py:37
  86.6 39.5 %collective-permute-start.20 = (bf16[384,2560]{1,0:T(8,128)(2,1)}, bf16[384,2560]{1,0:T(8,128)(2,1)}, u32[]{:S(2)}, u32[]{:S(2)}) collective-permute-start(bf16[384,2560]{1,0:T(8,128)(2,1)} %collective-permute-done.19), channel_id=1, source_target_pairs={{0,8},{8,0},{16,24},{24,16},{32,40},{40,32},{48,56},{56,48},{64,72... | collective-permute-start | bytes 5898248 | tf_op jit(solution)/shard_map/ppermute | solution.py:37
  100.7 16.1 %collective-permute-start.17 = (bf16[2,256,512]{2,1,0:T(8,128)(2,1)S(1)}, bf16[2,256,512]{2,1,0:T(8,128)(2,1)S(1)}, u32[]{:S(2)}, u32[]{:S(2)}) collective-permute-start(bf16[2,256,512]{2,1,0:T(8,128)(2,1)S(1)} %pad_maximum_fusion.2), channel_id=1, source_target_pairs={{0,64},{8,72},{16,80},{24,88},{32,96},{40,104},{48,112},{56,120},{... | collective-permute-start | bytes 1572872 | tf_op jit(solution)/shard_map/ppermute | solution.py:37
  119.4 6.6 %collective-permute-start.18 = (bf16[2,128,384]{2,1,0:T(8,128)(2,1)S(1)}, bf16[2,128,384]{2,1,0:T(8,128)(2,1)S(1)}, u32[]{:S(2)}, u32[]{:S(2)}) collective-permute-start(bf16[2,128,384]{2,1,0:T(8,128)(2,1)S(1)} %slice.172), channel_id=1, source_target_pairs={{0,4},{1,5},{2,6},{3,7},{4,0},{5,1},{6,2},{7,3},{8,12},{9,13},{10,... | collective-permute-start | bytes 589832 | tf_op jit(solution)/shard_map/ppermute | solution.py:27
  126.1 4.5 %copy-start.1 = (bf16[384,5120]{1,0:T(8,128)(2,1)S(1)}, bf16[384,5120]{1,0:T(8,128)(2,1)}, u32[]{:S(2)}) copy-start(bf16[384,5120]{1,0:T(8,128)(2,1)} %wa_ref.3) | copy-start | bytes 11796484
  135.1 10.5 %collective-permute-start.21 = (bf16[1,32,5120]{2,1,0:T(8,128)(2,1)S(1)}, bf16[1,32,5120]{2,1,0:T(8,128)(2,1)S(1)}, u32[]{:S(2)}, u32[]{:S(2)}) collective-permute-start(bf16[1,32,5120]{2,1,0:T(8,128)(2,1)S(1)} %get-tuple-element.41), channel_id=1, source_target_pairs={{0,3},{1,0},{2,1},{3,2},{4,7},{5,4},{6,5},{7,6},{8,11},{9,8},{10,9... | collective-permute-start | bytes 983048 | tf_op jit(solution)/shard_map/ppermute | solution.py:27
  137.4 9.0 %collective-permute-start.23 = (bf16[1,32,5120]{2,1,0:T(8,128)(2,1)S(1)}, bf16[1,32,5120]{2,1,0:T(8,128)(2,1)S(1)}, u32[]{:S(2)}, u32[]{:S(2)}) collective-permute-start(bf16[1,32,5120]{2,1,0:T(8,128)(2,1)S(1)} %get-tuple-element.42), channel_id=1, source_target_pairs={{0,1},{1,2},{2,3},{3,0},{4,5},{5,6},{6,7},{7,4},{8,9},{9,10},{10,1... | collective-permute-start | bytes 983048 | tf_op jit(solution)/shard_map/ppermute | solution.py:27
  144.4 20.1 %copy-start.3 = (bf16[2,32,5120]{2,1,0:T(8,128)(2,1)S(1)}, bf16[2,32,5120]{2,1,0:T(8,128)(2,1)}, u32[]{:S(2)}) copy-start(bf16[2,32,5120]{2,1,0:T(8,128)(2,1)} %x_ref.1) | copy-start | bytes 1966084
  146.6 14.6 %collective-permute-start.24 = (bf16[2,32,5120]{2,1,0:T(8,128)(2,1)S(1)}, bf16[2,32,5120]{2,1,0:T(8,128)(2,1)S(1)}, u32[]{:S(2)}, u32[]{:S(2)}) collective-permute-start(bf16[2,32,5120]{2,1,0:T(8,128)(2,1)S(1)} %pad_maximum_fusion.1), channel_id=1, source_target_pairs={{0,1},{1,2},{2,3},{3,0},{4,5},{5,6},{6,7},{7,4},{8,9},{9,10},{10,1... | collective-permute-start | bytes 1966088 | tf_op jit(solution)/shard_map/ppermute | solution.py:27
  148.9 15.5 %collective-permute-start.22 = (bf16[2,32,5120]{2,1,0:T(8,128)(2,1)S(1)}, bf16[2,32,5120]{2,1,0:T(8,128)(2,1)S(1)}, u32[]{:S(2)}, u32[]{:S(2)}) collective-permute-start(bf16[2,32,5120]{2,1,0:T(8,128)(2,1)S(1)} %pad_maximum_fusion), channel_id=1, source_target_pairs={{0,3},{1,0},{2,1},{3,2},{4,7},{5,4},{6,5},{7,6},{8,11},{9,8},{10,9... | collective-permute-start | bytes 1966088 | tf_op jit(solution)/shard_map/ppermute | solution.py:27
  (5 other events, 7.9 us)

commit v2 on v1

--- a/solution.py
+++ b/solution.py
@@ -37,6 +37,20 @@
     return lax.ppermute(a, "branch", perm)
 
 
+def turned(a, axis, step):
+    perm = []
+    for b in range(16):
+        for s in range(8):
+            way = step if b % 2 == 0 else -step
+            z, x, y = b // 8 * 8, b // 2 % 4, s % 4
+            if axis == "x":
+                to = (z + (x + way) % 4 * 2 + b % 2, s)
+            else:
+                to = (b, s - y + (y + way) % 4)
+            perm.append((b * 8 + s, to[0] * 8 + to[1]))
+    return lax.ppermute(a, ("branch", "seq"), perm)
+
+
 def across_z(a):
     perm = []
     for b in range(16):
@@ -45,7 +59,11 @@
     return lax.ppermute(a, ("branch", "seq"), perm)
 
 
-def norm_kernel(actions, x_ref, table_ref, hidden_ref, gate_ref):
+def norm_kernel(actions, x_ref, table_ref, w_ref, hidden_ref, gate_ref, half_ref, sem):
+    count = half_ref.shape[0]
+    at = lax.rem(lax.axis_index("branch"), 2) * count
+    copy = pltpu.make_async_copy(w_ref.at[pl.ds(pl.multiple_of(at, 16), count)], half_ref, sem)
+    copy.start()
     rows = lax.broadcasted_iota(jnp.int32, (ACTIONS, 1), 0)
     for b in range(x_ref.shape[0]):
         pick = rows == actions[b]
@@ -61,19 +79,22 @@
         variance = jnp.mean(centred * centred, axis=-1, keepdims=True)
         normed = centred * (1.0 / jnp.sqrt(variance + 1e-06))
         hidden_ref[b] = (normed * (1.0 + scale) + shift).astype(jnp.bfloat16)
-
-
-def norm(actions, x, table):
+    copy.wait()
+
+
+def norm(actions, x, table, w_out):
     return pl.pallas_call(
         norm_kernel,
         out_shape=(
             jax.ShapeDtypeStruct(x.shape, jnp.bfloat16),
             jax.ShapeDtypeStruct((x.shape[0], 1, x.shape[2]), jnp.float32),
+            jax.ShapeDtypeStruct((w_out.shape[0] // 2, w_out.shape[1]), w_out.dtype),
         ),
-        in_specs=[SMEM, VMEM, VMEM],
-        out_specs=(VMEM, VMEM),
+        in_specs=[SMEM, VMEM, VMEM, ANY],
+        out_specs=(VMEM, VMEM, ANY),
+        scratch_shapes=[pltpu.SemaphoreType.DMA],
         compiler_params=pltpu.CompilerParams(vmem_limit_bytes=24 << 20),
-    )(actions, x, table)
+    )(actions, x, table, w_out)
 
 
 def qkv_kernel(count, *refs):
@@ -117,10 +138,11 @@
     )(*shards, w)
 
 
-def attend_kernel(branches, chunk, blocks, own, start_ref, q_ref, frame_ref, *rest):
+def attend_kernel(branches, chunk, blocks, own, q_ref, frame_ref, *rest):
     if own:
         own_k, own_v, rest = rest[0], rest[1], rest[2:]
-    parts, o_ref, stat_ref, kv, top_s, sum_s, acc_s, sems = rest[:blocks], *rest[blocks:]
+    parts, outs, (kv, top_s, sum_s, acc_s, sems) = rest[:blocks], rest[blocks:-5], rest[-5:]
+    o_ref = outs[0]
     copies = [
         pltpu.make_async_copy(parts[i], kv.at[:, pl.ds(i * 512, 512)], sems.at[i])
         for i in range(blocks)
@@ -129,7 +151,7 @@
         copy.start()
 
     def block_step(b, h, k, v, bias, first):
-        q = q_ref[b, :, h * HDIM : (h + 1) * HDIM]
+        q = q_ref[b, :FRAME_TOK, h * HDIM : (h + 1) * HDIM]
         s = lax.dot_general(q, k, (((1,), (1,)), ((), ())), preferred_element_type=jnp.float32)
         s = s * SCALE2
         if bias is not None:
@@ -169,7 +191,8 @@
     def loop(i, _):
         rows = pl.ds(pl.multiple_of(i * chunk, chunk), chunk)
         for b in range(branches):
-            bias = jnp.where(frame_ref[pl.ds(i, 1), :] >= start_ref[b], 0.0, MASKED)
+            start = q_ref[b, FRAME_TOK:, :1].astype(jnp.float32)[:1]
+            bias = jnp.where(frame_ref[pl.ds(i, 1), :] >= start, 0.0, MASKED)
             for h in range(HERE):
                 cols = slice(h * HDIM, (h + 1) * HDIM)
                 block_step(b, h, kv[0, rows, cols], kv[1, rows, cols], bias, False)
@@ -187,20 +210,25 @@
                 piece = left.astype(jnp.bfloat16).astype(jnp.float32)
                 stats = jnp.where(lane == h * 3 + part, piece, stats)
                 left = left - piece
-        stat_ref[b] = stats.astype(jnp.bfloat16)
-
-
-def attend(start, q, frames, parts, own=None, dtype=jnp.bfloat16):
+        if own:
+            outs[1][b] = stats.astype(jnp.bfloat16)
+        else:
+            o_ref[b, :, WIDTH:] = stats.astype(jnp.bfloat16)
+
+
+def attend(q, frames, parts, own=None):
     branches, blocks, chunk = q.shape[0], len(parts), 2048
     state = pltpu.VMEM((branches, HERE, FRAME_TOK, HDIM), jnp.float32)
     return pl.pallas_call(
         functools.partial(attend_kernel, branches, chunk, blocks, own is not None),
         out_shape=(
-            jax.ShapeDtypeStruct((branches, FRAME_TOK, WIDTH), dtype),
+            jax.ShapeDtypeStruct((branches, FRAME_TOK, WIDTH), jnp.float32),
             jax.ShapeDtypeStruct((branches, FRAME_TOK, HDIM), jnp.bfloat16),
-        ),
-        in_specs=[SMEM, VMEM, VMEM] + ([VMEM, VMEM] if own else []) + [ANY] * blocks,
-        out_specs=(VMEM, VMEM),
+        )
+        if own
+        else jax.ShapeDtypeStruct((branches, FRAME_TOK, WIDTH + HDIM), jnp.bfloat16),
+        in_specs=[VMEM, VMEM] + ([VMEM, VMEM] if own else []) + [ANY] * blocks,
+        out_specs=(VMEM, VMEM) if own else VMEM,
         scratch_shapes=[
             pltpu.VMEM((2, blocks * 512, WIDTH), jnp.bfloat16),
             state,
@@ -214,105 +242,137 @@
             bytes_accessed=blocks * 512 * WIDTH * 4,
             transcendentals=branches * FRAME_TOK * blocks * 512 * HERE,
         ),
-    )(start, q, frames.reshape(-1, chunk), *(own or ()), *parts)
-
-
-def log_sums(stats):
-    s = stats[..., : 3 * HERE].astype(jnp.float32)
-    return s.reshape(s.shape[:-1] + (HERE, 3)).sum(-1)
-
-
-def out_kernel(a_ref, b_ref, wa_ref, wb_ref, o_ref):
+    )(q, frames.reshape(-1, chunk), *(own or ()), *parts)
+
+
+def merge_kernel(*refs):
+    here, there = refs[-2:]
+    packed = refs[-3]
+    count = (len(refs) - 3) // 2
+    for b in range(count):
+        o_ref, stat_ref = refs[2 * b : 2 * b + 2]
+        for h in range(HERE):
+            cols = slice(h * HDIM, (h + 1) * HDIM)
+            own = stat_ref[0, :, h * 3 : h * 3 + 3].astype(jnp.float32)
+            far = packed[b, :, WIDTH + h * 3 : WIDTH + h * 3 + 3].astype(jnp.float32)
+            own = jnp.sum(own, axis=1, keepdims=True)
+            far = jnp.sum(far, axis=1, keepdims=True)
+            top = jnp.maximum(own, far)
+            own, far = jnp.exp2(own - top), jnp.exp2(far - top)
+            scale = 1.0 / (own + far)
+            o = (
+                o_ref[0, :, cols] * (own * scale)
+                + packed[b, :, cols].astype(jnp.float32) * (far * scale)
+            ).astype(jnp.bfloat16)
+            here[b, :, cols] = o[:128]
+            there[b, :, cols] = o[128:]
+
+
+def merge(parts, packed):
+    out = jax.ShapeDtypeStruct((len(parts), 128, WIDTH), jnp.bfloat16)
+    flat = [a for part in parts for a in part]
+    return pl.pallas_call(
+        merge_kernel,
+        out_shape=(out, out),
+        in_specs=[VMEM] * (len(flat) + 1),
+        out_specs=(VMEM, VMEM),
+        compiler_params=pltpu.CompilerParams(vmem_limit_bytes=24 << 20),
+    )(*flat, packed)
+
+
+def out_kernel(core, a_ref, b_ref, wa_ref, near_ref, far_ref, *rest):
+    outs, w = rest[:-1], rest[-1]
+    half = near_ref.shape[0]
+    for side, ref in ((core[0], near_ref), (1 - core[0], far_ref)):
+        w[pl.ds(pl.multiple_of(side * half, 16), half)] = ref[...]
     rows = a_ref.shape[1]
-    for b in range(2):
-        o_ref[b] = (
-            jnp.dot(a_ref[b], wa_ref[...], preferred_element_type=jnp.float32)
-            + jnp.dot(b_ref[b], wb_ref[...], preferred_element_type=jnp.float32)
-        ).astype(jnp.bfloat16)
-
-
-def project_out(a, b, wa, wb):
-    rows, width, block = a.shape[1], wa.shape[1], 512
+    stack = lambda ref: jnp.concatenate([ref[b] for b in range(ref.shape[0])], axis=0)
+    o = (
+        jnp.dot(stack(a_ref), wa_ref[...], preferred_element_type=jnp.float32)
+        + jnp.dot(stack(b_ref), w[...], preferred_element_type=jnp.float32)
+    ).astype(jnp.bfloat16)
+    for b in range(a_ref.shape[0]):
+        for j, ref in enumerate(outs):
+            ref[b] = o[b * rows + j * 32 : b * rows + (j + 1) * 32]
+
+
+def project_out(core, a, b, wa, near, far):
+    branches, rows, width, block = a.shape[0], a.shape[1], wa.shape[1], 512
+    count = rows // 32
     return pl.pallas_call(
         out_kernel,
         grid=(width // block,),
-        out_shape=jax.ShapeDtypeStruct((2, rows, width), jnp.bfloat16),
+        out_shape=(jax.ShapeDtypeStruct((branches, 32, width), jnp.bfloat16),) * count,
         in_specs=[
-            pl.BlockSpec((2, rows, WIDTH), lambda i: (0, 0, 0)),
-            pl.BlockSpec((2, rows, WIDTH), lambda i: (0, 0, 0)),
+            SMEM,
+            pl.BlockSpec((branches, rows, WIDTH), lambda i: (0, 0, 0)),
+            pl.BlockSpec((branches, rows, WIDTH), lambda i: (0, 0, 0)),
             pl.BlockSpec((WIDTH, block), lambda i: (0, i)),
-            pl.BlockSpec((WIDTH, block), lambda i: (0, i)),
-        ],
-        out_specs=pl.BlockSpec((2, rows, block), lambda i: (0, 0, i)),
+        ]
+        + [pl.BlockSpec((WIDTH // 2, block), lambda i: (0, i))] * 2,
+        out_specs=(pl.BlockSpec((branches, 32, block), lambda i: (0, 0, i)),) * count,
+        scratch_shapes=[pltpu.VMEM((WIDTH, block), jnp.bfloat16)],
         compiler_params=pltpu.CompilerParams(vmem_limit_bytes=24 << 20),
         cost_estimate=pl.CostEstimate(
-            flops=8 * rows * WIDTH * width,
-            bytes_accessed=4 * WIDTH * width + 4 * rows * width,
+            flops=4 * branches * rows * WIDTH * width,
+            bytes_accessed=4 * WIDTH * width + 2 * branches * rows * width,
             transcendentals=0,
         ),
-    )(a, b, wa, wb)
+    )(core, a, b, wa, near, far)
 
 
 def shards(x, actions, visible_from, table, w_qkv, w_out, ctx):
     branch = lax.axis_index("branch")
     core, base = branch % 2, branch // 8 * 8
-    hidden, gate = norm(actions, x, jnp.transpose(table, (1, 0, 2)))
+    hidden, gate, half = norm(actions, x, jnp.transpose(table, (1, 0, 2)), w_out)
     w = jnp.transpose(w_qkv, (1, 0, 2))
 
     a0 = hidden
-    a1, a3, b0 = along_seq(a0, 1), along_seq(a0, -1), along_seq(a0, 0, 1)
-    a2 = jnp.concatenate([along_seq(a1[:1], 1), along_seq(a3[1:], -1)], axis=0)
-    b1, b3 = along_seq(b0, 1), along_seq(b0, -1)
+    a1, a3, b0 = turned(a0, "y", 1), turned(a0, "y", -1), along_seq(a0, 0, 1)
+    a2 = turned(a1, "y", 1)
+    b1, b3 = turned(b0, "y", 1), turned(b0, "y", -1)
     b2 = along_seq(a2, 0, 1)
 
+    near = across_z(half)
+    far = along_branch(near, 0, 0, 1)
+
     ctx, _ = lax.optimization_barrier((ctx, hidden))
-    mine = [ctx, along_branch(ctx, 1), along_branch(ctx, -1), along_branch(ctx, 2)]
+    c1 = turned(ctx, "x", 1)
+    c3 = turned(lax.optimization_barrier((ctx, c1))[0], "x", -1)
+    c2 = turned(lax.optimization_barrier((c1, c3))[0], "x", 1)
+    mine = [ctx, c1, c3, c2]
     parts = mine + [along_branch(part, 0, 0, 1) for part in mine]
     at = branch // 2 % 4
-    order = [base + (at + d) % 4 * 2 + c for c in (core, 1 - core) for d in (0, 3, 1, 2)]
+    order = []
+    for c in (core, 1 - core):
+        for d in (0, 2 * c - 1, 1 - 2 * c, 2):
+            order.append(base + (at + d + 4) % 4 * 2 + c)
     frames = jnp.stack(order)[:, None] * 2 + jnp.arange(512, dtype=jnp.int32) // FRAME_TOK
-    far_start = along_branch(visible_from, 0, 1)
-
-    half = w_out.shape[1] // 2
-    near = across_z(lax.dynamic_slice_in_dim(w_out, core * half, half, 1))
-    far = along_branch(near, 0, 0, 1)
-    w_other = jnp.where(
-        core == 0, jnp.concatenate([near, far], 1), jnp.concatenate([far, near], 1)
-    )
+    frames = frames.astype(jnp.float32)
 
     first = project_qkv([a0, a1, a3, b0], w)
     second = project_qkv([a2, b1, b3, b2], w)
+    start = jnp.broadcast_to(visible_from.astype(jnp.bfloat16)[:, None, None], (2, 16, WIDTH))
     q, k, v = (
-        jnp.concatenate([f[:, :96], s[:, :32], f[:, 96:], s[:, 32:]], axis=1)
-        for f, s in zip(first, second)
+        jnp.concatenate([f[:, :96], s[:, :32], f[:, 96:], s[:, 32:]] + tail, axis=1)
+        for f, s, tail in zip(first, second, ([start], [], []))
     )
     far_q = along_branch(q, 0, 1)
-    o_0, s_0 = attend(visible_from[:1], q[:1], frames, parts, (k[:1], v[:1]), jnp.float32)
+    o_0, s_0 = attend(q[:1], frames, parts, (k[:1], v[:1]))
     far_q, _ = lax.optimization_barrier((far_q, s_0))
-    far_o = attend(far_start, far_q, frames, parts)
-    packed = along_branch(jnp.concatenate(far_o, axis=2), 0, 1)
-    o_1, s_1 = attend(visible_from[1:], q[1:], frames, parts, (k[1:], v[1:]), jnp.float32)
-    own_o, own_l = jnp.concatenate([o_0, o_1]), log_sums(jnp.concatenate([s_0, s_1]))
-    far_l = log_sums(packed[..., WIDTH:])
-    top = jnp.maximum(own_l, far_l)
-    own_w, far_w = jnp.exp2(own_l - top), jnp.exp2(far_l - top)
-    total = own_w + far_w
-    spread = lambda u: jnp.repeat(u / total, HDIM, axis=2)
-    attended = (
-        own_o * spread(own_w) + packed[..., :WIDTH].astype(jnp.float32) * spread(far_w)
-    ).astype(jnp.bfloat16)
-
-    here, there = attended[:, :128], attended[:, 128:]
+    packed = along_branch(attend(far_q, frames, parts), 0, 1)
+    o_1, s_1 = attend(q[1:], frames, parts, (k[1:], v[1:]))
+    here, there = merge([(o_0, s_0), (o_1, s_1)], packed)
     other = along_seq(there, 0, 1)
-    p2 = project_out(here[:, 96:], other[:, 96:], w_out, w_other)
-    down, up = along_seq(p2[:1], -1), along_seq(p2[1:], 1)
-    rest = project_out(here[:, :96], other[:, :96], w_out, w_other).astype(jnp.float32)
-    p0, p1, p3 = rest[:, :32], rest[:, 32:64], rest[:, 64:]
-    p1 = jnp.concatenate([p1[:1] + down.astype(jnp.float32), p1[1:]]).astype(jnp.bfloat16)
-    p3 = jnp.concatenate([p3[:1], p3[1:] + up.astype(jnp.float32)]).astype(jnp.bfloat16)
-    t1, t3 = along_seq(p1, -1), along_seq(p3, 1)
-    projected = p0 + t1.astype(jnp.float32) + t3.astype(jnp.float32)
-    return (x.astype(jnp.float32) + gate * projected).astype(jnp.bfloat16)
+    p0, p1, p3, p2 = project_out(
+        core.astype(jnp.int32).reshape(1), here, other, w_out, near, far
+    )
+    back = turned(p2, "y", -1)
+    t3 = turned(p3, "y", 1)
+    p1 = (p1.astype(jnp.float32) + back.astype(jnp.float32)).astype(jnp.bfloat16)
+    t1 = turned(p1, "y", -1)
+    sums = p0.astype(jnp.float32) + t1.astype(jnp.float32) + t3.astype(jnp.float32)
+    return (x.astype(jnp.float32) + gate * sums).astype(jnp.bfloat16)
 
 
 def solution(mesh):

time: 166 us -> 156 us (0.940)
  waiting for transfers between devices: 52.3 us -> 61.2 us
  other arithmetic: 7.78 us -> 1.48 us
  Pallas kernels: 56.4 us -> 51.7 us
  local copies, waits for them, and re-layouts: 15.1 us -> 11.1 us
  starting transfers between devices: 33.5 us -> 29.7 us
    ppermute x0 -> x11, waiting for transfers between devices: none -> 42.2 us  [turned(): return lax.ppermute(a, ('branch', 'seq'), perm)]
    ppermute x13 -> x3, waiting for transfers between devices: 42.3 us -> 12.3 us  [along_seq(): return lax.ppermute(a, 'seq', perm)]
    ppermute x13 -> x3, starting transfers between devices: 19.7 us -> 3.71 us  [along_seq(): return lax.ppermute(a, 'seq', perm)]
    ppermute x0 -> x11, starting transfers between devices: none -> 11 us  [turned(): return lax.ppermute(a, ('branch', 'seq'), perm)]
    ppermute x1, waiting for transfers between devices: 4.99 us -> 0.01 us  [across_z(): return lax.ppermute(a, ('branch', 'seq'), perm)]
    select_n x1 -> x0, other arithmetic: 4.46 us -> none  [shards(): jnp.where(core == 0, jnp.concatenate([near, far], 1), jnp.concatenate([fa...]
    dynamic_slice x1 -> x0, local copies, waits for them, and re-layouts: 3.13 us -> none  [shards(): near = across_z(lax.dynamic_slice_in_dim(w_out, core * half, half, 1))]
    pallas_call x2, Pallas kernels: 9.41 us -> 6.65 us  [the longest x1 5.46 us: project_out(): pl.pallas_call(out_kernel, grid=(width // block,), out_shape=(jax.ShapeDt...]
  transfers between devices with their start and end apart: 25 -> 22, of which waited for: 11 -> 9; matrix products, arithmetic and copies ran while one was open for 6% -> 1% of each run, Pallas kernels for 30% -> 28%
where the time goes in v2:
time: 156 us; the launch traced here: 155 us
  waiting for transfers between devices  61.2 us (39%)
  Pallas kernels  51.7 us (33%)
  starting transfers between devices  29.7 us (19%)
  local copies, waits for them, and re-layouts  11.1 us (7%)
    ppermute x11, waiting for transfers between devices, turned(): return lax.ppermute(a, ('branch', 'seq'), perm)  42.2 us
    pallas_call x3, Pallas kernels, attend(): pl.pallas_call(functools.partial(attend_kernel, branches, chunk, blocks,...  28.8 us
    pallas_call x2, Pallas kernels, project_qkv(): pl.pallas_call(functools.partial(qkv_kernel, count), grid=(depth // block...  14.2 us
    ppermute x3, waiting for transfers between devices, along_seq(): return lax.ppermute(a, 'seq', perm)  12.3 us
    ppermute x11, starting transfers between devices, turned(): return lax.ppermute(a, ('branch', 'seq'), perm)  11 us
    ppermute x7, starting transfers between devices, along_branch(): return lax.ppermute(a, 'branch', perm)  10.9 us
    unnamed x31, local copies, waits for them, and re-layouts  10.6 us
    ppermute x7, waiting for transfers between devices, along_branch(): return lax.ppermute(a, 'branch', perm)  6.68 us
  transfers between devices with their start and end apart: 22, of which 9 were waited for; matrix products, arithmetic and copies ran while one was open for 1% of the time, Pallas kernels for 28%

profile of v2, /device:TPU:28, one launch (start us, length us, event | category | flops | bytes accessed | tf_op | source)
XLA Modules:
  0.0 155.4 jit_solution(5142335362446901936)
XLA Ops:
  0.0 2.1 %copy-done.2 = bf16[384,5120]{1,0:T(8,128)(2,1)S(1)} copy-done((bf16[384,5120]{1,0:T(8,128)(2,1)S(1)}, bf16[384,5120]{1,0:T(8,128)(2,1)}, u32[]{:S(2)}) %copy-start.2) | copy-done | bytes 3932184
  2.1 1.1 copy-done.4
  3.2 1.0 copy-done.6
  4.2 0.7 copy-done.7
  4.9 2.0 %shard_map.73 = (bf16[2,32,5120]{2,1,0:T(8,128)(2,1)S(1)}, f32[2,1,5120]{2,1,0:T(1,128)S(1)}, bf16[192,5120]{1,0:T(8,128)(2,1)}) custom-call(s32[2]{0:T(128)S(1)} %copy-done.7, bf16[2,32,5120]{2,1,0:T(8,128)(2,1)S(1)} %copy-done.4, bf16[3,16,5120]{2,1,0:T(8,128)(2,1)S(1)} %bitcast.22, bf16[384,5120]{1,0:T(8,128)(2,1)S(1)} %copy-done.2), custom_call_target="tpu_custom_call" | custom-call | tf_op jit(solution)/shard_map/pallas_call | solution.py:86
  7.2 1.2 collective-permute-start.7
  8.4 4.0 %collective-permute-start.17 = (bf16[192,5120]{1,0:T(8,128)(2,1)}, bf16[192,5120]{1,0:T(8,128)(2,1)S(1)}, u32[]{:S(2)}, u32[]{:S(2)}) collective-permute-start(bf16[192,5120]{1,0:T(8,128)(2,1)} %get-tuple-element.46), channel_id=1, source_target_pairs={{0,68},{1,69},{2,70},{3,71},{4,64},{5,65},{6,66},{7,67},{8,76},{9,... | collective-permute-start | bytes 5898248 | tf_op jit(solution)/shard_map/ppermute | solution.py:59
  12.4 1.8 %collective-permute-start.1 = (bf16[2,32,5120]{2,1,0:T(8,128)(2,1)S(1)}, bf16[2,32,5120]{2,1,0:T(8,128)(2,1)}, u32[]{:S(2)}, u32[]{:S(2)}) collective-permute-start(bf16[2,32,5120]{2,1,0:T(8,128)(2,1)S(1)} %get-tuple-element.29.refs_0_), channel_id=1, source_target_pairs={{0,3},{1,0},{2,1},{3,2},{4,7},{5,4},{6,5},{7,6},{8,9},{9,10},{10,1... | collective-permute-start | bytes 1966088 | tf_op jit(solution)/shard_map/ppermute | solution.py:51
  14.3 6.9 %collective-permute-done.refs_1_ = bf16[2,32,5120]{2,1,0:T(8,128)(2,1)} collective-permute-done((bf16[2,32,5120]{2,1,0:T(8,128)(2,1)S(1)}, bf16[2,32,5120]{2,1,0:T(8,128)(2,1)}, u32[]{:S(2)}, u32[]{:S(2)}) %collective-permute-start) | collective-permute-done | bytes 655392 | tf_op jit(solution)/shard_map/ppermute | solution.py:51
  21.5 6.4 %collective-permute-done.2.refs_3_ = bf16[2,32,5120]{2,1,0:T(8,128)(2,1)S(1)} collective-permute-done((bf16[2,32,5120]{2,1,0:T(8,128)(2,1)S(1)}, bf16[2,32,5120]{2,1,0:T(8,128)(2,1)S(1)}, u32[]{:S(2)}, u32[]{:S(2)}) %collective-permute-start.2) | collective-permute-done | bytes 655392 | tf_op jit(solution)/shard_map/ppermute | solution.py:27
  28.3 2.8 %collective-permute-start.4 = (bf16[2,32,5120]{2,1,0:T(8,128)(2,1)S(1)}, bf16[2,32,5120]{2,1,0:T(8,128)(2,1)S(1)}, u32[]{:S(2)}, u32[]{:S(2)}) collective-permute-start(bf16[2,32,5120]{2,1,0:T(8,128)(2,1)S(1)} %collective-permute-done.2.refs_3_), channel_id=1, source_target_pairs={{0,1},{1,2},{2,3},{3,0},{4,5},{5,6},{6,7},{7,4},{8,11},{9,8},{10,9... | collective-permute-start | bytes 1966088 | tf_op jit(solution)/shard_map/ppermute | solution.py:51
  31.7 3.9 %collective-permute-done.3.refs_0_ = bf16[2,32,5120]{2,1,0:T(8,128)(2,1)} collective-permute-done((bf16[2,32,5120]{2,1,0:T(8,128)(2,1)}, bf16[2,32,5120]{2,1,0:T(8,128)(2,1)}, u32[]{:S(2)}, u32[]{:S(2)}) %collective-permute-start.3) | collective-permute-done | bytes 655392 | tf_op jit(solution)/shard_map/ppermute | solution.py:51
  35.6 3.6 %collective-permute-start.6 = (bf16[2,32,5120]{2,1,0:T(8,128)(2,1)}, bf16[2,32,5120]{2,1,0:T(8,128)(2,1)S(1)}, u32[]{:S(2)}, u32[]{:S(2)}) collective-permute-start(bf16[2,32,5120]{2,1,0:T(8,128)(2,1)} %collective-permute-done.3.refs_0_), channel_id=1, source_target_pairs={{0,4},{1,5},{2,6},{3,7},{4,0},{5,1},{6,2},{7,3},{8,12},{9,13},{10,... | collective-permute-start | bytes 1966088 | tf_op jit(solution)/shard_map/ppermute | solution.py:27
  39.3 4.3 %copy-done = bf16[5120,3,384]{2,0,1:T(8,128)(2,1)S(1)} copy-done((bf16[5120,3,384]{2,0,1:T(8,128)(2,1)S(1)}, bf16[5120,3,384]{2,0,1:T(8,128)(2,1)}, u32[]{:S(2)}) %copy-start) | copy-done | bytes 11796504
  43.6 7.2 %shard_map.74 = (bf16[2,128,384]{2,1,0:T(8,128)(2,1)S(1)}, bf16[2,128,384]{2,1,0:T(8,128)(2,1)S(1)}, bf16[2,128,384]{2,1,0:T(8,128)(2,1)S(1)}) custom-call(bf16[2,32,5120]{2,1,0:T(8,128)(2,1)S(1)} %get-tuple-element.29.refs_0_, bf16[2,32,5120]{2,1,0:T(8,128)(2,1)} %collective-permute-done.refs_1_, bf16[2,32,5120]{2,1,0:T(8,128)(2,1)} %collective-permute-done.1.refs_2_, ...), custom_call_target="tpu_custom_call" | custom-call | flops 3019898880 | bytes 14417920 | tf_op jit(solution)/shard_map/pallas_call | solution.py:124
  52.2 7.0 %shard_map.75 = (bf16[2,128,384]{2,1,0:T(8,128)(2,1)S(1)}, bf16[2,128,384]{2,1,0:T(8,128)(2,1)S(1)}, bf16[2,128,384]{2,1,0:T(8,128)(2,1)S(1)}) custom-call(bf16[2,32,5120]{2,1,0:T(8,128)(2,1)} %collective-permute-done.3.refs_0_, bf16[2,32,5120]{2,1,0:T(8,128)(2,1)S(1)} %collective-permute-done.4.refs_1_, ...), custom_call_target="tpu_custom_call" | custom-call | flops 3019898880 | bytes 14417920 | tf_op jit(solution)/shard_map/pallas_call | solution.py:124
  59.5 4.2 %collective-permute-done.9.rest_5_.rest_3_ = bf16[2,512,384]{2,1,0:T(8,128)(2,1)S(1)} collective-permute-done((bf16[2,512,384]{2,1,0:T(8,128)(2,1)}, bf16[2,512,384]{2,1,0:T(8,128)(2,1)S(1)}, u32[]{:S(2)}, u32[]{:S(2)}) %collective-permute-start.9) | collective-permute-done | bytes 786464 | tf_op jit(solution)/shard_map/ppermute | solution.py:51
  64.0 6.0 %collective-permute-start.14 = (bf16[2,272,384]{2,1,0:T(8,128)(2,1)S(1)}, bf16[2,272,384]{2,1,0:T(8,128)(2,1)S(1)}, u32[]{:S(2)}, u32[]{:S(2)}) collective-permute-start(bf16[2,272,384]{2,1,0:T(8,128)(2,1)S(1)} %broadcast_dynamic-update-slice_fusion), channel_id=1, source_target_pairs={{0,64},{8,72},{16,80},{24,88},{32,96},{40,104},{48,112},{56,120},{... | collective-permute-start | bytes 1253384 | tf_op jit(solution)/shard_map/ppermute | solution.py:37
  70.1 7.8 %shard_map.76 = (f32[1,256,384]{2,1,0:T(8,128)S(1)}, bf16[1,256,128]{2,1,0:T(8,128)(2,1)S(1)}) custom-call(bf16[1,272,384]{2,1,0:T(8,128)(2,1)S(1)} %get-tuple-element.52.q_ref, f32[2,2048]{1,0:T(2,128)S(1)} %add_convert_fusion.2.frame_ref, bf16[1,256,384]{2,1,0:T(8,128)(2,1)S(1)} %get-tuple-element.57.rest_0_, ...), custom_call_target="tpu_custom_call" | custom-call | flops 3221225472 | bytes 6291456 | tf_op jit(solution)/shard_map/pallas_call | solution.py:222
  78.0 2.4 %collective-permute-done.14.q_ref = bf16[2,272,384]{2,1,0:T(8,128)(2,1)S(1)} collective-permute-done((bf16[2,272,384]{2,1,0:T(8,128)(2,1)S(1)}, bf16[2,272,384]{2,1,0:T(8,128)(2,1)S(1)}, u32[]{:S(2)}, u32[]{:S(2)}) %collective-permute-start.14) | collective-permute-done | bytes 417824 | tf_op jit(solution)/shard_map/ppermute | solution.py:37
  80.3 1.1 copy-done.9
  81.5 13.3 %shard_map.78 = bf16[2,256,512]{2,1,0:T(8,128)(2,1)S(1)} custom-call(bf16[2,272,384]{2,1,0:T(8,128)(2,1)S(1)} %collective-permute-done.14.q_ref, f32[2,2048]{1,0:T(2,128)S(1)} %add_convert_fusion.2.frame_ref, bf16[2,512,384]{2,1,0:T(8,128)(2,1)} %rest_0_, bf16[2,512,384]{2,1,0:T(8,128)(2,1)} %collective-permute-done.7.rest_3_.rest_1_, ...), custom_call_target="tpu_custom_call" | custom-call | flops 6442450944 | bytes 6291456 | tf_op jit(solution)/shard_map/pallas_call | solution.py:222
  94.7 3.5 %collective-permute-start.15 = (bf16[2,256,512]{2,1,0:T(8,128)(2,1)S(1)}, bf16[2,256,512]{2,1,0:T(8,128)(2,1)S(1)}, u32[]{:S(2)}, u32[]{:S(2)}) collective-permute-start(bf16[2,256,512]{2,1,0:T(8,128)(2,1)S(1)} %shard_map.78), channel_id=1, source_target_pairs={{0,64},{8,72},{16,80},{24,88},{32,96},{40,104},{48,112},{56,120},{... | collective-permute-start | bytes 1572872 | tf_op jit(solution)/shard_map/ppermute | solution.py:37
  98.3 7.7 %shard_map.77 = (f32[1,256,384]{2,1,0:T(8,128)S(1)}, bf16[1,256,128]{2,1,0:T(8,128)(2,1)S(1)}) custom-call(bf16[1,272,384]{2,1,0:T(8,128)(2,1)S(1)} %get-tuple-element.51.q_ref, f32[2,2048]{1,0:T(2,128)S(1)} %add_convert_fusion.2.frame_ref, bf16[1,256,384]{2,1,0:T(8,128)(2,1)S(1)} %get-tuple-element.58.rest_0_, ...), custom_call_target="tpu_custom_call" | custom-call | flops 3221225472 | bytes 6291456 | tf_op jit(solution)/shard_map/pallas_call | solution.py:222
  106.0 4.3 %collective-permute-done.15.refs_4_ = bf16[2,256,512]{2,1,0:T(8,128)(2,1)S(1)} collective-permute-done((bf16[2,256,512]{2,1,0:T(8,128)(2,1)S(1)}, bf16[2,256,512]{2,1,0:T(8,128)(2,1)S(1)}, u32[]{:S(2)}, u32[]{:S(2)}) %collective-permute-start.15) | collective-permute-done | bytes 524320 | tf_op jit(solution)/shard_map/ppermute | solution.py:37
  110.3 1.2 shard_map.79
  111.6 5.8 %collective-permute-done.16.b_ref = bf16[2,128,384]{2,1,0:T(8,128)(2,1)S(1)} collective-permute-done((bf16[2,128,384]{2,1,0:T(8,128)(2,1)S(1)}, bf16[2,128,384]{2,1,0:T(8,128)(2,1)S(1)}, u32[]{:S(2)}, u32[]{:S(2)}) %collective-permute-start.16) | collective-permute-done | bytes 196640 | tf_op jit(solution)/shard_map/ppermute | solution.py:27
  117.4 5.5 %shard_map.80 = (bf16[2,32,5120]{2,1,0:T(8,128)(2,1)S(1)}, bf16[2,32,5120]{2,1,0:T(8,128)(2,1)S(1)}, bf16[2,32,5120]{2,1,0:T(8,128)(2,1)S(1)}, bf16[2,32,5120]{2,1,0:T(8,128)(2,1)S(1)}) custom-call(s32[1]{0:T(128)} %bitcast.1.core, bf16[2,128,384]{2,1,0:T(8,128)(2,1)S(1)} %get-tuple-element.44.a_ref, bf16[2,128,384]{2,1,0:T(8,128)(2,1)S(1)} %collective-permute-done.16.b_ref, ...), custom_call_target="tpu_custom_call" | custom-call | flops 2013265920 | bytes 10485760 | tf_op jit(solution)/shard_map/pallas_call | solution.py:302
  123.1 3.7 %collective-permute-start.21 = (bf16[2,32,5120]{2,1,0:T(8,128)(2,1)S(1)}, bf16[2,32,5120]{2,1,0:T(8,128)(2,1)S(1)}, u32[]{:S(2)}, u32[]{:S(2)}) collective-permute-start(bf16[2,32,5120]{2,1,0:T(8,128)(2,1)S(1)} %get-tuple-element.50), channel_id=1, source_target_pairs={{0,1},{1,2},{2,3},{3,0},{4,5},{5,6},{6,7},{7,4},{8,11},{9,8},{10,9... | collective-permute-start | bytes 1966088 | tf_op jit(solution)/shard_map/ppermute | solution.py:51
  126.8 15.4 %collective-permute-done.19 = bf16[2,32,5120]{2,1,0:T(8,128)(2,1)S(1)} collective-permute-done((bf16[2,32,5120]{2,1,0:T(8,128)(2,1)S(1)}, bf16[2,32,5120]{2,1,0:T(8,128)(2,1)S(1)}, u32[]{:S(2)}, u32[]{:S(2)}) %collective-permute-start.19) | collective-permute-done | bytes 655392 | tf_op jit(solution)/shard_map/ppermute | solution.py:51
  142.5 11.7 %collective-permute-done.20 = bf16[2,32,5120]{2,1,0:T(8,128)(2,1)S(1)} collective-permute-done((bf16[2,32,5120]{2,1,0:T(8,128)(2,1)S(1)}, bf16[2,32,5120]{2,1,0:T(8,128)(2,1)S(1)}, u32[]{:S(2)}, u32[]{:S(2)}) %collective-permute-start.20) | collective-permute-done | bytes 655392 | tf_op jit(solution)/shard_map/ppermute | solution.py:51
  154.2 1.2 add_convert_fusion
  (72 shorter events, 3.9 us)
Async XLA Ops:
  0.0 2.1 %copy-start.2 = (bf16[384,5120]{1,0:T(8,128)(2,1)S(1)}, bf16[384,5120]{1,0:T(8,128)(2,1)}, u32[]{:S(2)}) copy-start(bf16[384,5120]{1,0:T(8,128)(2,1)} %wa_ref.1) | copy-start | bytes 11796484
  2.1 1.1 copy-start.4
  3.2 1.0 copy-start.6
  4.9 34.3 %copy-start.10 = (s32[2]{0:T(128)S(1)}, s32[2]{0:T(128)}, u32[]{:S(2)}) copy-start(s32[2]{0:T(128)} %param.9) | copy-start | bytes 28
  6.9 14.4 %collective-permute-start = (bf16[2,32,5120]{2,1,0:T(8,128)(2,1)S(1)}, bf16[2,32,5120]{2,1,0:T(8,128)(2,1)}, u32[]{:S(2)}, u32[]{:S(2)}) collective-permute-start(bf16[2,32,5120]{2,1,0:T(8,128)(2,1)S(1)} %get-tuple-element.29.refs_0_), channel_id=1, source_target_pairs={{0,1},{1,2},{2,3},{3,0},{4,5},{5,6},{6,7},{7,4},{8,11},{9,8},{10,9... | collective-permute-start | bytes 1966088 | tf_op jit(solution)/shard_map/ppermute | solution.py:51
  7.2 21.2 %collective-permute-start.7 = (bf16[2,512,384]{2,1,0:T(8,128)(2,1)}, bf16[2,512,384]{2,1,0:T(8,128)(2,1)}, u32[]{:S(2)}, u32[]{:S(2)}) collective-permute-start(bf16[2,512,384]{2,1,0:T(8,128)(2,1)} %rest_0_), channel_id=1, source_target_pairs={{0,16},{1,17},{2,18},{3,19},{4,20},{5,21},{6,22},{7,23},{8,56},{9,... | collective-permute-start | bytes 2359304 | tf_op jit(solution)/shard_map/ppermute | solution.py:51
  8.4 50.9 %collective-permute-start.17 = (bf16[192,5120]{1,0:T(8,128)(2,1)}, bf16[192,5120]{1,0:T(8,128)(2,1)S(1)}, u32[]{:S(2)}, u32[]{:S(2)}) collective-permute-start(bf16[192,5120]{1,0:T(8,128)(2,1)} %get-tuple-element.46), channel_id=1, source_target_pairs={{0,68},{1,69},{2,70},{3,71},{4,64},{5,65},{6,66},{7,67},{8,76},{9,... | collective-permute-start | bytes 5898248 | tf_op jit(solution)/shard_map/ppermute | solution.py:59
  12.4 15.5 %collective-permute-start.2 = (bf16[2,32,5120]{2,1,0:T(8,128)(2,1)S(1)}, bf16[2,32,5120]{2,1,0:T(8,128)(2,1)S(1)}, u32[]{:S(2)}, u32[]{:S(2)}) collective-permute-start(bf16[2,32,5120]{2,1,0:T(8,128)(2,1)S(1)} %get-tuple-element.29.refs_0_), channel_id=1, source_target_pairs={{0,4},{1,5},{2,6},{3,7},{4,0},{5,1},{6,2},{7,3},{8,12},{9,13},{10,... | collective-permute-start | bytes 1966088 | tf_op jit(solution)/shard_map/ppermute | solution.py:27
  12.4 18.7 %collective-permute-start.1 = (bf16[2,32,5120]{2,1,0:T(8,128)(2,1)S(1)}, bf16[2,32,5120]{2,1,0:T(8,128)(2,1)}, u32[]{:S(2)}, u32[]{:S(2)}) collective-permute-start(bf16[2,32,5120]{2,1,0:T(8,128)(2,1)S(1)} %get-tuple-element.29.refs_0_), channel_id=1, source_target_pairs={{0,3},{1,0},{2,1},{3,2},{4,7},{5,4},{6,5},{7,6},{8,9},{9,10},{10,1... | collective-permute-start | bytes 1966088 | tf_op jit(solution)/shard_map/ppermute | solution.py:51
  21.2 14.4 %collective-permute-start.3 = (bf16[2,32,5120]{2,1,0:T(8,128)(2,1)}, bf16[2,32,5120]{2,1,0:T(8,128)(2,1)}, u32[]{:S(2)}, u32[]{:S(2)}) collective-permute-start(bf16[2,32,5120]{2,1,0:T(8,128)(2,1)} %collective-permute-done.refs_1_), channel_id=1, source_target_pairs={{0,1},{1,2},{2,3},{3,0},{4,5},{5,6},{6,7},{7,4},{8,11},{9,8},{10,9... | collective-permute-start | bytes 1966088 | tf_op jit(solution)/shard_map/ppermute | solution.py:51
  27.9 23.2 %collective-permute-start.5 = (bf16[2,32,5120]{2,1,0:T(8,128)(2,1)S(1)}, bf16[2,32,5120]{2,1,0:T(8,128)(2,1)S(1)}, u32[]{:S(2)}, u32[]{:S(2)}) collective-permute-start(bf16[2,32,5120]{2,1,0:T(8,128)(2,1)S(1)} %collective-permute-done.2.refs_3_), channel_id=1, source_target_pairs={{0,3},{1,0},{2,1},{3,2},{4,7},{5,4},{6,5},{7,6},{8,9},{9,10},{10,1... | collective-permute-start | bytes 1966088 | tf_op jit(solution)/shard_map/ppermute | solution.py:51
  28.3 23.2 %collective-permute-start.4 = (bf16[2,32,5120]{2,1,0:T(8,128)(2,1)S(1)}, bf16[2,32,5120]{2,1,0:T(8,128)(2,1)S(1)}, u32[]{:S(2)}, u32[]{:S(2)}) collective-permute-start(bf16[2,32,5120]{2,1,0:T(8,128)(2,1)S(1)} %collective-permute-done.2.refs_3_), channel_id=1, source_target_pairs={{0,1},{1,2},{2,3},{3,0},{4,5},{5,6},{6,7},{7,4},{8,11},{9,8},{10,9... | collective-permute-start | bytes 1966088 | tf_op jit(solution)/shard_map/ppermute | solution.py:51
  31.1 19.8 %collective-permute-start.8 = (bf16[2,512,384]{2,1,0:T(8,128)(2,1)}, bf16[2,512,384]{2,1,0:T(8,128)(2,1)S(1)}, u32[]{:S(2)}, u32[]{:S(2)}) collective-permute-start(bf16[2,512,384]{2,1,0:T(8,128)(2,1)} %rest_0_), channel_id=1, source_target_pairs={{0,48},{1,49},{2,50},{3,51},{4,52},{5,53},{6,54},{7,55},{8,24},{9,... | collective-permute-start | bytes 2359304 | tf_op jit(solution)/shard_map/ppermute | solution.py:51
  35.6 16.0 %collective-permute-start.6 = (bf16[2,32,5120]{2,1,0:T(8,128)(2,1)}, bf16[2,32,5120]{2,1,0:T(8,128)(2,1)S(1)}, u32[]{:S(2)}, u32[]{:S(2)}) collective-permute-start(bf16[2,32,5120]{2,1,0:T(8,128)(2,1)} %collective-permute-done.3.refs_0_), channel_id=1, source_target_pairs={{0,4},{1,5},{2,6},{3,7},{4,0},{5,1},{6,2},{7,3},{8,12},{9,13},{10,... | collective-permute-start | bytes 1966088 | tf_op jit(solution)/shard_map/ppermute | solution.py:27
  39.3 4.4 %copy-start = (bf16[5120,3,384]{2,0,1:T(8,128)(2,1)S(1)}, bf16[5120,3,384]{2,0,1:T(8,128)(2,1)}, u32[]{:S(2)}) copy-start(bf16[5120,3,384]{2,0,1:T(8,128)(2,1)} %param.11) | copy-start | bytes 35389444
  43.6 8.6 %copy-start.1 = (bf16[5120,3,384]{2,0,1:T(8,128)(2,1)S(1)}, bf16[5120,3,384]{2,0,1:T(8,128)(2,1)}, u32[]{:S(2)}) copy-start(bf16[5120,3,384]{2,0,1:T(8,128)(2,1)} %param.11) | copy-start | bytes 35389444
  51.0 13.0 %collective-permute-start.10 = (bf16[2,512,384]{2,1,0:T(8,128)(2,1)}, bf16[2,512,384]{2,1,0:T(8,128)(2,1)S(1)}, u32[]{:S(2)}, u32[]{:S(2)}) collective-permute-start(bf16[2,512,384]{2,1,0:T(8,128)(2,1)} %rest_0_), channel_id=1, source_target_pairs={{0,8},{8,0},{16,24},{24,16},{32,40},{40,32},{48,56},{56,48},{64,72... | collective-permute-start | bytes 2359304 | tf_op jit(solution)/shard_map/ppermute | solution.py:37
  51.1 19.0 %collective-permute-start.11 = (bf16[2,512,384]{2,1,0:T(8,128)(2,1)}, bf16[2,512,384]{2,1,0:T(8,128)(2,1)S(1)}, u32[]{:S(2)}, u32[]{:S(2)}) collective-permute-start(bf16[2,512,384]{2,1,0:T(8,128)(2,1)} %collective-permute-done.7.rest_3_.rest_1_), channel_id=1, source_target_pairs={{0,8},{8,0},{16,24},{24,16},{32,40},{40,32},{48,56},{56,48},{64,72... | collective-permute-start | bytes 2359304 | tf_op jit(solution)/shard_map/ppermute | solution.py:37
  51.6 12.2 %collective-permute-start.9 = (bf16[2,512,384]{2,1,0:T(8,128)(2,1)}, bf16[2,512,384]{2,1,0:T(8,128)(2,1)S(1)}, u32[]{:S(2)}, u32[]{:S(2)}) collective-permute-start(bf16[2,512,384]{2,1,0:T(8,128)(2,1)} %collective-permute-done.7.rest_3_.rest_1_), channel_id=1, source_target_pairs={{0,16},{1,17},{2,18},{3,19},{4,20},{5,21},{6,22},{7,23},{8,56},{9,... | collective-permute-start | bytes 2359304 | tf_op jit(solution)/shard_map/ppermute | solution.py:51
  51.6 18.5 %collective-permute-start.12 = (bf16[2,512,384]{2,1,0:T(8,128)(2,1)S(1)}, bf16[2,512,384]{2,1,0:T(8,128)(2,1)S(1)}, u32[]{:S(2)}, u32[]{:S(2)}) collective-permute-start(bf16[2,512,384]{2,1,0:T(8,128)(2,1)S(1)} %collective-permute-done.8.rest_4_.rest_2_), channel_id=1, source_target_pairs={{0,8},{8,0},{16,24},{24,16},{32,40},{40,32},{48,56},{56,48},{64,72... | collective-permute-start | bytes 2359304 | tf_op jit(solution)/shard_map/ppermute | solution.py:37
  59.3 58.1 %collective-permute-start.18 = (bf16[192,5120]{1,0:T(8,128)(2,1)S(1)}, bf16[192,5120]{1,0:T(8,128)(2,1)S(1)}, u32[]{:S(2)}, u32[]{:S(2)}) collective-permute-start(bf16[192,5120]{1,0:T(8,128)(2,1)S(1)} %collective-permute-done.17.near_ref), channel_id=1, source_target_pairs={{0,8},{8,0},{16,24},{24,16},{32,40},{40,32},{48,56},{56,48},{64,72... | collective-permute-start | bytes 5898248 | tf_op jit(solution)/shard_map/ppermute | solution.py:37
  63.8 6.3 %collective-permute-start.13 = (bf16[2,512,384]{2,1,0:T(8,128)(2,1)S(1)}, bf16[2,512,384]{2,1,0:T(8,128)(2,1)S(1)}, u32[]{:S(2)}, u32[]{:S(2)}) collective-permute-start(bf16[2,512,384]{2,1,0:T(8,128)(2,1)S(1)} %collective-permute-done.9.rest_5_.rest_3_), channel_id=1, source_target_pairs={{0,8},{8,0},{16,24},{24,16},{32,40},{40,32},{48,56},{56,48},{64,72... | collective-permute-start | bytes 2359304 | tf_op jit(solution)/shard_map/ppermute | solution.py:37
  64.0 16.4 %collective-permute-start.14 = (bf16[2,272,384]{2,1,0:T(8,128)(2,1)S(1)}, bf16[2,272,384]{2,1,0:T(8,128)(2,1)S(1)}, u32[]{:S(2)}, u32[]{:S(2)}) collective-permute-start(bf16[2,272,384]{2,1,0:T(8,128)(2,1)S(1)} %broadcast_dynamic-update-slice_fusion), channel_id=1, source_target_pairs={{0,64},{8,72},{16,80},{24,88},{32,96},{40,104},{48,112},{56,120},{... | collective-permute-start | bytes 1253384 | tf_op jit(solution)/shard_map/ppermute | solution.py:37
  70.1 7.9 %copy-start.8 = (bf16[2,512,384]{2,1,0:T(8,128)(2,1)}, bf16[2,512,384]{2,1,0:T(8,128)(2,1)S(1)}, u32[]{:S(2)}) copy-start(bf16[2,512,384]{2,1,0:T(8,128)(2,1)S(1)} %collective-permute-done.11.rest_7_.rest_5_) | copy-start | bytes 2359300
  80.3 1.1 copy-start.9
  94.7 15.6 %collective-permute-start.15 = (bf16[2,256,512]{2,1,0:T(8,128)(2,1)S(1)}, bf16[2,256,512]{2,1,0:T(8,128)(2,1)S(1)}, u32[]{:S(2)}, u32[]{:S(2)}) collective-permute-start(bf16[2,256,512]{2,1,0:T(8,128)(2,1)S(1)} %shard_map.78), channel_id=1, source_target_pairs={{0,64},{8,72},{16,80},{24,88},{32,96},{40,104},{48,112},{56,120},{... | collective-permute-start | bytes 1572872 | tf_op jit(solution)/shard_map/ppermute | solution.py:37
  98.3 19.2 %copy-start.3 = (bf16[384,5120]{1,0:T(8,128)(2,1)S(1)}, bf16[384,5120]{1,0:T(8,128)(2,1)}, u32[]{:S(2)}) copy-start(bf16[384,5120]{1,0:T(8,128)(2,1)} %wa_ref.1) | copy-start | bytes 11796484
  111.5 5.9 %collective-permute-start.16 = (bf16[2,128,384]{2,1,0:T(8,128)(2,1)S(1)}, bf16[2,128,384]{2,1,0:T(8,128)(2,1)S(1)}, u32[]{:S(2)}, u32[]{:S(2)}) collective-permute-start(bf16[2,128,384]{2,1,0:T(8,128)(2,1)S(1)} %get-tuple-element.45), channel_id=1, source_target_pairs={{0,4},{1,5},{2,6},{3,7},{4,0},{5,1},{6,2},{7,3},{8,12},{9,13},{10,... | collective-permute-start | bytes 589832 | tf_op jit(solution)/shard_map/ppermute | solution.py:27
  122.9 31.3 %copy-start.5 = (bf16[2,32,5120]{2,1,0:T(8,128)(2,1)S(1)}, bf16[2,32,5120]{2,1,0:T(8,128)(2,1)}, u32[]{:S(2)}) copy-start(bf16[2,32,5120]{2,1,0:T(8,128)(2,1)} %x_ref.1) | copy-start | bytes 1966084
  122.9 19.3 %collective-permute-start.19 = (bf16[2,32,5120]{2,1,0:T(8,128)(2,1)S(1)}, bf16[2,32,5120]{2,1,0:T(8,128)(2,1)S(1)}, u32[]{:S(2)}, u32[]{:S(2)}) collective-permute-start(bf16[2,32,5120]{2,1,0:T(8,128)(2,1)S(1)} %get-tuple-element.49), channel_id=1, source_target_pairs={{0,3},{1,0},{2,1},{3,2},{4,7},{5,4},{6,5},{7,6},{8,9},{9,10},{10,1... | collective-permute-start | bytes 1966088 | tf_op jit(solution)/shard_map/ppermute | solution.py:51
  123.1 19.4 %collective-permute-start.21 = (bf16[2,32,5120]{2,1,0:T(8,128)(2,1)S(1)}, bf16[2,32,5120]{2,1,0:T(8,128)(2,1)S(1)}, u32[]{:S(2)}, u32[]{:S(2)}) collective-permute-start(bf16[2,32,5120]{2,1,0:T(8,128)(2,1)S(1)} %get-tuple-element.50), channel_id=1, source_target_pairs={{0,1},{1,2},{2,3},{3,0},{4,5},{5,6},{6,7},{7,4},{8,11},{9,8},{10,9... | collective-permute-start | bytes 1966088 | tf_op jit(solution)/shard_map/ppermute | solution.py:51
  142.3 11.9 %collective-permute-start.20 = (bf16[2,32,5120]{2,1,0:T(8,128)(2,1)S(1)}, bf16[2,32,5120]{2,1,0:T(8,128)(2,1)S(1)}, u32[]{:S(2)}, u32[]{:S(2)}) collective-permute-start(bf16[2,32,5120]{2,1,0:T(8,128)(2,1)S(1)} %add_convert_fusion.1), channel_id=1, source_target_pairs={{0,3},{1,0},{2,1},{3,2},{4,7},{5,4},{6,5},{7,6},{8,9},{9,10},{10,1... | collective-permute-start | bytes 1966088 | tf_op jit(solution)/shard_map/ppermute | solution.py:51
  (1 other events, 0.7 us)

commit v3 on v2

--- a/solution.py
+++ b/solution.py
@@ -59,11 +59,22 @@
     return lax.ppermute(a, ("branch", "seq"), perm)
 
 
-def norm_kernel(actions, x_ref, table_ref, w_ref, hidden_ref, gate_ref, half_ref, sem):
-    count = half_ref.shape[0]
-    at = lax.rem(lax.axis_index("branch"), 2) * count
-    copy = pltpu.make_async_copy(w_ref.at[pl.ds(pl.multiple_of(at, 16), count)], half_ref, sem)
-    copy.start()
+def norm_kernel(
+    actions, x_hbm, table_hbm, w_hbm, hidden_ref, gate_ref, w_0, w_1, x_ref, table_ref, sems
+):
+    count = w_0.shape[0]
+    at = lax.rem(lax.axis_index("branch"), 2) * 2 * count
+    quarters = [pl.ds(pl.multiple_of(at + j * count, 16), count) for j in range(2)]
+    copies = [
+        pltpu.make_async_copy(x_hbm, x_ref, sems.at[0]),
+        pltpu.make_async_copy(table_hbm, table_ref, sems.at[1]),
+        pltpu.make_async_copy(w_hbm.at[quarters[0]], w_0, sems.at[2]),
+        pltpu.make_async_copy(w_hbm.at[quarters[1]], w_1, sems.at[3]),
+    ]
+    for copy in copies:
+        copy.start()
+    copies[0].wait()
+    copies[1].wait()
     rows = lax.broadcasted_iota(jnp.int32, (ACTIONS, 1), 0)
     for b in range(x_ref.shape[0]):
         pick = rows == actions[b]
@@ -79,21 +90,28 @@
         variance = jnp.mean(centred * centred, axis=-1, keepdims=True)
         normed = centred * (1.0 / jnp.sqrt(variance + 1e-06))
         hidden_ref[b] = (normed * (1.0 + scale) + shift).astype(jnp.bfloat16)
-    copy.wait()
+    copies[2].wait()
+    copies[3].wait()
 
 
 def norm(actions, x, table, w_out):
+    quarter = jax.ShapeDtypeStruct((w_out.shape[0] // 4, w_out.shape[1]), w_out.dtype)
     return pl.pallas_call(
         norm_kernel,
         out_shape=(
             jax.ShapeDtypeStruct(x.shape, jnp.bfloat16),
             jax.ShapeDtypeStruct((x.shape[0], 1, x.shape[2]), jnp.float32),
-            jax.ShapeDtypeStruct((w_out.shape[0] // 2, w_out.shape[1]), w_out.dtype),
+            quarter,
+            quarter,
         ),
-        in_specs=[SMEM, VMEM, VMEM, ANY],
-        out_specs=(VMEM, VMEM, ANY),
-        scratch_shapes=[pltpu.SemaphoreType.DMA],
-        compiler_params=pltpu.CompilerParams(vmem_limit_bytes=24 << 20),
+        in_specs=[SMEM, ANY, ANY, ANY],
+        out_specs=(VMEM,) * 4,
+        scratch_shapes=[
+            pltpu.VMEM(x.shape, x.dtype),
+            pltpu.VMEM(table.shape, table.dtype),
+            pltpu.SemaphoreType.DMA((4,)),
+        ],
+        compiler_params=pltpu.CompilerParams(vmem_limit_bytes=56 << 20),
     )(actions, x, table, w_out)
 
 
@@ -280,23 +298,25 @@
     )(*flat, packed)
 
 
-def out_kernel(core, a_ref, b_ref, wa_ref, near_ref, far_ref, *rest):
-    outs, w = rest[:-1], rest[-1]
-    half = near_ref.shape[0]
-    for side, ref in ((core[0], near_ref), (1 - core[0], far_ref)):
-        w[pl.ds(pl.multiple_of(side * half, 16), half)] = ref[...]
-    rows = a_ref.shape[1]
-    stack = lambda ref: jnp.concatenate([ref[b] for b in range(ref.shape[0])], axis=0)
-    o = (
-        jnp.dot(stack(a_ref), wa_ref[...], preferred_element_type=jnp.float32)
-        + jnp.dot(stack(b_ref), w[...], preferred_element_type=jnp.float32)
-    ).astype(jnp.bfloat16)
+def out_kernel(core, a_ref, b_ref, wa_ref, *rest):
+    pieces, outs, w = rest[:4], rest[4:-1], rest[-1]
+    count, depth = pieces[0].shape[0], wa_ref.shape[0]
+    w[:depth] = wa_ref[...]
+    for j, ref in enumerate(pieces):
+        side = core[0] if j < 2 else 1 - core[0]
+        at = depth + (side * 2 + j % 2) * count
+        w[pl.ds(pl.multiple_of(at, 16), count)] = ref[...]
+    rows, branches = a_ref.shape[1], range(a_ref.shape[0])
+    x = jnp.concatenate(
+        [jnp.concatenate([ref[b] for b in branches], axis=0) for ref in (a_ref, b_ref)], axis=1
+    )
+    o = jnp.dot(x, w[...], preferred_element_type=jnp.float32).astype(jnp.bfloat16)
     for b in range(a_ref.shape[0]):
         for j, ref in enumerate(outs):
             ref[b] = o[b * rows + j * 32 : b * rows + (j + 1) * 32]
 
 
-def project_out(core, a, b, wa, near, far):
+def project_out(core, a, b, wa, pieces):
     branches, rows, width, block = a.shape[0], a.shape[1], wa.shape[1], 512
     count = rows // 32
     return pl.pallas_call(
@@ -309,22 +329,22 @@
             pl.BlockSpec((branches, rows, WIDTH), lambda i: (0, 0, 0)),
             pl.BlockSpec((WIDTH, block), lambda i: (0, i)),
         ]
-        + [pl.BlockSpec((WIDTH // 2, block), lambda i: (0, i))] * 2,
+        + [pl.BlockSpec((WIDTH // 4, block), lambda i: (0, i))] * 4,
         out_specs=(pl.BlockSpec((branches, 32, block), lambda i: (0, 0, i)),) * count,
-        scratch_shapes=[pltpu.VMEM((WIDTH, block), jnp.bfloat16)],
+        scratch_shapes=[pltpu.VMEM((2 * WIDTH, block), jnp.bfloat16)],
         compiler_params=pltpu.CompilerParams(vmem_limit_bytes=24 << 20),
         cost_estimate=pl.CostEstimate(
             flops=4 * branches * rows * WIDTH * width,
             bytes_accessed=4 * WIDTH * width + 2 * branches * rows * width,
             transcendentals=0,
         ),
-    )(core, a, b, wa, near, far)
+    )(core, a, b, wa, *pieces)
 
 
 def shards(x, actions, visible_from, table, w_qkv, w_out, ctx):
     branch = lax.axis_index("branch")
     core, base = branch % 2, branch // 8 * 8
-    hidden, gate, half = norm(actions, x, jnp.transpose(table, (1, 0, 2)), w_out)
+    hidden, gate, *quarters = norm(actions, x, jnp.transpose(table, (1, 0, 2)), w_out)
     w = jnp.transpose(w_qkv, (1, 0, 2))
 
     a0 = hidden
@@ -333,15 +353,19 @@
     b1, b3 = turned(b0, "y", 1), turned(b0, "y", -1)
     b2 = along_seq(a2, 0, 1)
 
-    near = across_z(half)
+    near = across_z(quarters[0])
+    b2, near = lax.optimization_barrier((b2, near))
     far = along_branch(near, 0, 0, 1)
 
     ctx, _ = lax.optimization_barrier((ctx, hidden))
     c1 = turned(ctx, "x", 1)
-    c3 = turned(lax.optimization_barrier((ctx, c1))[0], "x", -1)
-    c2 = turned(lax.optimization_barrier((c1, c3))[0], "x", 1)
+    c3 = turned(ctx, "x", -1)
+    c2 = turned(c1, "x", 1)
     mine = [ctx, c1, c3, c2]
-    parts = mine + [along_branch(part, 0, 0, 1) for part in mine]
+    parts = list(mine)
+    for part in mine:
+        part, _ = lax.optimization_barrier((part, b0))
+        parts.append(along_branch(part, 0, 0, 1))
     at = branch // 2 % 4
     order = []
     for c in (core, 1 - core):
@@ -358,14 +382,20 @@
         for f, s, tail in zip(first, second, ([start], [], []))
     )
     far_q = along_branch(q, 0, 1)
+    quarter, _ = lax.optimization_barrier((quarters[1], q))
+    near_1 = across_z(quarter)
     o_0, s_0 = attend(q[:1], frames, parts, (k[:1], v[:1]))
     far_q, _ = lax.optimization_barrier((far_q, s_0))
-    packed = along_branch(attend(far_q, frames, parts), 0, 1)
-    o_1, s_1 = attend(q[1:], frames, parts, (k[1:], v[1:]))
+    far_o = attend(far_q, frames, parts)
+    packed = along_branch(far_o, 0, 1)
+    last, _ = lax.optimization_barrier((q[1:], far_o))
+    o_1, s_1 = attend(last, frames, parts, (k[1:], v[1:]))
+    near_1, packed, o_1 = lax.optimization_barrier((near_1, packed, o_1))
+    pieces = [near, near_1, far, along_branch(near_1, 0, 0, 1)]
     here, there = merge([(o_0, s_0), (o_1, s_1)], packed)
     other = along_seq(there, 0, 1)
     p0, p1, p3, p2 = project_out(
-        core.astype(jnp.int32).reshape(1), here, other, w_out, near, far
+        core.astype(jnp.int32).reshape(1), here, other, w_out, pieces
     )
     back = turned(p2, "y", -1)
     t3 = turned(p3, "y", 1)

time: 156 us -> 152 us (0.974)
  waiting for transfers between devices: 61.2 us -> 56.1 us
  local copies, waits for them, and re-layouts: 11.1 us -> 7.16 us
  starting transfers between devices: 29.7 us -> 33.3 us
    ppermute x3, starting transfers between devices: 3.71 us -> 9.95 us  [along_seq(): return lax.ppermute(a, 'seq', perm)]
    ppermute x1 -> x2, waiting for transfers between devices: 0.01 us -> 4.11 us  [across_z(): return lax.ppermute(a, ('branch', 'seq'), perm)]
    unnamed x31 -> x27, local copies, waits for them, and re-layouts: 10.6 us -> 6.68 us
    ppermute x3, waiting for transfers between devices: 12.3 us -> 8.63 us  [along_seq(): return lax.ppermute(a, 'seq', perm)]
    ppermute x11, waiting for transfers between devices: 42.2 us -> 38.7 us  [turned(): return lax.ppermute(a, ('branch', 'seq'), perm)]
    ppermute x7 -> x8, starting transfers between devices: 10.9 us -> 7.79 us  [along_branch(): return lax.ppermute(a, 'branch', perm)]
    pallas_call x1, Pallas kernels: 1.98 us -> 4.62 us  [norm(): pl.pallas_call(norm_kernel, out_shape=(jax.ShapeDtypeStruct(x.shape, jnp....]
    ppermute x7 -> x8, waiting for transfers between devices: 6.68 us -> 4.75 us  [along_branch(): return lax.ppermute(a, 'branch', perm)]
  transfers between devices with their start and end apart: 22 -> 24, of which waited for: 9 -> 9; matrix products, arithmetic and copies ran while one was open for 1% -> 1% of each run, Pallas kernels for 28% -> 29%
where the time goes in v3:
time: 152 us; the launch traced here: 151 us
  waiting for transfers between devices  56.1 us (37%)
  Pallas kernels  53 us (35%)
  starting transfers between devices  33.3 us (22%)
  local copies, waits for them, and re-layouts  7.16 us (5%)
    ppermute x11, waiting for transfers between devices, turned(): return lax.ppermute(a, ('branch', 'seq'), perm)  38.7 us
    pallas_call x3, Pallas kernels, attend(): pl.pallas_call(functools.partial(attend_kernel, branches, chunk, blocks,...  28.7 us
    pallas_call x2, Pallas kernels, project_qkv(): pl.pallas_call(functools.partial(qkv_kernel, count), grid=(depth // block...  13.3 us
    ppermute x11, starting transfers between devices, turned(): return lax.ppermute(a, ('branch', 'seq'), perm)  11.7 us
    ppermute x3, starting transfers between devices, along_seq(): return lax.ppermute(a, 'seq', perm)  9.95 us
    ppermute x3, waiting for transfers between devices, along_seq(): return lax.ppermute(a, 'seq', perm)  8.63 us
    ppermute x8, starting transfers between devices, along_branch(): return lax.ppermute(a, 'branch', perm)  7.79 us
    unnamed x27, local copies, waits for them, and re-layouts  6.68 us
  transfers between devices with their start and end apart: 24, of which 9 were waited for; matrix products, arithmetic and copies ran while one was open for 1% of the time, Pallas kernels for 29%

profile of v3, /device:TPU:28, one launch (start us, length us, event | category | flops | bytes accessed | tf_op | source)
XLA Modules:
  0.0 151.4 jit_solution(4803787051231231002)
XLA Ops:
  0.0 4.6 %shard_map.73 = (bf16[2,32,5120]{2,1,0:T(8,128)(2,1)}, f32[2,1,5120]{2,1,0:T(1,128)}, bf16[96,5120]{1,0:T(8,128)(2,1)}, bf16[96,5120]{1,0:T(8,128)(2,1)}) custom-call(s32[2]{0:T(128)} %actions.1, bf16[2,32,5120]{2,1,0:T(8,128)(2,1)} %x_hbm.1, bf16[3,16,5120]{2,1,0:T(8,128)(2,1)} %bitcast.22, bf16[384,5120]{1,0:T(8,128)(2,1)} %wa_ref.1), custom_call_target="tpu_custom_call" | custom-call | tf_op jit(solution)/shard_map/pallas_call | solution.py:99
  4.9 1.9 %collective-permute-start.2 = (bf16[2,32,5120]{2,1,0:T(8,128)(2,1)}, bf16[2,32,5120]{2,1,0:T(8,128)(2,1)S(1)}, u32[]{:S(2)}, u32[]{:S(2)}) collective-permute-start(bf16[2,32,5120]{2,1,0:T(8,128)(2,1)} %get-tuple-element.39.refs_0_), channel_id=1, source_target_pairs={{0,4},{1,5},{2,6},{3,7},{4,0},{5,1},{6,2},{7,3},{8,12},{9,13},{10,... | collective-permute-start | bytes 1966088 | tf_op jit(solution)/shard_map/ppermute | solution.py:27
  6.8 1.2 collective-permute-start.8
  8.9 1.8 %collective-permute-start.1 = (bf16[2,32,5120]{2,1,0:T(8,128)(2,1)}, bf16[2,32,5120]{2,1,0:T(8,128)(2,1)S(1)}, u32[]{:S(2)}, u32[]{:S(2)}) collective-permute-start(bf16[2,32,5120]{2,1,0:T(8,128)(2,1)} %get-tuple-element.39.refs_0_), channel_id=1, source_target_pairs={{0,3},{1,0},{2,1},{3,2},{4,7},{5,4},{6,5},{7,6},{8,9},{9,10},{10,1... | collective-permute-start | bytes 1966088 | tf_op jit(solution)/shard_map/ppermute | solution.py:51
  10.8 9.2 %collective-permute-done.refs_1_ = bf16[2,32,5120]{2,1,0:T(8,128)(2,1)S(1)} collective-permute-done((bf16[2,32,5120]{2,1,0:T(8,128)(2,1)}, bf16[2,32,5120]{2,1,0:T(8,128)(2,1)S(1)}, u32[]{:S(2)}, u32[]{:S(2)}) %collective-permute-start) | collective-permute-done | bytes 655392 | tf_op jit(solution)/shard_map/ppermute | solution.py:51
  20.2 1.9 %collective-permute-done.2.refs_3_ = bf16[2,32,5120]{2,1,0:T(8,128)(2,1)S(1)} collective-permute-done((bf16[2,32,5120]{2,1,0:T(8,128)(2,1)}, bf16[2,32,5120]{2,1,0:T(8,128)(2,1)S(1)}, u32[]{:S(2)}, u32[]{:S(2)}) %collective-permute-start.2) | collective-permute-done | bytes 655392 | tf_op jit(solution)/shard_map/ppermute | solution.py:27
  22.1 3.8 %collective-permute-start.7 = (bf16[96,5120]{1,0:T(8,128)(2,1)}, bf16[96,5120]{1,0:T(8,128)(2,1)S(1)}, u32[]{:S(2)}, u32[]{:S(2)}) collective-permute-start(bf16[96,5120]{1,0:T(8,128)(2,1)} %get-tuple-element.41), channel_id=1, source_target_pairs={{0,68},{1,69},{2,70},{3,71},{4,64},{5,65},{6,66},{7,67},{8,76},{9,... | collective-permute-start | bytes 2949128 | tf_op jit(solution)/shard_map/ppermute | solution.py:59
  25.9 2.5 %collective-permute-start.4 = (bf16[2,32,5120]{2,1,0:T(8,128)(2,1)S(1)}, bf16[2,32,5120]{2,1,0:T(8,128)(2,1)S(1)}, u32[]{:S(2)}, u32[]{:S(2)}) collective-permute-start(bf16[2,32,5120]{2,1,0:T(8,128)(2,1)S(1)} %collective-permute-done.2.refs_3_), channel_id=1, source_target_pairs={{0,1},{1,2},{2,3},{3,0},{4,5},{5,6},{6,7},{7,4},{8,11},{9,8},{10,9... | collective-permute-start | bytes 1966088 | tf_op jit(solution)/shard_map/ppermute | solution.py:51
  28.4 1.3 collective-permute-start.10
  29.7 3.7 %collective-permute-done.3.refs_0_ = bf16[2,32,5120]{2,1,0:T(8,128)(2,1)S(1)} collective-permute-done((bf16[2,32,5120]{2,1,0:T(8,128)(2,1)S(1)}, bf16[2,32,5120]{2,1,0:T(8,128)(2,1)S(1)}, u32[]{:S(2)}, u32[]{:S(2)}) %collective-permute-start.3) | collective-permute-done | bytes 655392 | tf_op jit(solution)/shard_map/ppermute | solution.py:51
  33.4 7.4 %collective-permute-start.6 = (bf16[2,32,5120]{2,1,0:T(8,128)(2,1)S(1)}, bf16[2,32,5120]{2,1,0:T(8,128)(2,1)S(1)}, u32[]{:S(2)}, u32[]{:S(2)}) collective-permute-start(bf16[2,32,5120]{2,1,0:T(8,128)(2,1)S(1)} %collective-permute-done.3.refs_0_), channel_id=1, source_target_pairs={{0,4},{1,5},{2,6},{3,7},{4,0},{5,1},{6,2},{7,3},{8,12},{9,13},{10,... | collective-permute-start | bytes 1966088 | tf_op jit(solution)/shard_map/ppermute | solution.py:27
  40.9 4.3 %copy-done = bf16[5120,3,384]{2,0,1:T(8,128)(2,1)S(1)} copy-done((bf16[5120,3,384]{2,0,1:T(8,128)(2,1)S(1)}, bf16[5120,3,384]{2,0,1:T(8,128)(2,1)}, u32[]{:S(2)}) %copy-start) | copy-done | bytes 11796504
  45.2 1.1 copy-done.3
  46.3 6.7 %shard_map.74 = (bf16[2,128,384]{2,1,0:T(8,128)(2,1)S(1)}, bf16[2,128,384]{2,1,0:T(8,128)(2,1)S(1)}, bf16[2,128,384]{2,1,0:T(8,128)(2,1)S(1)}) custom-call(bf16[2,32,5120]{2,1,0:T(8,128)(2,1)S(1)} %copy-done.3, bf16[2,32,5120]{2,1,0:T(8,128)(2,1)S(1)} %collective-permute-done.refs_1_, bf16[2,32,5120]{2,1,0:T(8,128)(2,1)S(1)} %collective-permute-done.1.refs_2_, ...), custom_call_target="tpu_custom_call" | custom-call | flops 3019898880 | bytes 14417920 | tf_op jit(solution)/shard_map/pallas_call | solution.py:142
  54.2 6.7 %shard_map.75 = (bf16[2,128,384]{2,1,0:T(8,128)(2,1)S(1)}, bf16[2,128,384]{2,1,0:T(8,128)(2,1)S(1)}, bf16[2,128,384]{2,1,0:T(8,128)(2,1)S(1)}) custom-call(bf16[2,32,5120]{2,1,0:T(8,128)(2,1)S(1)} %collective-permute-done.3.refs_0_, bf16[2,32,5120]{2,1,0:T(8,128)(2,1)S(1)} %collective-permute-done.4.refs_1_, ...), custom_call_target="tpu_custom_call" | custom-call | flops 3019898880 | bytes 14417920 | tf_op jit(solution)/shard_map/pallas_call | solution.py:142
  61.1 3.4 %collective-permute-start.16 = (bf16[2,272,384]{2,1,0:T(8,128)(2,1)S(1)}, bf16[2,272,384]{2,1,0:T(8,128)(2,1)S(1)}, u32[]{:S(2)}, u32[]{:S(2)}) collective-permute-start(bf16[2,272,384]{2,1,0:T(8,128)(2,1)S(1)} %broadcast_dynamic-update-slice_fusion), channel_id=1, source_target_pairs={{0,64},{8,72},{16,80},{24,88},{32,96},{40,104},{48,112},{56,120},{... | collective-permute-start | bytes 1253384 | tf_op jit(solution)/shard_map/ppermute | solution.py:37
  64.8 1.0 copy-done.7
  65.8 7.6 %shard_map.76 = (f32[1,256,384]{2,1,0:T(8,128)S(1)}, bf16[1,256,128]{2,1,0:T(8,128)(2,1)S(1)}) custom-call(bf16[1,272,384]{2,1,0:T(8,128)(2,1)S(1)} %get-tuple-element.72.q_ref, f32[2,2048]{1,0:T(2,128)S(1)} %add_convert_fusion.2.frame_ref, bf16[1,256,384]{2,1,0:T(8,128)(2,1)S(1)} %get-tuple-element.77.rest_0_, ...), custom_call_target="tpu_custom_call" | custom-call | flops 3221225472 | bytes 6291456 | tf_op jit(solution)/shard_map/pallas_call | solution.py:240
  73.5 1.1 collective-permute-done.16.q_ref
  74.5 13.3 %shard_map.77 = bf16[2,256,512]{2,1,0:T(8,128)(2,1)S(1)} custom-call(bf16[2,272,384]{2,1,0:T(8,128)(2,1)S(1)} %collective-permute-done.16.q_ref, f32[2,2048]{1,0:T(2,128)S(1)} %add_convert_fusion.2.frame_ref, bf16[2,512,384]{2,1,0:T(8,128)(2,1)S(1)} %copy-done.4, bf16[2,512,384]{2,1,0:T(8,128)(2,1)} %collective-permute-done.8.rest_3_.rest_1_, ...), custom_call_target="tpu_custom_call" | custom-call | flops 6442450944 | bytes 6291456 | tf_op jit(solution)/shard_map/pallas_call | solution.py:240
  87.9 3.3 %collective-permute-start.17 = (bf16[2,256,512]{2,1,0:T(8,128)(2,1)S(1)}, bf16[2,256,512]{2,1,0:T(8,128)(2,1)S(1)}, u32[]{:S(2)}, u32[]{:S(2)}) collective-permute-start(bf16[2,256,512]{2,1,0:T(8,128)(2,1)S(1)} %shard_map.77), channel_id=1, source_target_pairs={{0,64},{8,72},{16,80},{24,88},{32,96},{40,104},{48,112},{56,120},{... | collective-permute-start | bytes 1572872 | tf_op jit(solution)/shard_map/ppermute | solution.py:37
  91.2 7.8 %shard_map.78 = (f32[1,256,384]{2,1,0:T(8,128)S(1)}, bf16[1,256,128]{2,1,0:T(8,128)(2,1)S(1)}) custom-call(bf16[1,272,384]{2,1,0:T(8,128)(2,1)S(1)} %get-tuple-element.58.q_ref, f32[2,2048]{1,0:T(2,128)S(1)} %add_convert_fusion.2.frame_ref, bf16[1,256,384]{2,1,0:T(8,128)(2,1)S(1)} %get-tuple-element.78.rest_0_, ...), custom_call_target="tpu_custom_call" | custom-call | flops 3221225472 | bytes 6291456 | tf_op jit(solution)/shard_map/pallas_call | solution.py:240
  98.9 3.7 %collective-permute-done.17.refs_4_ = bf16[2,256,512]{2,1,0:T(8,128)(2,1)S(1)} collective-permute-done((bf16[2,256,512]{2,1,0:T(8,128)(2,1)S(1)}, bf16[2,256,512]{2,1,0:T(8,128)(2,1)S(1)}, u32[]{:S(2)}, u32[]{:S(2)}) %collective-permute-start.17) | collective-permute-done | bytes 524320 | tf_op jit(solution)/shard_map/ppermute | solution.py:37
  102.6 4.1 %collective-permute-done.15.rest_1_ = bf16[96,5120]{1,0:T(8,128)(2,1)S(1)} collective-permute-done((bf16[96,5120]{1,0:T(8,128)(2,1)S(1)}, bf16[96,5120]{1,0:T(8,128)(2,1)S(1)}, u32[]{:S(2)}, u32[]{:S(2)}) %collective-permute-start.15) | collective-permute-done | bytes 983072 | tf_op jit(solution)/shard_map/ppermute | solution.py:59
  106.7 1.2 shard_map.79
  108.5 6.8 %collective-permute-done.18.b_ref = bf16[2,128,384]{2,1,0:T(8,128)(2,1)S(1)} collective-permute-done((bf16[2,128,384]{2,1,0:T(8,128)(2,1)S(1)}, bf16[2,128,384]{2,1,0:T(8,128)(2,1)S(1)}, u32[]{:S(2)}, u32[]{:S(2)}) %collective-permute-start.18) | collective-permute-done | bytes 196640 | tf_op jit(solution)/shard_map/ppermute | solution.py:27
  115.3 5.1 %shard_map.80 = (bf16[2,32,5120]{2,1,0:T(8,128)(2,1)S(1)}, bf16[2,32,5120]{2,1,0:T(8,128)(2,1)S(1)}, bf16[2,32,5120]{2,1,0:T(8,128)(2,1)S(1)}, bf16[2,32,5120]{2,1,0:T(8,128)(2,1)S(1)}) custom-call(s32[1]{0:T(128)} %bitcast.1.core, bf16[2,128,384]{2,1,0:T(8,128)(2,1)S(1)} %get-tuple-element.63.a_ref, bf16[2,128,384]{2,1,0:T(8,128)(2,1)S(1)} %collective-permute-done.18.b_ref, ...), custom_call_target="tpu_custom_call" | custom-call | flops 2013265920 | bytes 10485760 | tf_op jit(solution)/shard_map/pallas_call | solution.py:322
  120.5 1.4 collective-permute-start.21
  121.9 1.9 %collective-permute-start.23 = (bf16[2,32,5120]{2,1,0:T(8,128)(2,1)S(1)}, bf16[2,32,5120]{2,1,0:T(8,128)(2,1)S(1)}, u32[]{:S(2)}, u32[]{:S(2)}) collective-permute-start(bf16[2,32,5120]{2,1,0:T(8,128)(2,1)S(1)} %get-tuple-element.70), channel_id=1, source_target_pairs={{0,1},{1,2},{2,3},{3,0},{4,5},{5,6},{6,7},{7,4},{8,11},{9,8},{10,9... | collective-permute-start | bytes 1966088 | tf_op jit(solution)/shard_map/ppermute | solution.py:51
  123.8 14.4 %collective-permute-done.21 = bf16[2,32,5120]{2,1,0:T(8,128)(2,1)S(1)} collective-permute-done((bf16[2,32,5120]{2,1,0:T(8,128)(2,1)S(1)}, bf16[2,32,5120]{2,1,0:T(8,128)(2,1)S(1)}, u32[]{:S(2)}, u32[]{:S(2)}) %collective-permute-start.21) | collective-permute-done | bytes 655392 | tf_op jit(solution)/shard_map/ppermute | solution.py:51
  138.9 11.3 %collective-permute-done.22 = bf16[2,32,5120]{2,1,0:T(8,128)(2,1)S(1)} collective-permute-done((bf16[2,32,5120]{2,1,0:T(8,128)(2,1)S(1)}, bf16[2,32,5120]{2,1,0:T(8,128)(2,1)S(1)}, u32[]{:S(2)}, u32[]{:S(2)}) %collective-permute-start.22) | collective-permute-done | bytes 655392 | tf_op jit(solution)/shard_map/ppermute | solution.py:51
  150.2 1.2 add_convert_fusion
  (72 shorter events, 4.4 us)
Async XLA Ops:
  0.0 6.8 %copy-start.4 = (bf16[2,512,384]{2,1,0:T(8,128)(2,1)S(1)}, bf16[2,512,384]{2,1,0:T(8,128)(2,1)}, u32[]{:S(2)}) copy-start(bf16[2,512,384]{2,1,0:T(8,128)(2,1)} %rest_2_.1) | copy-start | bytes 2359300
  0.0 40.9 %copy-start.8 = (s32[2]{0:T(128)S(1)}, s32[2]{0:T(128)}, u32[]{:S(2)}) copy-start(s32[2]{0:T(128)} %param.9) | copy-start | bytes 28
  4.6 15.4 %collective-permute-start = (bf16[2,32,5120]{2,1,0:T(8,128)(2,1)}, bf16[2,32,5120]{2,1,0:T(8,128)(2,1)S(1)}, u32[]{:S(2)}, u32[]{:S(2)}) collective-permute-start(bf16[2,32,5120]{2,1,0:T(8,128)(2,1)} %get-tuple-element.39.refs_0_), channel_id=1, source_target_pairs={{0,1},{1,2},{2,3},{3,0},{4,5},{5,6},{6,7},{7,4},{8,11},{9,8},{10,9... | collective-permute-start | bytes 1966088 | tf_op jit(solution)/shard_map/ppermute | solution.py:51
  4.9 17.1 %collective-permute-start.2 = (bf16[2,32,5120]{2,1,0:T(8,128)(2,1)}, bf16[2,32,5120]{2,1,0:T(8,128)(2,1)S(1)}, u32[]{:S(2)}, u32[]{:S(2)}) collective-permute-start(bf16[2,32,5120]{2,1,0:T(8,128)(2,1)} %get-tuple-element.39.refs_0_), channel_id=1, source_target_pairs={{0,4},{1,5},{2,6},{3,7},{4,0},{5,1},{6,2},{7,3},{8,12},{9,13},{10,... | collective-permute-start | bytes 1966088 | tf_op jit(solution)/shard_map/ppermute | solution.py:27
  6.8 21.6 %collective-permute-start.8 = (bf16[2,512,384]{2,1,0:T(8,128)(2,1)S(1)}, bf16[2,512,384]{2,1,0:T(8,128)(2,1)}, u32[]{:S(2)}, u32[]{:S(2)}) collective-permute-start(bf16[2,512,384]{2,1,0:T(8,128)(2,1)S(1)} %copy-done.4), channel_id=1, source_target_pairs={{0,16},{1,17},{2,18},{3,19},{4,20},{5,21},{6,22},{7,23},{8,56},{9,... | collective-permute-start | bytes 2359304 | tf_op jit(solution)/shard_map/ppermute | solution.py:51
  8.0 20.4 %collective-permute-start.9 = (bf16[2,512,384]{2,1,0:T(8,128)(2,1)S(1)}, bf16[2,512,384]{2,1,0:T(8,128)(2,1)}, u32[]{:S(2)}, u32[]{:S(2)}) collective-permute-start(bf16[2,512,384]{2,1,0:T(8,128)(2,1)S(1)} %copy-done.4), channel_id=1, source_target_pairs={{0,48},{1,49},{2,50},{3,51},{4,52},{5,53},{6,54},{7,55},{8,24},{9,... | collective-permute-start | bytes 2359304 | tf_op jit(solution)/shard_map/ppermute | solution.py:51
  8.9 17.0 %collective-permute-start.1 = (bf16[2,32,5120]{2,1,0:T(8,128)(2,1)}, bf16[2,32,5120]{2,1,0:T(8,128)(2,1)S(1)}, u32[]{:S(2)}, u32[]{:S(2)}) collective-permute-start(bf16[2,32,5120]{2,1,0:T(8,128)(2,1)} %get-tuple-element.39.refs_0_), channel_id=1, source_target_pairs={{0,3},{1,0},{2,1},{3,2},{4,7},{5,4},{6,5},{7,6},{8,9},{9,10},{10,1... | collective-permute-start | bytes 1966088 | tf_op jit(solution)/shard_map/ppermute | solution.py:51
  20.0 13.4 %collective-permute-start.3 = (bf16[2,32,5120]{2,1,0:T(8,128)(2,1)S(1)}, bf16[2,32,5120]{2,1,0:T(8,128)(2,1)S(1)}, u32[]{:S(2)}, u32[]{:S(2)}) collective-permute-start(bf16[2,32,5120]{2,1,0:T(8,128)(2,1)S(1)} %collective-permute-done.refs_1_), channel_id=1, source_target_pairs={{0,1},{1,2},{2,3},{3,0},{4,5},{5,6},{6,7},{7,4},{8,11},{9,8},{10,9... | collective-permute-start | bytes 1966088 | tf_op jit(solution)/shard_map/ppermute | solution.py:51
  22.1 31.2 %collective-permute-start.7 = (bf16[96,5120]{1,0:T(8,128)(2,1)}, bf16[96,5120]{1,0:T(8,128)(2,1)S(1)}, u32[]{:S(2)}, u32[]{:S(2)}) collective-permute-start(bf16[96,5120]{1,0:T(8,128)(2,1)} %get-tuple-element.41), channel_id=1, source_target_pairs={{0,68},{1,69},{2,70},{3,71},{4,64},{5,65},{6,66},{7,67},{8,76},{9,... | collective-permute-start | bytes 2949128 | tf_op jit(solution)/shard_map/ppermute | solution.py:59
  25.9 27.9 %collective-permute-start.4 = (bf16[2,32,5120]{2,1,0:T(8,128)(2,1)S(1)}, bf16[2,32,5120]{2,1,0:T(8,128)(2,1)S(1)}, u32[]{:S(2)}, u32[]{:S(2)}) collective-permute-start(bf16[2,32,5120]{2,1,0:T(8,128)(2,1)S(1)} %collective-permute-done.2.refs_3_), channel_id=1, source_target_pairs={{0,1},{1,2},{2,3},{3,0},{4,5},{5,6},{6,7},{7,4},{8,11},{9,8},{10,9... | collective-permute-start | bytes 1966088 | tf_op jit(solution)/shard_map/ppermute | solution.py:51
  28.4 25.8 %collective-permute-start.5 = (bf16[2,32,5120]{2,1,0:T(8,128)(2,1)S(1)}, bf16[2,32,5120]{2,1,0:T(8,128)(2,1)S(1)}, u32[]{:S(2)}, u32[]{:S(2)}) collective-permute-start(bf16[2,32,5120]{2,1,0:T(8,128)(2,1)S(1)} %collective-permute-done.2.refs_3_), channel_id=1, source_target_pairs={{0,3},{1,0},{2,1},{3,2},{4,7},{5,4},{6,5},{7,6},{8,9},{9,10},{10,1... | collective-permute-start | bytes 1966088 | tf_op jit(solution)/shard_map/ppermute | solution.py:51
  28.4 24.7 %collective-permute-start.10 = (bf16[2,512,384]{2,1,0:T(8,128)(2,1)}, bf16[2,512,384]{2,1,0:T(8,128)(2,1)S(1)}, u32[]{:S(2)}, u32[]{:S(2)}) collective-permute-start(bf16[2,512,384]{2,1,0:T(8,128)(2,1)} %collective-permute-done.8.rest_3_.rest_1_), channel_id=1, source_target_pairs={{0,16},{1,17},{2,18},{3,19},{4,20},{5,21},{6,22},{7,23},{8,56},{9,... | collective-permute-start | bytes 2359304 | tf_op jit(solution)/shard_map/ppermute | solution.py:51
  33.4 20.3 %collective-permute-start.6 = (bf16[2,32,5120]{2,1,0:T(8,128)(2,1)S(1)}, bf16[2,32,5120]{2,1,0:T(8,128)(2,1)S(1)}, u32[]{:S(2)}, u32[]{:S(2)}) collective-permute-start(bf16[2,32,5120]{2,1,0:T(8,128)(2,1)S(1)} %collective-permute-done.3.refs_0_), channel_id=1, source_target_pairs={{0,4},{1,5},{2,6},{3,7},{4,0},{5,1},{6,2},{7,3},{8,12},{9,13},{10,... | collective-permute-start | bytes 1966088 | tf_op jit(solution)/shard_map/ppermute | solution.py:27
  40.9 4.4 %copy-start = (bf16[5120,3,384]{2,0,1:T(8,128)(2,1)S(1)}, bf16[5120,3,384]{2,0,1:T(8,128)(2,1)}, u32[]{:S(2)}) copy-start(bf16[5120,3,384]{2,0,1:T(8,128)(2,1)} %param.11) | copy-start | bytes 35389444
  46.3 7.9 %copy-start.1 = (bf16[5120,3,384]{2,0,1:T(8,128)(2,1)S(1)}, bf16[5120,3,384]{2,0,1:T(8,128)(2,1)}, u32[]{:S(2)}) copy-start(bf16[5120,3,384]{2,0,1:T(8,128)(2,1)} %param.11) | copy-start | bytes 35389444
  53.1 11.7 %collective-permute-start.11 = (bf16[2,512,384]{2,1,0:T(8,128)(2,1)S(1)}, bf16[2,512,384]{2,1,0:T(8,128)(2,1)S(1)}, u32[]{:S(2)}, u32[]{:S(2)}) collective-permute-start(bf16[2,512,384]{2,1,0:T(8,128)(2,1)S(1)} %copy-done.4), channel_id=1, source_target_pairs={{0,8},{8,0},{16,24},{24,16},{32,40},{40,32},{48,56},{56,48},{64,72... | collective-permute-start | bytes 2359304 | tf_op jit(solution)/shard_map/ppermute | solution.py:37
  53.2 12.6 %collective-permute-start.12 = (bf16[2,512,384]{2,1,0:T(8,128)(2,1)}, bf16[2,512,384]{2,1,0:T(8,128)(2,1)S(1)}, u32[]{:S(2)}, u32[]{:S(2)}) collective-permute-start(bf16[2,512,384]{2,1,0:T(8,128)(2,1)} %collective-permute-done.8.rest_3_.rest_1_), channel_id=1, source_target_pairs={{0,8},{8,0},{16,24},{24,16},{32,40},{40,32},{48,56},{56,48},{64,72... | collective-permute-start | bytes 2359304 | tf_op jit(solution)/shard_map/ppermute | solution.py:37
  53.7 12.1 %collective-permute-start.13 = (bf16[2,512,384]{2,1,0:T(8,128)(2,1)}, bf16[2,512,384]{2,1,0:T(8,128)(2,1)S(1)}, u32[]{:S(2)}, u32[]{:S(2)}) collective-permute-start(bf16[2,512,384]{2,1,0:T(8,128)(2,1)} %collective-permute-done.9.rest_4_.rest_2_), channel_id=1, source_target_pairs={{0,8},{8,0},{16,24},{24,16},{32,40},{40,32},{48,56},{56,48},{64,72... | collective-permute-start | bytes 2359304 | tf_op jit(solution)/shard_map/ppermute | solution.py:37
  53.8 12.0 %collective-permute-start.14 = (bf16[2,512,384]{2,1,0:T(8,128)(2,1)S(1)}, bf16[2,512,384]{2,1,0:T(8,128)(2,1)S(1)}, u32[]{:S(2)}, u32[]{:S(2)}) collective-permute-start(bf16[2,512,384]{2,1,0:T(8,128)(2,1)S(1)} %collective-permute-done.10.rest_5_.rest_3_), channel_id=1, source_target_pairs={{0,8},{8,0},{16,24},{24,16},{32,40},{40,32},{48,56},{56,48},{64,72... | collective-permute-start | bytes 2359304 | tf_op jit(solution)/shard_map/ppermute | solution.py:37
  61.1 13.4 %collective-permute-start.16 = (bf16[2,272,384]{2,1,0:T(8,128)(2,1)S(1)}, bf16[2,272,384]{2,1,0:T(8,128)(2,1)S(1)}, u32[]{:S(2)}, u32[]{:S(2)}) collective-permute-start(bf16[2,272,384]{2,1,0:T(8,128)(2,1)S(1)} %broadcast_dynamic-update-slice_fusion), channel_id=1, source_target_pairs={{0,64},{8,72},{16,80},{24,88},{32,96},{40,104},{48,112},{56,120},{... | collective-permute-start | bytes 1253384 | tf_op jit(solution)/shard_map/ppermute | solution.py:37
  64.6 1.2 copy-start.7
  65.8 40.9 %collective-permute-start.15 = (bf16[96,5120]{1,0:T(8,128)(2,1)S(1)}, bf16[96,5120]{1,0:T(8,128)(2,1)S(1)}, u32[]{:S(2)}, u32[]{:S(2)}) collective-permute-start(bf16[96,5120]{1,0:T(8,128)(2,1)S(1)} %copy-done.7), channel_id=1, source_target_pairs={{0,68},{1,69},{2,70},{3,71},{4,64},{5,65},{6,66},{7,67},{8,76},{9,... | collective-permute-start | bytes 2949128 | tf_op jit(solution)/shard_map/ppermute | solution.py:59
  87.9 14.8 %collective-permute-start.17 = (bf16[2,256,512]{2,1,0:T(8,128)(2,1)S(1)}, bf16[2,256,512]{2,1,0:T(8,128)(2,1)S(1)}, u32[]{:S(2)}, u32[]{:S(2)}) collective-permute-start(bf16[2,256,512]{2,1,0:T(8,128)(2,1)S(1)} %shard_map.77), channel_id=1, source_target_pairs={{0,64},{8,72},{16,80},{24,88},{32,96},{40,104},{48,112},{56,120},{... | collective-permute-start | bytes 1572872 | tf_op jit(solution)/shard_map/ppermute | solution.py:37
  91.2 17.4 %collective-permute-start.19 = (bf16[96,5120]{1,0:T(8,128)(2,1)S(1)}, bf16[96,5120]{1,0:T(8,128)(2,1)S(1)}, u32[]{:S(2)}, u32[]{:S(2)}) collective-permute-start(bf16[96,5120]{1,0:T(8,128)(2,1)S(1)} %collective-permute-done.7.rest_0_), channel_id=1, source_target_pairs={{0,8},{8,0},{16,24},{24,16},{32,40},{40,32},{48,56},{56,48},{64,72... | collective-permute-start | bytes 2949128 | tf_op jit(solution)/shard_map/ppermute | solution.py:37
  91.2 24.2 %copy-start.2 = (bf16[384,5120]{1,0:T(8,128)(2,1)S(1)}, bf16[384,5120]{1,0:T(8,128)(2,1)}, u32[]{:S(2)}) copy-start(bf16[384,5120]{1,0:T(8,128)(2,1)} %wa_ref.1) | copy-start | bytes 11796484
  106.7 8.6 %collective-permute-start.20 = (bf16[96,5120]{1,0:T(8,128)(2,1)S(1)}, bf16[96,5120]{1,0:T(8,128)(2,1)S(1)}, u32[]{:S(2)}, u32[]{:S(2)}) collective-permute-start(bf16[96,5120]{1,0:T(8,128)(2,1)S(1)} %collective-permute-done.15.rest_1_), channel_id=1, source_target_pairs={{0,8},{8,0},{16,24},{24,16},{32,40},{40,32},{48,56},{56,48},{64,72... | collective-permute-start | bytes 2949128 | tf_op jit(solution)/shard_map/ppermute | solution.py:37
  107.9 7.4 %collective-permute-start.18 = (bf16[2,128,384]{2,1,0:T(8,128)(2,1)S(1)}, bf16[2,128,384]{2,1,0:T(8,128)(2,1)S(1)}, u32[]{:S(2)}, u32[]{:S(2)}) collective-permute-start(bf16[2,128,384]{2,1,0:T(8,128)(2,1)S(1)} %get-tuple-element.64), channel_id=1, source_target_pairs={{0,4},{1,5},{2,6},{3,7},{4,0},{5,1},{6,2},{7,3},{8,12},{9,13},{10,... | collective-permute-start | bytes 589832 | tf_op jit(solution)/shard_map/ppermute | solution.py:27
  120.4 18.4 %copy-start.6 = (f32[2,1,5120]{2,1,0:T(1,128)S(1)}, f32[2,1,5120]{2,1,0:T(1,128)}, u32[]{:S(2)}) copy-start(f32[2,1,5120]{2,1,0:T(1,128)} %get-tuple-element.38) | copy-start | bytes 122884
  120.5 29.8 %copy-start.5 = (bf16[2,32,5120]{2,1,0:T(8,128)(2,1)S(1)}, bf16[2,32,5120]{2,1,0:T(8,128)(2,1)}, u32[]{:S(2)}) copy-start(bf16[2,32,5120]{2,1,0:T(8,128)(2,1)} %x_hbm.1) | copy-start | bytes 1966084
  120.5 17.7 %collective-permute-start.21 = (bf16[2,32,5120]{2,1,0:T(8,128)(2,1)S(1)}, bf16[2,32,5120]{2,1,0:T(8,128)(2,1)S(1)}, u32[]{:S(2)}, u32[]{:S(2)}) collective-permute-start(bf16[2,32,5120]{2,1,0:T(8,128)(2,1)S(1)} %get-tuple-element.69), channel_id=1, source_target_pairs={{0,3},{1,0},{2,1},{3,2},{4,7},{5,4},{6,5},{7,6},{8,9},{9,10},{10,1... | collective-permute-start | bytes 1966088 | tf_op jit(solution)/shard_map/ppermute | solution.py:51
  121.9 17.0 %collective-permute-start.23 = (bf16[2,32,5120]{2,1,0:T(8,128)(2,1)S(1)}, bf16[2,32,5120]{2,1,0:T(8,128)(2,1)S(1)}, u32[]{:S(2)}, u32[]{:S(2)}) collective-permute-start(bf16[2,32,5120]{2,1,0:T(8,128)(2,1)S(1)} %get-tuple-element.70), channel_id=1, source_target_pairs={{0,1},{1,2},{2,3},{3,0},{4,5},{5,6},{6,7},{7,4},{8,11},{9,8},{10,9... | collective-permute-start | bytes 1966088 | tf_op jit(solution)/shard_map/ppermute | solution.py:51
  138.3 11.9 %collective-permute-start.22 = (bf16[2,32,5120]{2,1,0:T(8,128)(2,1)S(1)}, bf16[2,32,5120]{2,1,0:T(8,128)(2,1)S(1)}, u32[]{:S(2)}, u32[]{:S(2)}) collective-permute-start(bf16[2,32,5120]{2,1,0:T(8,128)(2,1)S(1)} %add_convert_fusion.1), channel_id=1, source_target_pairs={{0,3},{1,0},{2,1},{3,2},{4,7},{5,4},{6,5},{7,6},{8,9},{9,10},{10,1... | collective-permute-start | bytes 1966088 | tf_op jit(solution)/shard_map/ppermute | solution.py:51
  (1 other events, 1.1 us)

commit v4 on v3

--- a/solution.py
+++ b/solution.py
@@ -341,6 +341,10 @@
     )(core, a, b, wa, *pieces)
 
 
+def add(a, b):
+    return (a.astype(jnp.float32) + b.astype(jnp.float32)).astype(jnp.bfloat16)
+
+
 def shards(x, actions, visible_from, table, w_qkv, w_out, ctx):
     branch = lax.axis_index("branch")
     core, base = branch % 2, branch // 8 * 8
@@ -382,25 +386,35 @@
         for f, s, tail in zip(first, second, ([start], [], []))
     )
     far_q = along_branch(q, 0, 1)
-    quarter, _ = lax.optimization_barrier((quarters[1], q))
+    quarter, _ = lax.optimization_barrier((quarters[1], b2))
     near_1 = across_z(quarter)
     o_0, s_0 = attend(q[:1], frames, parts, (k[:1], v[:1]))
     far_q, _ = lax.optimization_barrier((far_q, s_0))
-    far_o = attend(far_q, frames, parts)
-    packed = along_branch(far_o, 0, 1)
-    last, _ = lax.optimization_barrier((q[1:], far_o))
+    far_0 = attend(far_q[:1], frames, parts)
+    packed_0 = along_branch(far_0, 0, 1)
+    far_q, _ = lax.optimization_barrier((far_q[1:], far_0))
+    far_1 = attend(far_q, frames, parts)
+    packed_1 = along_branch(far_1, 0, 1)
+    packed_0, _ = lax.optimization_barrier((packed_0, far_1))
+    here_0, there_0 = merge([(o_0, s_0)], packed_0)
+    other_0 = along_seq(there_0, 0, 1)
+    last, _ = lax.optimization_barrier((q[1:], there_0))
     o_1, s_1 = attend(last, frames, parts, (k[1:], v[1:]))
-    near_1, packed, o_1 = lax.optimization_barrier((near_1, packed, o_1))
+    near_1, packed_1, o_1, other_0 = lax.optimization_barrier((near_1, packed_1, o_1, other_0))
     pieces = [near, near_1, far, along_branch(near_1, 0, 0, 1)]
-    here, there = merge([(o_0, s_0), (o_1, s_1)], packed)
-    other = along_seq(there, 0, 1)
-    p0, p1, p3, p2 = project_out(
-        core.astype(jnp.int32).reshape(1), here, other, w_out, pieces
-    )
-    back = turned(p2, "y", -1)
-    t3 = turned(p3, "y", 1)
-    p1 = (p1.astype(jnp.float32) + back.astype(jnp.float32)).astype(jnp.bfloat16)
-    t1 = turned(p1, "y", -1)
+    here_1, there_1 = merge([(o_1, s_1)], packed_1)
+    other_1 = along_seq(there_1, 0, 1)
+
+    core = core.astype(jnp.int32).reshape(1)
+    here_0, _ = lax.optimization_barrier((here_0, there_1))
+    p0, p1, p3, p2 = project_out(core, here_0, other_0, w_out, pieces)
+    back, t3 = turned(p2, "y", -1), turned(p3, "y", 1)
+    other_1, _ = lax.optimization_barrier((other_1, p0))
+    r0, r1, r3, r2 = project_out(core, here_1, other_1, w_out, pieces)
+    t1 = turned(add(p1, back), "y", -1)
+    back, u3 = turned(r2, "y", -1), turned(r3, "y", 1)
+    u1 = turned(add(r1, back), "y", -1)
+    p0, t1, t3 = (jnp.concatenate(pair, 0) for pair in ((p0, r0), (t1, u1), (t3, u3)))
     sums = p0.astype(jnp.float32) + t1.astype(jnp.float32) + t3.astype(jnp.float32)
     return (x.astype(jnp.float32) + gate * sums).astype(jnp.bfloat16)
 

time: 152 us -> 145 us (0.954)
  waiting for transfers between devices: 56.1 us -> 42.2 us
  Pallas kernels: 53 us -> 58.1 us
    ppermute x3 -> x4, waiting for transfers between devices: 8.63 us -> 0.01 us  [along_seq(): return lax.ppermute(a, 'seq', perm)]
    ppermute x11 -> x14, starting transfers between devices: 11.7 us -> 16.4 us  [turned(): return lax.ppermute(a, ('branch', 'seq'), perm)]
    ppermute x3 -> x4, starting transfers between devices: 9.95 us -> 5.39 us  [along_seq(): return lax.ppermute(a, 'seq', perm)]
    ppermute x11 -> x14, waiting for transfers between devices: 38.7 us -> 35.4 us  [turned(): return lax.ppermute(a, ('branch', 'seq'), perm)]
    pallas_call x1 -> x2, Pallas kernels: 5.11 us -> 8.18 us  [project_out(): pl.pallas_call(out_kernel, grid=(width // block,), out_shape=(jax.ShapeDt...]
    pallas_call x3 -> x4, Pallas kernels: 28.7 us -> 30.6 us  [attend(): pl.pallas_call(functools.partial(attend_kernel, branches, chunk, blocks,...]
    ppermute x8 -> x9, waiting for transfers between devices: 4.75 us -> 3.12 us  [along_branch(): return lax.ppermute(a, 'branch', perm)]
    ppermute x8 -> x9, starting transfers between devices: 7.79 us -> 8.47 us  [along_branch(): return lax.ppermute(a, 'branch', perm)]
  transfers between devices with their start and end apart: 24 -> 29, of which waited for: 9 -> 12; matrix products, arithmetic and copies ran while one was open for 1% -> 1% of each run, Pallas kernels for 29% -> 34%
where the time goes in v4:
time: 145 us; the launch traced here: 144 us
  Pallas kernels  58.1 us (40%)
  waiting for transfers between devices  42.2 us (29%)
  starting transfers between devices  34.3 us (24%)
  local copies, waits for them, and re-layouts  7.21 us (5%)
  other arithmetic  1.5 us (1%)
    ppermute x14, waiting for transfers between devices, turned(): return lax.ppermute(a, ('branch', 'seq'), perm)  35.4 us
    pallas_call x4, Pallas kernels, attend(): pl.pallas_call(functools.partial(attend_kernel, branches, chunk, blocks,...  30.6 us
    ppermute x14, starting transfers between devices, turned(): return lax.ppermute(a, ('branch', 'seq'), perm)  16.4 us
    pallas_call x2, Pallas kernels, project_qkv(): pl.pallas_call(functools.partial(qkv_kernel, count), grid=(depth // block...  13.3 us
    ppermute x9, starting transfers between devices, along_branch(): return lax.ppermute(a, 'branch', perm)  8.47 us
    pallas_call x2, Pallas kernels, project_out(): pl.pallas_call(out_kernel, grid=(width // block,), out_shape=(jax.ShapeDt...  8.18 us
    unnamed x27, local copies, waits for them, and re-layouts  6.68 us
    ppermute x4, starting transfers between devices, along_seq(): return lax.ppermute(a, 'seq', perm)  5.39 us
  transfers between devices with their start and end apart: 29, of which 12 were waited for; matrix products, arithmetic and copies ran while one was open for 1% of the time, Pallas kernels for 34%

profile of v4, /device:TPU:28, one launch (start us, length us, event | category | flops | bytes accessed | tf_op | source)
XLA Modules:
  0.0 143.6 jit_solution(17942792171897494460)
XLA Ops:
  0.0 4.6 %shard_map.73 = (bf16[2,32,5120]{2,1,0:T(8,128)(2,1)}, f32[2,1,5120]{2,1,0:T(1,128)}, bf16[96,5120]{1,0:T(8,128)(2,1)}, bf16[96,5120]{1,0:T(8,128)(2,1)}) custom-call(s32[2]{0:T(128)} %actions.1, bf16[2,32,5120]{2,1,0:T(8,128)(2,1)} %x_hbm.1, bf16[3,16,5120]{2,1,0:T(8,128)(2,1)} %bitcast.22, bf16[384,5120]{1,0:T(8,128)(2,1)} %wa_ref.3), custom_call_target="tpu_custom_call" | custom-call | tf_op jit(solution)/shard_map/pallas_call | solution.py:99
  4.9 1.8 %collective-permute-start.1 = (bf16[2,32,5120]{2,1,0:T(8,128)(2,1)}, bf16[2,32,5120]{2,1,0:T(8,128)(2,1)S(1)}, u32[]{:S(2)}, u32[]{:S(2)}) collective-permute-start(bf16[2,32,5120]{2,1,0:T(8,128)(2,1)} %get-tuple-element.50.refs_0_), channel_id=1, source_target_pairs={{0,3},{1,0},{2,1},{3,2},{4,7},{5,4},{6,5},{7,6},{8,9},{9,10},{10,1... | collective-permute-start | bytes 1966088 | tf_op jit(solution)/shard_map/ppermute | solution.py:51
  8.8 1.9 %collective-permute-start.2 = (bf16[2,32,5120]{2,1,0:T(8,128)(2,1)}, bf16[2,32,5120]{2,1,0:T(8,128)(2,1)S(1)}, u32[]{:S(2)}, u32[]{:S(2)}) collective-permute-start(bf16[2,32,5120]{2,1,0:T(8,128)(2,1)} %get-tuple-element.50.refs_0_), channel_id=1, source_target_pairs={{0,4},{1,5},{2,6},{3,7},{4,0},{5,1},{6,2},{7,3},{8,12},{9,13},{10,... | collective-permute-start | bytes 1966088 | tf_op jit(solution)/shard_map/ppermute | solution.py:27
  10.8 11.1 %collective-permute-done.refs_1_ = bf16[2,32,5120]{2,1,0:T(8,128)(2,1)S(1)} collective-permute-done((bf16[2,32,5120]{2,1,0:T(8,128)(2,1)}, bf16[2,32,5120]{2,1,0:T(8,128)(2,1)S(1)}, u32[]{:S(2)}, u32[]{:S(2)}) %collective-permute-start) | collective-permute-done | bytes 655392 | tf_op jit(solution)/shard_map/ppermute | solution.py:51
  22.6 4.0 %collective-permute-start.7 = (bf16[96,5120]{1,0:T(8,128)(2,1)}, bf16[96,5120]{1,0:T(8,128)(2,1)S(1)}, u32[]{:S(2)}, u32[]{:S(2)}) collective-permute-start(bf16[96,5120]{1,0:T(8,128)(2,1)} %get-tuple-element.52), channel_id=1, source_target_pairs={{0,68},{1,69},{2,70},{3,71},{4,64},{5,65},{6,66},{7,67},{8,76},{9,... | collective-permute-start | bytes 2949128 | tf_op jit(solution)/shard_map/ppermute | solution.py:59
  26.7 1.7 %collective-permute-start.4 = (bf16[2,32,5120]{2,1,0:T(8,128)(2,1)S(1)}, bf16[2,32,5120]{2,1,0:T(8,128)(2,1)S(1)}, u32[]{:S(2)}, u32[]{:S(2)}) collective-permute-start(bf16[2,32,5120]{2,1,0:T(8,128)(2,1)S(1)} %collective-permute-done.2.refs_3_), channel_id=1, source_target_pairs={{0,1},{1,2},{2,3},{3,0},{4,5},{5,6},{6,7},{7,4},{8,11},{9,8},{10,9... | collective-permute-start | bytes 1966088 | tf_op jit(solution)/shard_map/ppermute | solution.py:51
  28.8 1.2 collective-permute-start.10
  30.0 6.5 %collective-permute-done.3.refs_0_ = bf16[2,32,5120]{2,1,0:T(8,128)(2,1)S(1)} collective-permute-done((bf16[2,32,5120]{2,1,0:T(8,128)(2,1)S(1)}, bf16[2,32,5120]{2,1,0:T(8,128)(2,1)S(1)}, u32[]{:S(2)}, u32[]{:S(2)}) %collective-permute-start.3) | collective-permute-done | bytes 655392 | tf_op jit(solution)/shard_map/ppermute | solution.py:51
  36.4 2.6 %collective-permute-start.6 = (bf16[2,32,5120]{2,1,0:T(8,128)(2,1)S(1)}, bf16[2,32,5120]{2,1,0:T(8,128)(2,1)S(1)}, u32[]{:S(2)}, u32[]{:S(2)}) collective-permute-start(bf16[2,32,5120]{2,1,0:T(8,128)(2,1)S(1)} %collective-permute-done.3.refs_0_), channel_id=1, source_target_pairs={{0,4},{1,5},{2,6},{3,7},{4,0},{5,1},{6,2},{7,3},{8,12},{9,13},{10,... | collective-permute-start | bytes 1966088 | tf_op jit(solution)/shard_map/ppermute | solution.py:27
  39.0 4.3 %copy-done = bf16[5120,3,384]{2,0,1:T(8,128)(2,1)S(1)} copy-done((bf16[5120,3,384]{2,0,1:T(8,128)(2,1)S(1)}, bf16[5120,3,384]{2,0,1:T(8,128)(2,1)}, u32[]{:S(2)}) %copy-start) | copy-done | bytes 11796504
  44.5 6.7 %shard_map.74 = (bf16[2,128,384]{2,1,0:T(8,128)(2,1)S(1)}, bf16[2,128,384]{2,1,0:T(8,128)(2,1)S(1)}, bf16[2,128,384]{2,1,0:T(8,128)(2,1)S(1)}) custom-call(bf16[2,32,5120]{2,1,0:T(8,128)(2,1)S(1)} %copy-done.3, bf16[2,32,5120]{2,1,0:T(8,128)(2,1)S(1)} %collective-permute-done.refs_1_, bf16[2,32,5120]{2,1,0:T(8,128)(2,1)S(1)} %collective-permute-done.1.refs_2_, ...), custom_call_target="tpu_custom_call" | custom-call | flops 3019898880 | bytes 14417920 | tf_op jit(solution)/shard_map/pallas_call | solution.py:142
  52.4 6.7 %shard_map.75 = (bf16[2,128,384]{2,1,0:T(8,128)(2,1)S(1)}, bf16[2,128,384]{2,1,0:T(8,128)(2,1)S(1)}, bf16[2,128,384]{2,1,0:T(8,128)(2,1)S(1)}) custom-call(bf16[2,32,5120]{2,1,0:T(8,128)(2,1)S(1)} %collective-permute-done.3.refs_0_, bf16[2,32,5120]{2,1,0:T(8,128)(2,1)S(1)} %collective-permute-done.4.refs_1_, ...), custom_call_target="tpu_custom_call" | custom-call | flops 3019898880 | bytes 14417920 | tf_op jit(solution)/shard_map/pallas_call | solution.py:142
  59.3 3.7 %collective-permute-start.15 = (bf16[2,272,384]{2,1,0:T(8,128)(2,1)S(1)}, bf16[2,272,384]{2,1,0:T(8,128)(2,1)S(1)}, u32[]{:S(2)}, u32[]{:S(2)}) collective-permute-start(bf16[2,272,384]{2,1,0:T(8,128)(2,1)S(1)} %broadcast_dynamic-update-slice_fusion), channel_id=1, source_target_pairs={{0,64},{8,72},{16,80},{24,88},{32,96},{40,104},{48,112},{56,120},{... | collective-permute-start | bytes 1253384 | tf_op jit(solution)/shard_map/ppermute | solution.py:37
  64.3 7.6 %shard_map.76 = (f32[1,256,384]{2,1,0:T(8,128)S(1)}, bf16[1,256,128]{2,1,0:T(8,128)(2,1)S(1)}) custom-call(bf16[1,272,384]{2,1,0:T(8,128)(2,1)S(1)} %get-tuple-element.94.q_ref, f32[2,2048]{1,0:T(2,128)S(1)} %add_convert_fusion.3.frame_ref, bf16[1,256,384]{2,1,0:T(8,128)(2,1)S(1)} %get-tuple-element.101.rest_0_, ...), custom_call_target="tpu_custom_call" | custom-call | flops 3221225472 | bytes 6291456 | tf_op jit(solution)/shard_map/pallas_call | solution.py:240
  73.0 7.6 %shard_map.77 = bf16[1,256,512]{2,1,0:T(8,128)(2,1)S(1)} custom-call(bf16[1,272,384]{2,1,0:T(8,128)(2,1)S(1)} %get-tuple-element.95.q_ref, f32[2,2048]{1,0:T(2,128)S(1)} %add_convert_fusion.3.frame_ref, bf16[2,512,384]{2,1,0:T(8,128)(2,1)S(1)} %copy-done.4, bf16[2,512,384]{2,1,0:T(8,128)(2,1)} %collective-permute-done.8.rest_3_.rest_1_, ...), custom_call_target="tpu_custom_call" | custom-call | flops 3221225472 | bytes 6291456 | tf_op jit(solution)/shard_map/pallas_call | solution.py:240
  80.7 3.3 %collective-permute-start.16 = (bf16[1,256,512]{2,1,0:T(8,128)(2,1)S(1)}, bf16[1,256,512]{2,1,0:T(8,128)(2,1)S(1)}, u32[]{:S(2)}, u32[]{:S(2)}) collective-permute-start(bf16[1,256,512]{2,1,0:T(8,128)(2,1)S(1)} %shard_map.77), channel_id=1, source_target_pairs={{0,64},{8,72},{16,80},{24,88},{32,96},{40,104},{48,112},{56,120},{... | collective-permute-start | bytes 786440 | tf_op jit(solution)/shard_map/ppermute | solution.py:37
  84.0 7.6 %shard_map.78 = bf16[1,256,512]{2,1,0:T(8,128)(2,1)S(1)} custom-call(bf16[1,272,384]{2,1,0:T(8,128)(2,1)S(1)} %get-tuple-element.67.q_ref, f32[2,2048]{1,0:T(2,128)S(1)} %add_convert_fusion.3.frame_ref, bf16[2,512,384]{2,1,0:T(8,128)(2,1)S(1)} %copy-done.4, bf16[2,512,384]{2,1,0:T(8,128)(2,1)} %collective-permute-done.8.rest_3_.rest_1_, ...), custom_call_target="tpu_custom_call" | custom-call | flops 3221225472 | bytes 6291456 | tf_op jit(solution)/shard_map/pallas_call | solution.py:240
  93.0 7.8 %shard_map.80 = (f32[1,256,384]{2,1,0:T(8,128)S(1)}, bf16[1,256,128]{2,1,0:T(8,128)(2,1)S(1)}) custom-call(bf16[1,272,384]{2,1,0:T(8,128)(2,1)S(1)} %get-tuple-element.73.q_ref, f32[2,2048]{1,0:T(2,128)S(1)} %add_convert_fusion.3.frame_ref, bf16[1,256,384]{2,1,0:T(8,128)(2,1)S(1)} %get-tuple-element.102.rest_0_, ...), custom_call_target="tpu_custom_call" | custom-call | flops 3221225472 | bytes 6291456 | tf_op jit(solution)/shard_map/pallas_call | solution.py:240
  101.5 3.7 %collective-permute-done.17.rest_1_ = bf16[96,5120]{1,0:T(8,128)(2,1)S(1)} collective-permute-done((bf16[96,5120]{1,0:T(8,128)(2,1)S(1)}, bf16[96,5120]{1,0:T(8,128)(2,1)S(1)}, u32[]{:S(2)}, u32[]{:S(2)}) %collective-permute-start.17) | collective-permute-done | bytes 983072 | tf_op jit(solution)/shard_map/ppermute | solution.py:59
  106.4 1.3 collective-permute-done.21.rest_3_
  107.7 4.1 %shard_map.82 = (bf16[1,32,5120]{2,1,0:T(8,128)(2,1)S(1)}, bf16[1,32,5120]{2,1,0:T(8,128)(2,1)S(1)}, bf16[1,32,5120]{2,1,0:T(8,128)(2,1)S(1)}, bf16[1,32,5120]{2,1,0:T(8,128)(2,1)S(1)}) custom-call(s32[1]{0:T(128)} %bitcast.1.core, bf16[1,128,384]{2,1,0:T(8,128)(2,1)S(1)} %get-tuple-element.79.a_ref, bf16[1,128,384]{2,1,0:T(8,128)(2,1)S(1)} %collective-permute-done.19.b_ref, ...), custom_call_target="tpu_custom_call" | custom-call | flops 1006632960 | bytes 9175040 | tf_op jit(solution)/shard_map/pallas_call | solution.py:322
  111.8 4.1 %shard_map.83 = (bf16[1,32,5120]{2,1,0:T(8,128)(2,1)S(1)}, bf16[1,32,5120]{2,1,0:T(8,128)(2,1)S(1)}, bf16[1,32,5120]{2,1,0:T(8,128)(2,1)S(1)}, bf16[1,32,5120]{2,1,0:T(8,128)(2,1)S(1)}) custom-call(s32[1]{0:T(128)} %bitcast.1.core, bf16[1,128,384]{2,1,0:T(8,128)(2,1)S(1)} %get-tuple-element.84.a_ref, bf16[1,128,384]{2,1,0:T(8,128)(2,1)S(1)} %collective-permute-done.22.b_ref, ...), custom_call_target="tpu_custom_call" | custom-call | flops 1006632960 | bytes 9175040 | tf_op jit(solution)/shard_map/pallas_call | solution.py:322
  116.0 2.2 %collective-permute-start.25 = (bf16[1,32,5120]{2,1,0:T(8,128)(2,1)S(1)}, bf16[1,32,5120]{2,1,0:T(8,128)(2,1)S(1)}, u32[]{:S(2)}, u32[]{:S(2)}) collective-permute-start(bf16[1,32,5120]{2,1,0:T(8,128)(2,1)S(1)} %get-tuple-element.90), channel_id=1, source_target_pairs={{0,3},{1,0},{2,1},{3,2},{4,7},{5,4},{6,5},{7,6},{8,9},{9,10},{10,1... | collective-permute-start | bytes 983048 | tf_op jit(solution)/shard_map/ppermute | solution.py:51
  118.3 3.2 %collective-permute-start.28 = (bf16[1,32,5120]{2,1,0:T(8,128)(2,1)S(1)}, bf16[1,32,5120]{2,1,0:T(8,128)(2,1)S(1)}, u32[]{:S(2)}, u32[]{:S(2)}) collective-permute-start(bf16[1,32,5120]{2,1,0:T(8,128)(2,1)S(1)} %get-tuple-element.92), channel_id=1, source_target_pairs={{0,1},{1,2},{2,3},{3,0},{4,5},{5,6},{6,7},{7,4},{8,11},{9,8},{10,9... | collective-permute-start | bytes 983048 | tf_op jit(solution)/shard_map/ppermute | solution.py:51
  121.4 5.5 %collective-permute-done.25 = bf16[1,32,5120]{2,1,0:T(8,128)(2,1)S(1)} collective-permute-done((bf16[1,32,5120]{2,1,0:T(8,128)(2,1)S(1)}, bf16[1,32,5120]{2,1,0:T(8,128)(2,1)S(1)}, u32[]{:S(2)}, u32[]{:S(2)}) %collective-permute-start.25) | collective-permute-done | bytes 327712 | tf_op jit(solution)/shard_map/ppermute | solution.py:51
  127.0 1.8 %collective-permute-start.26 = (bf16[1,32,5120]{2,1,0:T(8,128)(2,1)S(1)}, bf16[1,32,5120]{2,1,0:T(8,128)(2,1)S(1)}, u32[]{:S(2)}, u32[]{:S(2)}) collective-permute-start(bf16[1,32,5120]{2,1,0:T(8,128)(2,1)S(1)} %add_convert_fusion.1), channel_id=1, source_target_pairs={{0,3},{1,0},{2,1},{3,2},{4,7},{5,4},{6,5},{7,6},{8,9},{9,10},{10,1... | collective-permute-start | bytes 983048 | tf_op jit(solution)/shard_map/ppermute | solution.py:51
  128.9 5.1 %collective-permute-done.23 = bf16[1,32,5120]{2,1,0:T(8,128)(2,1)S(1)} collective-permute-done((bf16[1,32,5120]{2,1,0:T(8,128)(2,1)S(1)}, bf16[1,32,5120]{2,1,0:T(8,128)(2,1)S(1)}, u32[]{:S(2)}, u32[]{:S(2)}) %collective-permute-start.23) | collective-permute-done | bytes 327712 | tf_op jit(solution)/shard_map/ppermute | solution.py:51
  134.1 1.2 collective-permute-start.24
  135.3 1.3 collective-permute-done.27
  136.6 1.8 %collective-permute-done.26 = bf16[1,32,5120]{2,1,0:T(8,128)(2,1)S(1)} collective-permute-done((bf16[1,32,5120]{2,1,0:T(8,128)(2,1)S(1)}, bf16[1,32,5120]{2,1,0:T(8,128)(2,1)S(1)}, u32[]{:S(2)}, u32[]{:S(2)}) %collective-permute-start.26) | collective-permute-done | bytes 327712 | tf_op jit(solution)/shard_map/ppermute | solution.py:51
  138.4 4.0 %collective-permute-done.24 = bf16[1,32,5120]{2,1,0:T(8,128)(2,1)S(1)} collective-permute-done((bf16[1,32,5120]{2,1,0:T(8,128)(2,1)S(1)}, bf16[1,32,5120]{2,1,0:T(8,128)(2,1)S(1)}, u32[]{:S(2)}, u32[]{:S(2)}) %collective-permute-start.24) | collective-permute-done | bytes 327712 | tf_op jit(solution)/shard_map/ppermute | solution.py:51
  142.4 1.2 add_convert_fusion
  (87 shorter events, 12.1 us)
Async XLA Ops:
  0.0 39.0 %copy-start.8 = (s32[2]{0:T(128)S(1)}, s32[2]{0:T(128)}, u32[]{:S(2)}) copy-start(s32[2]{0:T(128)} %param.9) | copy-start | bytes 28
  4.6 17.2 %collective-permute-start = (bf16[2,32,5120]{2,1,0:T(8,128)(2,1)}, bf16[2,32,5120]{2,1,0:T(8,128)(2,1)S(1)}, u32[]{:S(2)}, u32[]{:S(2)}) collective-permute-start(bf16[2,32,5120]{2,1,0:T(8,128)(2,1)} %get-tuple-element.50.refs_0_), channel_id=1, source_target_pairs={{0,1},{1,2},{2,3},{3,0},{4,5},{5,6},{6,7},{7,4},{8,11},{9,8},{10,9... | collective-permute-start | bytes 1966088 | tf_op jit(solution)/shard_map/ppermute | solution.py:51
  4.9 17.7 %collective-permute-start.1 = (bf16[2,32,5120]{2,1,0:T(8,128)(2,1)}, bf16[2,32,5120]{2,1,0:T(8,128)(2,1)S(1)}, u32[]{:S(2)}, u32[]{:S(2)}) collective-permute-start(bf16[2,32,5120]{2,1,0:T(8,128)(2,1)} %get-tuple-element.50.refs_0_), channel_id=1, source_target_pairs={{0,3},{1,0},{2,1},{3,2},{4,7},{5,4},{6,5},{7,6},{8,9},{9,10},{10,1... | collective-permute-start | bytes 1966088 | tf_op jit(solution)/shard_map/ppermute | solution.py:51
  6.7 21.6 %collective-permute-start.8 = (bf16[2,512,384]{2,1,0:T(8,128)(2,1)S(1)}, bf16[2,512,384]{2,1,0:T(8,128)(2,1)}, u32[]{:S(2)}, u32[]{:S(2)}) collective-permute-start(bf16[2,512,384]{2,1,0:T(8,128)(2,1)S(1)} %copy-done.4), channel_id=1, source_target_pairs={{0,16},{1,17},{2,18},{3,19},{4,20},{5,21},{6,22},{7,23},{8,56},{9,... | collective-permute-start | bytes 2359304 | tf_op jit(solution)/shard_map/ppermute | solution.py:51
  7.9 20.8 %collective-permute-start.9 = (bf16[2,512,384]{2,1,0:T(8,128)(2,1)S(1)}, bf16[2,512,384]{2,1,0:T(8,128)(2,1)}, u32[]{:S(2)}, u32[]{:S(2)}) collective-permute-start(bf16[2,512,384]{2,1,0:T(8,128)(2,1)S(1)} %copy-done.4), channel_id=1, source_target_pairs={{0,48},{1,49},{2,50},{3,51},{4,52},{5,53},{6,54},{7,55},{8,24},{9,... | collective-permute-start | bytes 2359304 | tf_op jit(solution)/shard_map/ppermute | solution.py:51
  8.8 17.9 %collective-permute-start.2 = (bf16[2,32,5120]{2,1,0:T(8,128)(2,1)}, bf16[2,32,5120]{2,1,0:T(8,128)(2,1)S(1)}, u32[]{:S(2)}, u32[]{:S(2)}) collective-permute-start(bf16[2,32,5120]{2,1,0:T(8,128)(2,1)} %get-tuple-element.50.refs_0_), channel_id=1, source_target_pairs={{0,4},{1,5},{2,6},{3,7},{4,0},{5,1},{6,2},{7,3},{8,12},{9,13},{10,... | collective-permute-start | bytes 1966088 | tf_op jit(solution)/shard_map/ppermute | solution.py:27
  21.9 14.6 %collective-permute-start.3 = (bf16[2,32,5120]{2,1,0:T(8,128)(2,1)S(1)}, bf16[2,32,5120]{2,1,0:T(8,128)(2,1)S(1)}, u32[]{:S(2)}, u32[]{:S(2)}) collective-permute-start(bf16[2,32,5120]{2,1,0:T(8,128)(2,1)S(1)} %collective-permute-done.refs_1_), channel_id=1, source_target_pairs={{0,1},{1,2},{2,3},{3,0},{4,5},{5,6},{6,7},{7,4},{8,11},{9,8},{10,9... | collective-permute-start | bytes 1966088 | tf_op jit(solution)/shard_map/ppermute | solution.py:51
  22.6 28.8 %collective-permute-start.7 = (bf16[96,5120]{1,0:T(8,128)(2,1)}, bf16[96,5120]{1,0:T(8,128)(2,1)S(1)}, u32[]{:S(2)}, u32[]{:S(2)}) collective-permute-start(bf16[96,5120]{1,0:T(8,128)(2,1)} %get-tuple-element.52), channel_id=1, source_target_pairs={{0,68},{1,69},{2,70},{3,71},{4,64},{5,65},{6,66},{7,67},{8,76},{9,... | collective-permute-start | bytes 2949128 | tf_op jit(solution)/shard_map/ppermute | solution.py:59
  26.7 25.3 %collective-permute-start.4 = (bf16[2,32,5120]{2,1,0:T(8,128)(2,1)S(1)}, bf16[2,32,5120]{2,1,0:T(8,128)(2,1)S(1)}, u32[]{:S(2)}, u32[]{:S(2)}) collective-permute-start(bf16[2,32,5120]{2,1,0:T(8,128)(2,1)S(1)} %collective-permute-done.2.refs_3_), channel_id=1, source_target_pairs={{0,1},{1,2},{2,3},{3,0},{4,5},{5,6},{6,7},{7,4},{8,11},{9,8},{10,9... | collective-permute-start | bytes 1966088 | tf_op jit(solution)/shard_map/ppermute | solution.py:51
  28.3 24.1 %collective-permute-start.5 = (bf16[2,32,5120]{2,1,0:T(8,128)(2,1)S(1)}, bf16[2,32,5120]{2,1,0:T(8,128)(2,1)S(1)}, u32[]{:S(2)}, u32[]{:S(2)}) collective-permute-start(bf16[2,32,5120]{2,1,0:T(8,128)(2,1)S(1)} %collective-permute-done.2.refs_3_), channel_id=1, source_target_pairs={{0,3},{1,0},{2,1},{3,2},{4,7},{5,4},{6,5},{7,6},{8,9},{9,10},{10,1... | collective-permute-start | bytes 1966088 | tf_op jit(solution)/shard_map/ppermute | solution.py:51
  28.8 22.5 %collective-permute-start.10 = (bf16[2,512,384]{2,1,0:T(8,128)(2,1)}, bf16[2,512,384]{2,1,0:T(8,128)(2,1)S(1)}, u32[]{:S(2)}, u32[]{:S(2)}) collective-permute-start(bf16[2,512,384]{2,1,0:T(8,128)(2,1)} %collective-permute-done.8.rest_3_.rest_1_), channel_id=1, source_target_pairs={{0,16},{1,17},{2,18},{3,19},{4,20},{5,21},{6,22},{7,23},{8,56},{9,... | collective-permute-start | bytes 2359304 | tf_op jit(solution)/shard_map/ppermute | solution.py:51
  36.4 15.4 %collective-permute-start.6 = (bf16[2,32,5120]{2,1,0:T(8,128)(2,1)S(1)}, bf16[2,32,5120]{2,1,0:T(8,128)(2,1)S(1)}, u32[]{:S(2)}, u32[]{:S(2)}) collective-permute-start(bf16[2,32,5120]{2,1,0:T(8,128)(2,1)S(1)} %collective-permute-done.3.refs_0_), channel_id=1, source_target_pairs={{0,4},{1,5},{2,6},{3,7},{4,0},{5,1},{6,2},{7,3},{8,12},{9,13},{10,... | collective-permute-start | bytes 1966088 | tf_op jit(solution)/shard_map/ppermute | solution.py:27
  51.3 11.9 %collective-permute-start.11 = (bf16[2,512,384]{2,1,0:T(8,128)(2,1)S(1)}, bf16[2,512,384]{2,1,0:T(8,128)(2,1)S(1)}, u32[]{:S(2)}, u32[]{:S(2)}) collective-permute-start(bf16[2,512,384]{2,1,0:T(8,128)(2,1)S(1)} %copy-done.4), channel_id=1, source_target_pairs={{0,8},{8,0},{16,24},{24,16},{32,40},{40,32},{48,56},{56,48},{64,72... | collective-permute-start | bytes 2359304 | tf_op jit(solution)/shard_map/ppermute | solution.py:37
  51.4 12.9 %collective-permute-start.12 = (bf16[2,512,384]{2,1,0:T(8,128)(2,1)}, bf16[2,512,384]{2,1,0:T(8,128)(2,1)S(1)}, u32[]{:S(2)}, u32[]{:S(2)}) collective-permute-start(bf16[2,512,384]{2,1,0:T(8,128)(2,1)} %collective-permute-done.8.rest_3_.rest_1_), channel_id=1, source_target_pairs={{0,8},{8,0},{16,24},{24,16},{32,40},{40,32},{48,56},{56,48},{64,72... | collective-permute-start | bytes 2359304 | tf_op jit(solution)/shard_map/ppermute | solution.py:37
  51.9 12.4 %collective-permute-start.13 = (bf16[2,512,384]{2,1,0:T(8,128)(2,1)}, bf16[2,512,384]{2,1,0:T(8,128)(2,1)S(1)}, u32[]{:S(2)}, u32[]{:S(2)}) collective-permute-start(bf16[2,512,384]{2,1,0:T(8,128)(2,1)} %collective-permute-done.9.rest_4_.rest_2_), channel_id=1, source_target_pairs={{0,8},{8,0},{16,24},{24,16},{32,40},{40,32},{48,56},{56,48},{64,72... | collective-permute-start | bytes 2359304 | tf_op jit(solution)/shard_map/ppermute | solution.py:37
  52.0 12.3 %collective-permute-start.14 = (bf16[2,512,384]{2,1,0:T(8,128)(2,1)S(1)}, bf16[2,512,384]{2,1,0:T(8,128)(2,1)S(1)}, u32[]{:S(2)}, u32[]{:S(2)}) collective-permute-start(bf16[2,512,384]{2,1,0:T(8,128)(2,1)S(1)} %collective-permute-done.10.rest_5_.rest_3_), channel_id=1, source_target_pairs={{0,8},{8,0},{16,24},{24,16},{32,40},{40,32},{48,56},{56,48},{64,72... | collective-permute-start | bytes 2359304 | tf_op jit(solution)/shard_map/ppermute | solution.py:37
  59.3 13.7 %collective-permute-start.15 = (bf16[2,272,384]{2,1,0:T(8,128)(2,1)S(1)}, bf16[2,272,384]{2,1,0:T(8,128)(2,1)S(1)}, u32[]{:S(2)}, u32[]{:S(2)}) collective-permute-start(bf16[2,272,384]{2,1,0:T(8,128)(2,1)S(1)} %broadcast_dynamic-update-slice_fusion), channel_id=1, source_target_pairs={{0,64},{8,72},{16,80},{24,88},{32,96},{40,104},{48,112},{56,120},{... | collective-permute-start | bytes 1253384 | tf_op jit(solution)/shard_map/ppermute | solution.py:37
  64.3 40.9 %collective-permute-start.17 = (bf16[96,5120]{1,0:T(8,128)(2,1)S(1)}, bf16[96,5120]{1,0:T(8,128)(2,1)S(1)}, u32[]{:S(2)}, u32[]{:S(2)}) collective-permute-start(bf16[96,5120]{1,0:T(8,128)(2,1)S(1)} %copy-done.7), channel_id=1, source_target_pairs={{0,68},{1,69},{2,70},{3,71},{4,64},{5,65},{6,66},{7,67},{8,76},{9,... | collective-permute-start | bytes 2949128 | tf_op jit(solution)/shard_map/ppermute | solution.py:59
  64.3 42.2 %collective-permute-start.20 = (bf16[96,5120]{1,0:T(8,128)(2,1)S(1)}, bf16[96,5120]{1,0:T(8,128)(2,1)S(1)}, u32[]{:S(2)}, u32[]{:S(2)}) collective-permute-start(bf16[96,5120]{1,0:T(8,128)(2,1)S(1)} %collective-permute-done.7.rest_0_), channel_id=1, source_target_pairs={{0,8},{8,0},{16,24},{24,16},{32,40},{40,32},{48,56},{56,48},{64,72... | collective-permute-start | bytes 2949128 | tf_op jit(solution)/shard_map/ppermute | solution.py:37
  80.7 11.3 %collective-permute-start.16 = (bf16[1,256,512]{2,1,0:T(8,128)(2,1)S(1)}, bf16[1,256,512]{2,1,0:T(8,128)(2,1)S(1)}, u32[]{:S(2)}, u32[]{:S(2)}) collective-permute-start(bf16[1,256,512]{2,1,0:T(8,128)(2,1)S(1)} %shard_map.77), channel_id=1, source_target_pairs={{0,64},{8,72},{16,80},{24,88},{32,96},{40,104},{48,112},{56,120},{... | collective-permute-start | bytes 786440 | tf_op jit(solution)/shard_map/ppermute | solution.py:37
  91.6 9.9 %collective-permute-start.18 = (bf16[1,256,512]{2,1,0:T(8,128)(2,1)S(1)}, bf16[1,256,512]{2,1,0:T(8,128)(2,1)S(1)}, u32[]{:S(2)}, u32[]{:S(2)}) collective-permute-start(bf16[1,256,512]{2,1,0:T(8,128)(2,1)S(1)} %shard_map.78), channel_id=1, source_target_pairs={{0,64},{8,72},{16,80},{24,88},{32,96},{40,104},{48,112},{56,120},{... | collective-permute-start | bytes 786440 | tf_op jit(solution)/shard_map/ppermute | solution.py:37
  92.6 8.9 %collective-permute-start.19 = (bf16[1,128,384]{2,1,0:T(8,128)(2,1)S(1)}, bf16[1,128,384]{2,1,0:T(8,128)(2,1)S(1)}, u32[]{:S(2)}, u32[]{:S(2)}) collective-permute-start(bf16[1,128,384]{2,1,0:T(8,128)(2,1)S(1)} %get-tuple-element.72), channel_id=1, source_target_pairs={{0,4},{1,5},{2,6},{3,7},{4,0},{5,1},{6,2},{7,3},{8,12},{9,13},{10,... | collective-permute-start | bytes 294920 | tf_op jit(solution)/shard_map/ppermute | solution.py:27
  105.2 2.6 %collective-permute-start.21 = (bf16[96,5120]{1,0:T(8,128)(2,1)S(1)}, bf16[96,5120]{1,0:T(8,128)(2,1)S(1)}, u32[]{:S(2)}, u32[]{:S(2)}) collective-permute-start(bf16[96,5120]{1,0:T(8,128)(2,1)S(1)} %collective-permute-done.17.rest_1_), channel_id=1, source_target_pairs={{0,8},{8,0},{16,24},{24,16},{32,40},{40,32},{48,56},{56,48},{64,72... | collective-permute-start | bytes 2949128 | tf_op jit(solution)/shard_map/ppermute | solution.py:37
  105.8 6.0 %collective-permute-start.22 = (bf16[1,128,384]{2,1,0:T(8,128)(2,1)S(1)}, bf16[1,128,384]{2,1,0:T(8,128)(2,1)S(1)}, u32[]{:S(2)}, u32[]{:S(2)}) collective-permute-start(bf16[1,128,384]{2,1,0:T(8,128)(2,1)S(1)} %get-tuple-element.78), channel_id=1, source_target_pairs={{0,4},{1,5},{2,6},{3,7},{4,0},{5,1},{6,2},{7,3},{8,12},{9,13},{10,... | collective-permute-start | bytes 294920 | tf_op jit(solution)/shard_map/ppermute | solution.py:27
  115.9 19.3 %copy-start.6 = (f32[2,1,5120]{2,1,0:T(1,128)S(1)}, f32[2,1,5120]{2,1,0:T(1,128)}, u32[]{:S(2)}) copy-start(f32[2,1,5120]{2,1,0:T(1,128)} %get-tuple-element.49) | copy-start | bytes 122884
  116.0 26.5 %copy-start.5 = (bf16[2,32,5120]{2,1,0:T(8,128)(2,1)S(1)}, bf16[2,32,5120]{2,1,0:T(8,128)(2,1)}, u32[]{:S(2)}) copy-start(bf16[2,32,5120]{2,1,0:T(8,128)(2,1)} %x_hbm.1) | copy-start | bytes 1966084
  116.0 11.0 %collective-permute-start.25 = (bf16[1,32,5120]{2,1,0:T(8,128)(2,1)S(1)}, bf16[1,32,5120]{2,1,0:T(8,128)(2,1)S(1)}, u32[]{:S(2)}, u32[]{:S(2)}) collective-permute-start(bf16[1,32,5120]{2,1,0:T(8,128)(2,1)S(1)} %get-tuple-element.90), channel_id=1, source_target_pairs={{0,3},{1,0},{2,1},{3,2},{4,7},{5,4},{6,5},{7,6},{8,9},{9,10},{10,1... | collective-permute-start | bytes 983048 | tf_op jit(solution)/shard_map/ppermute | solution.py:51
  118.2 15.8 %collective-permute-start.23 = (bf16[1,32,5120]{2,1,0:T(8,128)(2,1)S(1)}, bf16[1,32,5120]{2,1,0:T(8,128)(2,1)S(1)}, u32[]{:S(2)}, u32[]{:S(2)}) collective-permute-start(bf16[1,32,5120]{2,1,0:T(8,128)(2,1)S(1)} %get-tuple-element.88), channel_id=1, source_target_pairs={{0,3},{1,0},{2,1},{3,2},{4,7},{5,4},{6,5},{7,6},{8,9},{9,10},{10,1... | collective-permute-start | bytes 983048 | tf_op jit(solution)/shard_map/ppermute | solution.py:51
  118.3 17.1 %collective-permute-start.28 = (bf16[1,32,5120]{2,1,0:T(8,128)(2,1)S(1)}, bf16[1,32,5120]{2,1,0:T(8,128)(2,1)S(1)}, u32[]{:S(2)}, u32[]{:S(2)}) collective-permute-start(bf16[1,32,5120]{2,1,0:T(8,128)(2,1)S(1)} %get-tuple-element.92), channel_id=1, source_target_pairs={{0,1},{1,2},{2,3},{3,0},{4,5},{5,6},{6,7},{7,4},{8,11},{9,8},{10,9... | collective-permute-start | bytes 983048 | tf_op jit(solution)/shard_map/ppermute | solution.py:51
  121.4 15.2 %collective-permute-start.27 = (bf16[1,32,5120]{2,1,0:T(8,128)(2,1)S(1)}, bf16[1,32,5120]{2,1,0:T(8,128)(2,1)S(1)}, u32[]{:S(2)}, u32[]{:S(2)}) collective-permute-start(bf16[1,32,5120]{2,1,0:T(8,128)(2,1)S(1)} %get-tuple-element.91), channel_id=1, source_target_pairs={{0,1},{1,2},{2,3},{3,0},{4,5},{5,6},{6,7},{7,4},{8,11},{9,8},{10,9... | collective-permute-start | bytes 983048 | tf_op jit(solution)/shard_map/ppermute | solution.py:51
  127.0 11.3 %collective-permute-start.26 = (bf16[1,32,5120]{2,1,0:T(8,128)(2,1)S(1)}, bf16[1,32,5120]{2,1,0:T(8,128)(2,1)S(1)}, u32[]{:S(2)}, u32[]{:S(2)}) collective-permute-start(bf16[1,32,5120]{2,1,0:T(8,128)(2,1)S(1)} %add_convert_fusion.1), channel_id=1, source_target_pairs={{0,3},{1,0},{2,1},{3,2},{4,7},{5,4},{6,5},{7,6},{8,9},{9,10},{10,1... | collective-permute-start | bytes 983048 | tf_op jit(solution)/shard_map/ppermute | solution.py:51
  134.1 8.4 %collective-permute-start.24 = (bf16[1,32,5120]{2,1,0:T(8,128)(2,1)S(1)}, bf16[1,32,5120]{2,1,0:T(8,128)(2,1)S(1)}, u32[]{:S(2)}, u32[]{:S(2)}) collective-permute-start(bf16[1,32,5120]{2,1,0:T(8,128)(2,1)S(1)} %add_convert_fusion.2), channel_id=1, source_target_pairs={{0,3},{1,0},{2,1},{3,2},{4,7},{5,4},{6,5},{7,6},{8,9},{9,10},{10,1... | collective-permute-start | bytes 983048 | tf_op jit(solution)/shard_map/ppermute | solution.py:51
  (6 other events, 36.1 us)

commit v5 on v4

--- a/solution.py
+++ b/solution.py
@@ -60,16 +60,19 @@
 
 
 def norm_kernel(
-    actions, x_hbm, table_hbm, w_hbm, hidden_ref, gate_ref, w_0, w_1, x_ref, table_ref, sems
+    actions, x_hbm, table_hbm, w_hbm, hidden_ref, gate_ref, w_0, w_1, w_2, x_ref, table_ref, sems
 ):
-    count = w_0.shape[0]
-    at = lax.rem(lax.axis_index("branch"), 2) * 2 * count
-    quarters = [pl.ds(pl.multiple_of(at + j * count, 16), count) for j in range(2)]
+    at = lax.rem(lax.axis_index("branch"), 2) * (w_hbm.shape[0] // 2)
+    cuts = []
+    for ref in (w_0, w_1, w_2):
+        cuts.append(pl.ds(pl.multiple_of(at, 16), ref.shape[0]))
+        at = at + ref.shape[0]
     copies = [
         pltpu.make_async_copy(x_hbm, x_ref, sems.at[0]),
         pltpu.make_async_copy(table_hbm, table_ref, sems.at[1]),
-        pltpu.make_async_copy(w_hbm.at[quarters[0]], w_0, sems.at[2]),
-        pltpu.make_async_copy(w_hbm.at[quarters[1]], w_1, sems.at[3]),
+        pltpu.make_async_copy(w_hbm.at[cuts[0]], w_0, sems.at[2]),
+        pltpu.make_async_copy(w_hbm.at[cuts[1]], w_1, sems.at[3]),
+        pltpu.make_async_copy(w_hbm.at[cuts[2]], w_2, sems.at[4]),
     ]
     for copy in copies:
         copy.start()
@@ -92,24 +95,27 @@
         hidden_ref[b] = (normed * (1.0 + scale) + shift).astype(jnp.bfloat16)
     copies[2].wait()
     copies[3].wait()
+    copies[4].wait()
 
 
 def norm(actions, x, table, w_out):
-    quarter = jax.ShapeDtypeStruct((w_out.shape[0] // 4, w_out.shape[1]), w_out.dtype)
+    rows, width = w_out.shape
+    cuts = [
+        jax.ShapeDtypeStruct((rows // part, width), w_out.dtype) for part in (4, 8, 8)
+    ]
     return pl.pallas_call(
         norm_kernel,
         out_shape=(
             jax.ShapeDtypeStruct(x.shape, jnp.bfloat16),
             jax.ShapeDtypeStruct((x.shape[0], 1, x.shape[2]), jnp.float32),
-            quarter,
-            quarter,
+            *cuts,
         ),
         in_specs=[SMEM, ANY, ANY, ANY],
-        out_specs=(VMEM,) * 4,
+        out_specs=(VMEM,) * 5,
         scratch_shapes=[
             pltpu.VMEM(x.shape, x.dtype),
             pltpu.VMEM(table.shape, table.dtype),
-            pltpu.SemaphoreType.DMA((4,)),
+            pltpu.SemaphoreType.DMA((5,)),
         ],
         compiler_params=pltpu.CompilerParams(vmem_limit_bytes=56 << 20),
     )(actions, x, table, w_out)
@@ -136,7 +142,7 @@
 
 
 def project_qkv(shards, w):
-    count, depth, block = len(shards), w.shape[1], 1024
+    count, depth, block = len(shards), w.shape[1], 2560
     rows = count * 32
     out = jax.ShapeDtypeStruct((2, rows, WIDTH), jnp.bfloat16)
     return pl.pallas_call(
@@ -299,13 +305,14 @@
 
 
 def out_kernel(core, a_ref, b_ref, wa_ref, *rest):
-    pieces, outs, w = rest[:4], rest[4:-1], rest[-1]
-    count, depth = pieces[0].shape[0], wa_ref.shape[0]
+    pieces, outs, w = rest[:6], rest[6:-1], rest[-1]
+    depth = wa_ref.shape[0]
     w[:depth] = wa_ref[...]
-    for j, ref in enumerate(pieces):
-        side = core[0] if j < 2 else 1 - core[0]
-        at = depth + (side * 2 + j % 2) * count
-        w[pl.ds(pl.multiple_of(at, 16), count)] = ref[...]
+    for side, refs in ((core[0], pieces[:3]), (1 - core[0], pieces[3:])):
+        at = depth + side * (depth // 2)
+        for ref in refs:
+            w[pl.ds(pl.multiple_of(at, 16), ref.shape[0])] = ref[...]
+            at = at + ref.shape[0]
     rows, branches = a_ref.shape[1], range(a_ref.shape[0])
     x = jnp.concatenate(
         [jnp.concatenate([ref[b] for b in branches], axis=0) for ref in (a_ref, b_ref)], axis=1
@@ -317,7 +324,7 @@
 
 
 def project_out(core, a, b, wa, pieces):
-    branches, rows, width, block = a.shape[0], a.shape[1], wa.shape[1], 512
+    branches, rows, width, block = a.shape[0], a.shape[1], wa.shape[1], 1280
     count = rows // 32
     return pl.pallas_call(
         out_kernel,
@@ -329,7 +336,7 @@
             pl.BlockSpec((branches, rows, WIDTH), lambda i: (0, 0, 0)),
             pl.BlockSpec((WIDTH, block), lambda i: (0, i)),
         ]
-        + [pl.BlockSpec((WIDTH // 4, block), lambda i: (0, i))] * 4,
+        + [pl.BlockSpec((piece.shape[0], block), lambda i: (0, i)) for piece in pieces],
         out_specs=(pl.BlockSpec((branches, 32, block), lambda i: (0, 0, i)),) * count,
         scratch_shapes=[pltpu.VMEM((2 * WIDTH, block), jnp.bfloat16)],
         compiler_params=pltpu.CompilerParams(vmem_limit_bytes=24 << 20),
@@ -348,7 +355,7 @@
 def shards(x, actions, visible_from, table, w_qkv, w_out, ctx):
     branch = lax.axis_index("branch")
     core, base = branch % 2, branch // 8 * 8
-    hidden, gate, *quarters = norm(actions, x, jnp.transpose(table, (1, 0, 2)), w_out)
+    hidden, gate, *cuts = norm(actions, x, jnp.transpose(table, (1, 0, 2)), w_out)
     w = jnp.transpose(w_qkv, (1, 0, 2))
 
     a0 = hidden
@@ -357,7 +364,7 @@
     b1, b3 = turned(b0, "y", 1), turned(b0, "y", -1)
     b2 = along_seq(a2, 0, 1)
 
-    near = across_z(quarters[0])
+    near = across_z(cuts[0])
     b2, near = lax.optimization_barrier((b2, near))
     far = along_branch(near, 0, 0, 1)
 
@@ -386,8 +393,8 @@
         for f, s, tail in zip(first, second, ([start], [], []))
     )
     far_q = along_branch(q, 0, 1)
-    quarter, _ = lax.optimization_barrier((quarters[1], b2))
-    near_1 = across_z(quarter)
+    cut_1, cut_2, _ = lax.optimization_barrier((cuts[1], cuts[2], b2))
+    near_1, near_2 = across_z(cut_1), along_seq(cut_2, 0, 1)
     o_0, s_0 = attend(q[:1], frames, parts, (k[:1], v[:1]))
     far_q, _ = lax.optimization_barrier((far_q, s_0))
     far_0 = attend(far_q[:1], frames, parts)
@@ -400,8 +407,11 @@
     other_0 = along_seq(there_0, 0, 1)
     last, _ = lax.optimization_barrier((q[1:], there_0))
     o_1, s_1 = attend(last, frames, parts, (k[1:], v[1:]))
-    near_1, packed_1, o_1, other_0 = lax.optimization_barrier((near_1, packed_1, o_1, other_0))
-    pieces = [near, near_1, far, along_branch(near_1, 0, 0, 1)]
+    near_1, near_2, packed_1, o_1, other_0 = lax.optimization_barrier(
+        (near_1, near_2, packed_1, o_1, other_0)
+    )
+    far_1, far_2 = along_branch(near_1, 0, 0, 1), along_branch(near_2, 0, 0, 1)
+    pieces = [near, near_1, near_2, far, far_1, far_2]
     here_1, there_1 = merge([(o_1, s_1)], packed_1)
     other_1 = along_seq(there_1, 0, 1)
 

time: 145 us -> 140 us (0.966)
  Pallas kernels: 58.1 us -> 54.8 us
    ppermute x2, waiting for transfers between devices: 3.67 us -> 0.01 us  [across_z(): return lax.ppermute(a, ('branch', 'seq'), perm)]
    pallas_call x2, Pallas kernels: 8.18 us -> 5.97 us  [project_out(): pl.pallas_call(out_kernel, grid=(width // block,), out_shape=(jax.ShapeDt...]
    ppermute x14, waiting for transfers between devices: 35.4 us -> 36.9 us  [turned(): return lax.ppermute(a, ('branch', 'seq'), perm)]
    ppermute x9 -> x10, waiting for transfers between devices: 3.12 us -> 4.05 us  [along_branch(): return lax.ppermute(a, 'branch', perm)]
    ppermute x9 -> x10, starting transfers between devices: 8.47 us -> 9.27 us  [along_branch(): return lax.ppermute(a, 'branch', perm)]
    ppermute x4 -> x5, starting transfers between devices: 5.39 us -> 5.32 us  [along_seq(): return lax.ppermute(a, 'seq', perm)]
    unnamed x27 -> x29, local copies, waits for them, and re-layouts: 6.68 us -> 6.64 us
  transfers between devices with their start and end apart: 29 -> 31, of which waited for: 12 -> 13; matrix products, arithmetic and copies ran while one was open for 1% -> 1% of each run, Pallas kernels for 34% -> 34%
where the time goes in v5:
time: 140 us; the launch traced here: 139 us
  Pallas kernels  54.8 us (39%)
  waiting for transfers between devices  41.4 us (30%)
  starting transfers between devices  33.8 us (24%)
  local copies, waits for them, and re-layouts  7.17 us (5%)
  other arithmetic  1.5 us (1%)
    ppermute x14, waiting for transfers between devices, turned(): return lax.ppermute(a, ('branch', 'seq'), perm)  36.9 us
    pallas_call x4, Pallas kernels, attend(): pl.pallas_call(functools.partial(attend_kernel, branches, chunk, blocks,...  30.6 us
    ppermute x14, starting transfers between devices, turned(): return lax.ppermute(a, ('branch', 'seq'), perm)  15.2 us
    pallas_call x2, Pallas kernels, project_qkv(): pl.pallas_call(functools.partial(qkv_kernel, count), grid=(depth // block...  12.3 us
    ppermute x10, starting transfers between devices, along_branch(): return lax.ppermute(a, 'branch', perm)  9.27 us
    unnamed x29, local copies, waits for them, and re-layouts  6.64 us
    pallas_call x2, Pallas kernels, project_out(): pl.pallas_call(out_kernel, grid=(width // block,), out_shape=(jax.ShapeDt...  5.97 us
    ppermute x5, starting transfers between devices, along_seq(): return lax.ppermute(a, 'seq', perm)  5.32 us
  transfers between devices with their start and end apart: 31, of which 13 were waited for; matrix products, arithmetic and copies ran while one was open for 1% of the time, Pallas kernels for 34%

profile of v5, /device:TPU:28, one launch (start us, length us, event | category | flops | bytes accessed | tf_op | source)
XLA Modules:
  0.0 139.1 jit_solution(512798634889373358)
XLA Ops:
  0.0 4.6 %shard_map.73 = (bf16[2,32,5120]{2,1,0:T(8,128)(2,1)}, f32[2,1,5120]{2,1,0:T(1,128)}, bf16[96,5120]{1,0:T(8,128)(2,1)}, bf16[48,5120]{1,0:T(8,128)(2,1)}, bf16[48,5120]{1,0:T(8,128)(2,1)}) custom-call(s32[2]{0:T(128)} %actions.1, bf16[2,32,5120]{2,1,0:T(8,128)(2,1)} %x_hbm.1, bf16[3,16,5120]{2,1,0:T(8,128)(2,1)} %bitcast.22, bf16[384,5120]{1,0:T(8,128)(2,1)} %wa_ref.3), custom_call_target="tpu_custom_call" | custom-call | tf_op jit(solution)/shard_map/pallas_call | solution.py:106
  4.9 1.8 %collective-permute-start.1 = (bf16[2,32,5120]{2,1,0:T(8,128)(2,1)}, bf16[2,32,5120]{2,1,0:T(8,128)(2,1)S(1)}, u32[]{:S(2)}, u32[]{:S(2)}) collective-permute-start(bf16[2,32,5120]{2,1,0:T(8,128)(2,1)} %get-tuple-element.53.refs_0_), channel_id=1, source_target_pairs={{0,3},{1,0},{2,1},{3,2},{4,7},{5,4},{6,5},{7,6},{8,9},{9,10},{10,1... | collective-permute-start | bytes 1966088 | tf_op jit(solution)/shard_map/ppermute | solution.py:51
  6.7 1.2 collective-permute-start.8
  8.8 1.9 %collective-permute-start.2 = (bf16[2,32,5120]{2,1,0:T(8,128)(2,1)}, bf16[2,32,5120]{2,1,0:T(8,128)(2,1)S(1)}, u32[]{:S(2)}, u32[]{:S(2)}) collective-permute-start(bf16[2,32,5120]{2,1,0:T(8,128)(2,1)} %get-tuple-element.53.refs_0_), channel_id=1, source_target_pairs={{0,4},{1,5},{2,6},{3,7},{4,0},{5,1},{6,2},{7,3},{8,12},{9,13},{10,... | collective-permute-start | bytes 1966088 | tf_op jit(solution)/shard_map/ppermute | solution.py:27
  10.8 11.1 %collective-permute-done.refs_1_ = bf16[2,32,5120]{2,1,0:T(8,128)(2,1)S(1)} collective-permute-done((bf16[2,32,5120]{2,1,0:T(8,128)(2,1)}, bf16[2,32,5120]{2,1,0:T(8,128)(2,1)S(1)}, u32[]{:S(2)}, u32[]{:S(2)}) %collective-permute-start) | collective-permute-done | bytes 655392 | tf_op jit(solution)/shard_map/ppermute | solution.py:51
  22.6 4.0 %collective-permute-start.7 = (bf16[96,5120]{1,0:T(8,128)(2,1)}, bf16[96,5120]{1,0:T(8,128)(2,1)S(1)}, u32[]{:S(2)}, u32[]{:S(2)}) collective-permute-start(bf16[96,5120]{1,0:T(8,128)(2,1)} %get-tuple-element.55), channel_id=1, source_target_pairs={{0,68},{1,69},{2,70},{3,71},{4,64},{5,65},{6,66},{7,67},{8,76},{9,... | collective-permute-start | bytes 2949128 | tf_op jit(solution)/shard_map/ppermute | solution.py:59
  26.7 1.7 %collective-permute-start.4 = (bf16[2,32,5120]{2,1,0:T(8,128)(2,1)S(1)}, bf16[2,32,5120]{2,1,0:T(8,128)(2,1)S(1)}, u32[]{:S(2)}, u32[]{:S(2)}) collective-permute-start(bf16[2,32,5120]{2,1,0:T(8,128)(2,1)S(1)} %collective-permute-done.2.refs_3_), channel_id=1, source_target_pairs={{0,1},{1,2},{2,3},{3,0},{4,5},{5,6},{6,7},{7,4},{8,11},{9,8},{10,9... | collective-permute-start | bytes 1966088 | tf_op jit(solution)/shard_map/ppermute | solution.py:51
  28.8 1.2 collective-permute-start.10
  30.0 6.5 %collective-permute-done.3.refs_0_ = bf16[2,32,5120]{2,1,0:T(8,128)(2,1)S(1)} collective-permute-done((bf16[2,32,5120]{2,1,0:T(8,128)(2,1)S(1)}, bf16[2,32,5120]{2,1,0:T(8,128)(2,1)S(1)}, u32[]{:S(2)}, u32[]{:S(2)}) %collective-permute-start.3) | collective-permute-done | bytes 655392 | tf_op jit(solution)/shard_map/ppermute | solution.py:51
  36.4 2.6 %collective-permute-start.6 = (bf16[2,32,5120]{2,1,0:T(8,128)(2,1)S(1)}, bf16[2,32,5120]{2,1,0:T(8,128)(2,1)S(1)}, u32[]{:S(2)}, u32[]{:S(2)}) collective-permute-start(bf16[2,32,5120]{2,1,0:T(8,128)(2,1)S(1)} %collective-permute-done.3.refs_0_), channel_id=1, source_target_pairs={{0,4},{1,5},{2,6},{3,7},{4,0},{5,1},{6,2},{7,3},{8,12},{9,13},{10,... | collective-permute-start | bytes 1966088 | tf_op jit(solution)/shard_map/ppermute | solution.py:27
  39.0 4.3 %copy-done = bf16[5120,3,384]{2,0,1:T(8,128)(2,1)S(1)} copy-done((bf16[5120,3,384]{2,0,1:T(8,128)(2,1)S(1)}, bf16[5120,3,384]{2,0,1:T(8,128)(2,1)}, u32[]{:S(2)}) %copy-start) | copy-done | bytes 11796504
  44.5 6.1 %shard_map.74 = (bf16[2,128,384]{2,1,0:T(8,128)(2,1)S(1)}, bf16[2,128,384]{2,1,0:T(8,128)(2,1)S(1)}, bf16[2,128,384]{2,1,0:T(8,128)(2,1)S(1)}) custom-call(bf16[2,32,5120]{2,1,0:T(8,128)(2,1)S(1)} %copy-done.3, bf16[2,32,5120]{2,1,0:T(8,128)(2,1)S(1)} %collective-permute-done.refs_1_, bf16[2,32,5120]{2,1,0:T(8,128)(2,1)S(1)} %collective-permute-done.1.refs_2_, ...), custom_call_target="tpu_custom_call" | custom-call | flops 3019898880 | bytes 14417920 | tf_op jit(solution)/shard_map/pallas_call | solution.py:148
  51.9 6.1 %shard_map.75 = (bf16[2,128,384]{2,1,0:T(8,128)(2,1)S(1)}, bf16[2,128,384]{2,1,0:T(8,128)(2,1)S(1)}, bf16[2,128,384]{2,1,0:T(8,128)(2,1)S(1)}) custom-call(bf16[2,32,5120]{2,1,0:T(8,128)(2,1)S(1)} %collective-permute-done.3.refs_0_, bf16[2,32,5120]{2,1,0:T(8,128)(2,1)S(1)} %collective-permute-done.4.refs_1_, ...), custom_call_target="tpu_custom_call" | custom-call | flops 3019898880 | bytes 14417920 | tf_op jit(solution)/shard_map/pallas_call | solution.py:148
  58.2 3.7 %collective-permute-start.15 = (bf16[2,272,384]{2,1,0:T(8,128)(2,1)S(1)}, bf16[2,272,384]{2,1,0:T(8,128)(2,1)S(1)}, u32[]{:S(2)}, u32[]{:S(2)}) collective-permute-start(bf16[2,272,384]{2,1,0:T(8,128)(2,1)S(1)} %broadcast_dynamic-update-slice_fusion), channel_id=1, source_target_pairs={{0,64},{8,72},{16,80},{24,88},{32,96},{40,104},{48,112},{56,120},{... | collective-permute-start | bytes 1253384 | tf_op jit(solution)/shard_map/ppermute | solution.py:37
  63.3 7.6 %shard_map.76 = (f32[1,256,384]{2,1,0:T(8,128)S(1)}, bf16[1,256,128]{2,1,0:T(8,128)(2,1)S(1)}) custom-call(bf16[1,272,384]{2,1,0:T(8,128)(2,1)S(1)} %get-tuple-element.100.q_ref, f32[2,2048]{1,0:T(2,128)S(1)} %add_convert_fusion.3.frame_ref, bf16[1,256,384]{2,1,0:T(8,128)(2,1)S(1)} %get-tuple-element.107.rest_0_, ...), custom_call_target="tpu_custom_call" | custom-call | flops 3221225472 | bytes 6291456 | tf_op jit(solution)/shard_map/pallas_call | solution.py:246
  70.9 1.5 %collective-permute-done.15 = bf16[2,272,384]{2,1,0:T(8,128)(2,1)S(1)} collective-permute-done((bf16[2,272,384]{2,1,0:T(8,128)(2,1)S(1)}, bf16[2,272,384]{2,1,0:T(8,128)(2,1)S(1)}, u32[]{:S(2)}, u32[]{:S(2)}) %collective-permute-start.15) | collective-permute-done | bytes 417824 | tf_op jit(solution)/shard_map/ppermute | solution.py:37
  72.4 7.6 %shard_map.77 = bf16[1,256,512]{2,1,0:T(8,128)(2,1)S(1)} custom-call(bf16[1,272,384]{2,1,0:T(8,128)(2,1)S(1)} %get-tuple-element.101.q_ref, f32[2,2048]{1,0:T(2,128)S(1)} %add_convert_fusion.3.frame_ref, bf16[2,512,384]{2,1,0:T(8,128)(2,1)S(1)} %copy-done.4, bf16[2,512,384]{2,1,0:T(8,128)(2,1)} %collective-permute-done.8.rest_3_.rest_1_, ...), custom_call_target="tpu_custom_call" | custom-call | flops 3221225472 | bytes 6291456 | tf_op jit(solution)/shard_map/pallas_call | solution.py:246
  80.0 3.9 %collective-permute-start.16 = (bf16[1,256,512]{2,1,0:T(8,128)(2,1)S(1)}, bf16[1,256,512]{2,1,0:T(8,128)(2,1)S(1)}, u32[]{:S(2)}, u32[]{:S(2)}) collective-permute-start(bf16[1,256,512]{2,1,0:T(8,128)(2,1)S(1)} %shard_map.77), channel_id=1, source_target_pairs={{0,64},{8,72},{16,80},{24,88},{32,96},{40,104},{48,112},{56,120},{... | collective-permute-start | bytes 786440 | tf_op jit(solution)/shard_map/ppermute | solution.py:37
  83.9 7.6 %shard_map.78 = bf16[1,256,512]{2,1,0:T(8,128)(2,1)S(1)} custom-call(bf16[1,272,384]{2,1,0:T(8,128)(2,1)S(1)} %get-tuple-element.70.q_ref, f32[2,2048]{1,0:T(2,128)S(1)} %add_convert_fusion.3.frame_ref, bf16[2,512,384]{2,1,0:T(8,128)(2,1)S(1)} %copy-done.4, bf16[2,512,384]{2,1,0:T(8,128)(2,1)} %collective-permute-done.8.rest_3_.rest_1_, ...), custom_call_target="tpu_custom_call" | custom-call | flops 3221225472 | bytes 6291456 | tf_op jit(solution)/shard_map/pallas_call | solution.py:246
  92.8 7.8 %shard_map.80 = (f32[1,256,384]{2,1,0:T(8,128)S(1)}, bf16[1,256,128]{2,1,0:T(8,128)(2,1)S(1)}) custom-call(bf16[1,272,384]{2,1,0:T(8,128)(2,1)S(1)} %get-tuple-element.78.q_ref, f32[2,2048]{1,0:T(2,128)S(1)} %add_convert_fusion.3.frame_ref, bf16[1,256,384]{2,1,0:T(8,128)(2,1)S(1)} %get-tuple-element.108.rest_0_, ...), custom_call_target="tpu_custom_call" | custom-call | flops 3221225472 | bytes 6291456 | tf_op jit(solution)/shard_map/pallas_call | solution.py:246
  100.6 1.4 %collective-permute-done.19.refs_2_ = bf16[1,256,512]{2,1,0:T(8,128)(2,1)S(1)} collective-permute-done((bf16[1,256,512]{2,1,0:T(8,128)(2,1)S(1)}, bf16[1,256,512]{2,1,0:T(8,128)(2,1)S(1)}, u32[]{:S(2)}, u32[]{:S(2)}) %collective-permute-start.19) | collective-permute-done | bytes 262176 | tf_op jit(solution)/shard_map/ppermute | solution.py:37
  104.7 3.0 %shard_map.82 = (bf16[1,32,5120]{2,1,0:T(8,128)(2,1)S(1)}, bf16[1,32,5120]{2,1,0:T(8,128)(2,1)S(1)}, bf16[1,32,5120]{2,1,0:T(8,128)(2,1)S(1)}, bf16[1,32,5120]{2,1,0:T(8,128)(2,1)S(1)}) custom-call(s32[1]{0:T(128)} %bitcast.1.core, bf16[1,128,384]{2,1,0:T(8,128)(2,1)S(1)} %get-tuple-element.84.a_ref, bf16[1,128,384]{2,1,0:T(8,128)(2,1)S(1)} %collective-permute-done.20.b_ref, ...), custom_call_target="tpu_custom_call" | custom-call | flops 1006632960 | bytes 9175040 | tf_op jit(solution)/shard_map/pallas_call | solution.py:329
  108.0 3.0 %shard_map.83 = (bf16[1,32,5120]{2,1,0:T(8,128)(2,1)S(1)}, bf16[1,32,5120]{2,1,0:T(8,128)(2,1)S(1)}, bf16[1,32,5120]{2,1,0:T(8,128)(2,1)S(1)}, bf16[1,32,5120]{2,1,0:T(8,128)(2,1)S(1)}) custom-call(s32[1]{0:T(128)} %bitcast.1.core, bf16[1,128,384]{2,1,0:T(8,128)(2,1)S(1)} %get-tuple-element.90.a_ref, bf16[1,128,384]{2,1,0:T(8,128)(2,1)S(1)} %collective-permute-done.24.b_ref, ...), custom_call_target="tpu_custom_call" | custom-call | flops 1006632960 | bytes 9175040 | tf_op jit(solution)/shard_map/pallas_call | solution.py:329
  111.1 2.2 %collective-permute-start.27 = (bf16[1,32,5120]{2,1,0:T(8,128)(2,1)S(1)}, bf16[1,32,5120]{2,1,0:T(8,128)(2,1)S(1)}, u32[]{:S(2)}, u32[]{:S(2)}) collective-permute-start(bf16[1,32,5120]{2,1,0:T(8,128)(2,1)S(1)} %get-tuple-element.96), channel_id=1, source_target_pairs={{0,3},{1,0},{2,1},{3,2},{4,7},{5,4},{6,5},{7,6},{8,9},{9,10},{10,1... | collective-permute-start | bytes 983048 | tf_op jit(solution)/shard_map/ppermute | solution.py:51
  113.3 3.2 %collective-permute-start.30 = (bf16[1,32,5120]{2,1,0:T(8,128)(2,1)S(1)}, bf16[1,32,5120]{2,1,0:T(8,128)(2,1)S(1)}, u32[]{:S(2)}, u32[]{:S(2)}) collective-permute-start(bf16[1,32,5120]{2,1,0:T(8,128)(2,1)S(1)} %get-tuple-element.98), channel_id=1, source_target_pairs={{0,1},{1,2},{2,3},{3,0},{4,5},{5,6},{6,7},{7,4},{8,11},{9,8},{10,9... | collective-permute-start | bytes 983048 | tf_op jit(solution)/shard_map/ppermute | solution.py:51
  116.5 5.9 %collective-permute-done.27 = bf16[1,32,5120]{2,1,0:T(8,128)(2,1)S(1)} collective-permute-done((bf16[1,32,5120]{2,1,0:T(8,128)(2,1)S(1)}, bf16[1,32,5120]{2,1,0:T(8,128)(2,1)S(1)}, u32[]{:S(2)}, u32[]{:S(2)}) %collective-permute-start.27) | collective-permute-done | bytes 327712 | tf_op jit(solution)/shard_map/ppermute | solution.py:51
  122.5 1.5 %collective-permute-start.28 = (bf16[1,32,5120]{2,1,0:T(8,128)(2,1)S(1)}, bf16[1,32,5120]{2,1,0:T(8,128)(2,1)S(1)}, u32[]{:S(2)}, u32[]{:S(2)}) collective-permute-start(bf16[1,32,5120]{2,1,0:T(8,128)(2,1)S(1)} %add_convert_fusion.1), channel_id=1, source_target_pairs={{0,3},{1,0},{2,1},{3,2},{4,7},{5,4},{6,5},{7,6},{8,9},{9,10},{10,1... | collective-permute-start | bytes 983048 | tf_op jit(solution)/shard_map/ppermute | solution.py:51
  124.0 5.5 %collective-permute-done.25 = bf16[1,32,5120]{2,1,0:T(8,128)(2,1)S(1)} collective-permute-done((bf16[1,32,5120]{2,1,0:T(8,128)(2,1)S(1)}, bf16[1,32,5120]{2,1,0:T(8,128)(2,1)S(1)}, u32[]{:S(2)}, u32[]{:S(2)}) %collective-permute-start.25) | collective-permute-done | bytes 327712 | tf_op jit(solution)/shard_map/ppermute | solution.py:51
  130.0 1.6 %collective-permute-done.29 = bf16[1,32,5120]{2,1,0:T(8,128)(2,1)S(1)} collective-permute-done((bf16[1,32,5120]{2,1,0:T(8,128)(2,1)S(1)}, bf16[1,32,5120]{2,1,0:T(8,128)(2,1)S(1)}, u32[]{:S(2)}, u32[]{:S(2)}) %collective-permute-start.29) | collective-permute-done | bytes 327712 | tf_op jit(solution)/shard_map/ppermute | solution.py:51
  131.7 1.8 %collective-permute-done.28 = bf16[1,32,5120]{2,1,0:T(8,128)(2,1)S(1)} collective-permute-done((bf16[1,32,5120]{2,1,0:T(8,128)(2,1)S(1)}, bf16[1,32,5120]{2,1,0:T(8,128)(2,1)S(1)}, u32[]{:S(2)}, u32[]{:S(2)}) %collective-permute-start.28) | collective-permute-done | bytes 327712 | tf_op jit(solution)/shard_map/ppermute | solution.py:51
  133.4 4.5 %collective-permute-done.26 = bf16[1,32,5120]{2,1,0:T(8,128)(2,1)S(1)} collective-permute-done((bf16[1,32,5120]{2,1,0:T(8,128)(2,1)S(1)}, bf16[1,32,5120]{2,1,0:T(8,128)(2,1)S(1)}, u32[]{:S(2)}, u32[]{:S(2)}) %collective-permute-start.26) | collective-permute-done | bytes 327712 | tf_op jit(solution)/shard_map/ppermute | solution.py:51
  137.9 1.2 add_convert_fusion
  (93 shorter events, 11.2 us)
Async XLA Ops:
  0.0 39.0 %copy-start.9 = (s32[2]{0:T(128)S(1)}, s32[2]{0:T(128)}, u32[]{:S(2)}) copy-start(s32[2]{0:T(128)} %param.9) | copy-start | bytes 28
  4.6 17.2 %collective-permute-start = (bf16[2,32,5120]{2,1,0:T(8,128)(2,1)}, bf16[2,32,5120]{2,1,0:T(8,128)(2,1)S(1)}, u32[]{:S(2)}, u32[]{:S(2)}) collective-permute-start(bf16[2,32,5120]{2,1,0:T(8,128)(2,1)} %get-tuple-element.53.refs_0_), channel_id=1, source_target_pairs={{0,1},{1,2},{2,3},{3,0},{4,5},{5,6},{6,7},{7,4},{8,11},{9,8},{10,9... | collective-permute-start | bytes 1966088 | tf_op jit(solution)/shard_map/ppermute | solution.py:51
  4.9 17.7 %collective-permute-start.1 = (bf16[2,32,5120]{2,1,0:T(8,128)(2,1)}, bf16[2,32,5120]{2,1,0:T(8,128)(2,1)S(1)}, u32[]{:S(2)}, u32[]{:S(2)}) collective-permute-start(bf16[2,32,5120]{2,1,0:T(8,128)(2,1)} %get-tuple-element.53.refs_0_), channel_id=1, source_target_pairs={{0,3},{1,0},{2,1},{3,2},{4,7},{5,4},{6,5},{7,6},{8,9},{9,10},{10,1... | collective-permute-start | bytes 1966088 | tf_op jit(solution)/shard_map/ppermute | solution.py:51
  6.7 21.6 %collective-permute-start.8 = (bf16[2,512,384]{2,1,0:T(8,128)(2,1)S(1)}, bf16[2,512,384]{2,1,0:T(8,128)(2,1)}, u32[]{:S(2)}, u32[]{:S(2)}) collective-permute-start(bf16[2,512,384]{2,1,0:T(8,128)(2,1)S(1)} %copy-done.4), channel_id=1, source_target_pairs={{0,16},{1,17},{2,18},{3,19},{4,20},{5,21},{6,22},{7,23},{8,56},{9,... | collective-permute-start | bytes 2359304 | tf_op jit(solution)/shard_map/ppermute | solution.py:51
  7.9 20.8 %collective-permute-start.9 = (bf16[2,512,384]{2,1,0:T(8,128)(2,1)S(1)}, bf16[2,512,384]{2,1,0:T(8,128)(2,1)}, u32[]{:S(2)}, u32[]{:S(2)}) collective-permute-start(bf16[2,512,384]{2,1,0:T(8,128)(2,1)S(1)} %copy-done.4), channel_id=1, source_target_pairs={{0,48},{1,49},{2,50},{3,51},{4,52},{5,53},{6,54},{7,55},{8,24},{9,... | collective-permute-start | bytes 2359304 | tf_op jit(solution)/shard_map/ppermute | solution.py:51
  8.8 17.9 %collective-permute-start.2 = (bf16[2,32,5120]{2,1,0:T(8,128)(2,1)}, bf16[2,32,5120]{2,1,0:T(8,128)(2,1)S(1)}, u32[]{:S(2)}, u32[]{:S(2)}) collective-permute-start(bf16[2,32,5120]{2,1,0:T(8,128)(2,1)} %get-tuple-element.53.refs_0_), channel_id=1, source_target_pairs={{0,4},{1,5},{2,6},{3,7},{4,0},{5,1},{6,2},{7,3},{8,12},{9,13},{10,... | collective-permute-start | bytes 1966088 | tf_op jit(solution)/shard_map/ppermute | solution.py:27
  21.9 14.6 %collective-permute-start.3 = (bf16[2,32,5120]{2,1,0:T(8,128)(2,1)S(1)}, bf16[2,32,5120]{2,1,0:T(8,128)(2,1)S(1)}, u32[]{:S(2)}, u32[]{:S(2)}) collective-permute-start(bf16[2,32,5120]{2,1,0:T(8,128)(2,1)S(1)} %collective-permute-done.refs_1_), channel_id=1, source_target_pairs={{0,1},{1,2},{2,3},{3,0},{4,5},{5,6},{6,7},{7,4},{8,11},{9,8},{10,9... | collective-permute-start | bytes 1966088 | tf_op jit(solution)/shard_map/ppermute | solution.py:51
  22.6 28.2 %collective-permute-start.7 = (bf16[96,5120]{1,0:T(8,128)(2,1)}, bf16[96,5120]{1,0:T(8,128)(2,1)S(1)}, u32[]{:S(2)}, u32[]{:S(2)}) collective-permute-start(bf16[96,5120]{1,0:T(8,128)(2,1)} %get-tuple-element.55), channel_id=1, source_target_pairs={{0,68},{1,69},{2,70},{3,71},{4,64},{5,65},{6,66},{7,67},{8,76},{9,... | collective-permute-start | bytes 2949128 | tf_op jit(solution)/shard_map/ppermute | solution.py:59
  26.7 24.8 %collective-permute-start.4 = (bf16[2,32,5120]{2,1,0:T(8,128)(2,1)S(1)}, bf16[2,32,5120]{2,1,0:T(8,128)(2,1)S(1)}, u32[]{:S(2)}, u32[]{:S(2)}) collective-permute-start(bf16[2,32,5120]{2,1,0:T(8,128)(2,1)S(1)} %collective-permute-done.2.refs_3_), channel_id=1, source_target_pairs={{0,1},{1,2},{2,3},{3,0},{4,5},{5,6},{6,7},{7,4},{8,11},{9,8},{10,9... | collective-permute-start | bytes 1966088 | tf_op jit(solution)/shard_map/ppermute | solution.py:51
  28.3 23.5 %collective-permute-start.5 = (bf16[2,32,5120]{2,1,0:T(8,128)(2,1)S(1)}, bf16[2,32,5120]{2,1,0:T(8,128)(2,1)S(1)}, u32[]{:S(2)}, u32[]{:S(2)}) collective-permute-start(bf16[2,32,5120]{2,1,0:T(8,128)(2,1)S(1)} %collective-permute-done.2.refs_3_), channel_id=1, source_target_pairs={{0,3},{1,0},{2,1},{3,2},{4,7},{5,4},{6,5},{7,6},{8,9},{9,10},{10,1... | collective-permute-start | bytes 1966088 | tf_op jit(solution)/shard_map/ppermute | solution.py:51
  28.8 22.0 %collective-permute-start.10 = (bf16[2,512,384]{2,1,0:T(8,128)(2,1)}, bf16[2,512,384]{2,1,0:T(8,128)(2,1)S(1)}, u32[]{:S(2)}, u32[]{:S(2)}) collective-permute-start(bf16[2,512,384]{2,1,0:T(8,128)(2,1)} %collective-permute-done.8.rest_3_.rest_1_), channel_id=1, source_target_pairs={{0,16},{1,17},{2,18},{3,19},{4,20},{5,21},{6,22},{7,23},{8,56},{9,... | collective-permute-start | bytes 2359304 | tf_op jit(solution)/shard_map/ppermute | solution.py:51
  36.4 14.9 %collective-permute-start.6 = (bf16[2,32,5120]{2,1,0:T(8,128)(2,1)S(1)}, bf16[2,32,5120]{2,1,0:T(8,128)(2,1)S(1)}, u32[]{:S(2)}, u32[]{:S(2)}) collective-permute-start(bf16[2,32,5120]{2,1,0:T(8,128)(2,1)S(1)} %collective-permute-done.3.refs_0_), channel_id=1, source_target_pairs={{0,4},{1,5},{2,6},{3,7},{4,0},{5,1},{6,2},{7,3},{8,12},{9,13},{10,... | collective-permute-start | bytes 1966088 | tf_op jit(solution)/shard_map/ppermute | solution.py:27
  50.7 11.4 %collective-permute-start.11 = (bf16[2,512,384]{2,1,0:T(8,128)(2,1)S(1)}, bf16[2,512,384]{2,1,0:T(8,128)(2,1)S(1)}, u32[]{:S(2)}, u32[]{:S(2)}) collective-permute-start(bf16[2,512,384]{2,1,0:T(8,128)(2,1)S(1)} %copy-done.4), channel_id=1, source_target_pairs={{0,8},{8,0},{16,24},{24,16},{32,40},{40,32},{48,56},{56,48},{64,72... | collective-permute-start | bytes 2359304 | tf_op jit(solution)/shard_map/ppermute | solution.py:37
  50.9 12.2 %collective-permute-start.12 = (bf16[2,512,384]{2,1,0:T(8,128)(2,1)}, bf16[2,512,384]{2,1,0:T(8,128)(2,1)S(1)}, u32[]{:S(2)}, u32[]{:S(2)}) collective-permute-start(bf16[2,512,384]{2,1,0:T(8,128)(2,1)} %collective-permute-done.8.rest_3_.rest_1_), channel_id=1, source_target_pairs={{0,8},{8,0},{16,24},{24,16},{32,40},{40,32},{48,56},{56,48},{64,72... | collective-permute-start | bytes 2359304 | tf_op jit(solution)/shard_map/ppermute | solution.py:37
  51.3 11.8 %collective-permute-start.13 = (bf16[2,512,384]{2,1,0:T(8,128)(2,1)}, bf16[2,512,384]{2,1,0:T(8,128)(2,1)S(1)}, u32[]{:S(2)}, u32[]{:S(2)}) collective-permute-start(bf16[2,512,384]{2,1,0:T(8,128)(2,1)} %collective-permute-done.9.rest_4_.rest_2_), channel_id=1, source_target_pairs={{0,8},{8,0},{16,24},{24,16},{32,40},{40,32},{48,56},{56,48},{64,72... | collective-permute-start | bytes 2359304 | tf_op jit(solution)/shard_map/ppermute | solution.py:37
  51.4 11.8 %collective-permute-start.14 = (bf16[2,512,384]{2,1,0:T(8,128)(2,1)S(1)}, bf16[2,512,384]{2,1,0:T(8,128)(2,1)S(1)}, u32[]{:S(2)}, u32[]{:S(2)}) collective-permute-start(bf16[2,512,384]{2,1,0:T(8,128)(2,1)S(1)} %collective-permute-done.10.rest_5_.rest_3_), channel_id=1, source_target_pairs={{0,8},{8,0},{16,24},{24,16},{32,40},{40,32},{48,56},{56,48},{64,72... | collective-permute-start | bytes 2359304 | tf_op jit(solution)/shard_map/ppermute | solution.py:37
  58.2 14.1 %collective-permute-start.15 = (bf16[2,272,384]{2,1,0:T(8,128)(2,1)S(1)}, bf16[2,272,384]{2,1,0:T(8,128)(2,1)S(1)}, u32[]{:S(2)}, u32[]{:S(2)}) collective-permute-start(bf16[2,272,384]{2,1,0:T(8,128)(2,1)S(1)} %broadcast_dynamic-update-slice_fusion), channel_id=1, source_target_pairs={{0,64},{8,72},{16,80},{24,88},{32,96},{40,104},{48,112},{56,120},{... | collective-permute-start | bytes 1253384 | tf_op jit(solution)/shard_map/ppermute | solution.py:37
  63.0 37.6 %collective-permute-start.17 = (bf16[48,5120]{1,0:T(8,128)(2,1)S(1)}, bf16[48,5120]{1,0:T(8,128)(2,1)S(1)}, u32[]{:S(2)}, u32[]{:S(2)}) collective-permute-start(bf16[48,5120]{1,0:T(8,128)(2,1)S(1)} %copy-done.8), channel_id=1, source_target_pairs={{0,68},{1,69},{2,70},{3,71},{4,64},{5,65},{6,66},{7,67},{8,76},{9,... | collective-permute-start | bytes 1474568 | tf_op jit(solution)/shard_map/ppermute | solution.py:59
  63.2 37.4 %collective-permute-start.18 = (bf16[48,5120]{1,0:T(8,128)(2,1)S(1)}, bf16[48,5120]{1,0:T(8,128)(2,1)S(1)}, u32[]{:S(2)}, u32[]{:S(2)}) collective-permute-start(bf16[48,5120]{1,0:T(8,128)(2,1)S(1)} %copy-done.7), channel_id=1, source_target_pairs={{0,4},{1,5},{2,6},{3,7},{4,0},{5,1},{6,2},{7,3},{8,12},{9,13},{10,... | collective-permute-start | bytes 1474568 | tf_op jit(solution)/shard_map/ppermute | solution.py:27
  63.2 40.4 %collective-permute-start.21 = (bf16[96,5120]{1,0:T(8,128)(2,1)S(1)}, bf16[96,5120]{1,0:T(8,128)(2,1)S(1)}, u32[]{:S(2)}, u32[]{:S(2)}) collective-permute-start(bf16[96,5120]{1,0:T(8,128)(2,1)S(1)} %collective-permute-done.7.rest_0_), channel_id=1, source_target_pairs={{0,8},{8,0},{16,24},{24,16},{32,40},{40,32},{48,56},{56,48},{64,72... | collective-permute-start | bytes 2949128 | tf_op jit(solution)/shard_map/ppermute | solution.py:37
  80.0 11.6 %collective-permute-start.16 = (bf16[1,256,512]{2,1,0:T(8,128)(2,1)S(1)}, bf16[1,256,512]{2,1,0:T(8,128)(2,1)S(1)}, u32[]{:S(2)}, u32[]{:S(2)}) collective-permute-start(bf16[1,256,512]{2,1,0:T(8,128)(2,1)S(1)} %shard_map.77), channel_id=1, source_target_pairs={{0,64},{8,72},{16,80},{24,88},{32,96},{40,104},{48,112},{56,120},{... | collective-permute-start | bytes 786440 | tf_op jit(solution)/shard_map/ppermute | solution.py:37
  91.5 10.5 %collective-permute-start.19 = (bf16[1,256,512]{2,1,0:T(8,128)(2,1)S(1)}, bf16[1,256,512]{2,1,0:T(8,128)(2,1)S(1)}, u32[]{:S(2)}, u32[]{:S(2)}) collective-permute-start(bf16[1,256,512]{2,1,0:T(8,128)(2,1)S(1)} %shard_map.78), channel_id=1, source_target_pairs={{0,64},{8,72},{16,80},{24,88},{32,96},{40,104},{48,112},{56,120},{... | collective-permute-start | bytes 786440 | tf_op jit(solution)/shard_map/ppermute | solution.py:37
  92.3 9.8 %collective-permute-start.20 = (bf16[1,128,384]{2,1,0:T(8,128)(2,1)S(1)}, bf16[1,128,384]{2,1,0:T(8,128)(2,1)S(1)}, u32[]{:S(2)}, u32[]{:S(2)}) collective-permute-start(bf16[1,128,384]{2,1,0:T(8,128)(2,1)S(1)} %get-tuple-element.77), channel_id=1, source_target_pairs={{0,4},{1,5},{2,6},{3,7},{4,0},{5,1},{6,2},{7,3},{8,12},{9,13},{10,... | collective-permute-start | bytes 294920 | tf_op jit(solution)/shard_map/ppermute | solution.py:27
  102.1 1.9 %collective-permute-start.22 = (bf16[48,5120]{1,0:T(8,128)(2,1)S(1)}, bf16[48,5120]{1,0:T(8,128)(2,1)S(1)}, u32[]{:S(2)}, u32[]{:S(2)}) collective-permute-start(bf16[48,5120]{1,0:T(8,128)(2,1)S(1)} %collective-permute-done.17.rest_1_), channel_id=1, source_target_pairs={{0,8},{8,0},{16,24},{24,16},{32,40},{40,32},{48,56},{56,48},{64,72... | collective-permute-start | bytes 1474568 | tf_op jit(solution)/shard_map/ppermute | solution.py:37
  102.1 2.6 %collective-permute-start.23 = (bf16[48,5120]{1,0:T(8,128)(2,1)S(1)}, bf16[48,5120]{1,0:T(8,128)(2,1)S(1)}, u32[]{:S(2)}, u32[]{:S(2)}) collective-permute-start(bf16[48,5120]{1,0:T(8,128)(2,1)S(1)} %collective-permute-done.18.rest_2_), channel_id=1, source_target_pairs={{0,8},{8,0},{16,24},{24,16},{32,40},{40,32},{48,56},{56,48},{64,72... | collective-permute-start | bytes 1474568 | tf_op jit(solution)/shard_map/ppermute | solution.py:37
  103.3 4.8 %collective-permute-start.24 = (bf16[1,128,384]{2,1,0:T(8,128)(2,1)S(1)}, bf16[1,128,384]{2,1,0:T(8,128)(2,1)S(1)}, u32[]{:S(2)}, u32[]{:S(2)}) collective-permute-start(bf16[1,128,384]{2,1,0:T(8,128)(2,1)S(1)} %get-tuple-element.83), channel_id=1, source_target_pairs={{0,4},{1,5},{2,6},{3,7},{4,0},{5,1},{6,2},{7,3},{8,12},{9,13},{10,... | collective-permute-start | bytes 294920 | tf_op jit(solution)/shard_map/ppermute | solution.py:27
  111.1 11.4 %collective-permute-start.27 = (bf16[1,32,5120]{2,1,0:T(8,128)(2,1)S(1)}, bf16[1,32,5120]{2,1,0:T(8,128)(2,1)S(1)}, u32[]{:S(2)}, u32[]{:S(2)}) collective-permute-start(bf16[1,32,5120]{2,1,0:T(8,128)(2,1)S(1)} %get-tuple-element.96), channel_id=1, source_target_pairs={{0,3},{1,0},{2,1},{3,2},{4,7},{5,4},{6,5},{7,6},{8,9},{9,10},{10,1... | collective-permute-start | bytes 983048 | tf_op jit(solution)/shard_map/ppermute | solution.py:51
  113.2 16.2 %collective-permute-start.25 = (bf16[1,32,5120]{2,1,0:T(8,128)(2,1)S(1)}, bf16[1,32,5120]{2,1,0:T(8,128)(2,1)S(1)}, u32[]{:S(2)}, u32[]{:S(2)}) collective-permute-start(bf16[1,32,5120]{2,1,0:T(8,128)(2,1)S(1)} %get-tuple-element.94), channel_id=1, source_target_pairs={{0,3},{1,0},{2,1},{3,2},{4,7},{5,4},{6,5},{7,6},{8,9},{9,10},{10,1... | collective-permute-start | bytes 983048 | tf_op jit(solution)/shard_map/ppermute | solution.py:51
  113.3 16.7 %collective-permute-start.30 = (bf16[1,32,5120]{2,1,0:T(8,128)(2,1)S(1)}, bf16[1,32,5120]{2,1,0:T(8,128)(2,1)S(1)}, u32[]{:S(2)}, u32[]{:S(2)}) collective-permute-start(bf16[1,32,5120]{2,1,0:T(8,128)(2,1)S(1)} %get-tuple-element.98), channel_id=1, source_target_pairs={{0,1},{1,2},{2,3},{3,0},{4,5},{5,6},{6,7},{7,4},{8,11},{9,8},{10,9... | collective-permute-start | bytes 983048 | tf_op jit(solution)/shard_map/ppermute | solution.py:51
  116.5 15.2 %collective-permute-start.29 = (bf16[1,32,5120]{2,1,0:T(8,128)(2,1)S(1)}, bf16[1,32,5120]{2,1,0:T(8,128)(2,1)S(1)}, u32[]{:S(2)}, u32[]{:S(2)}) collective-permute-start(bf16[1,32,5120]{2,1,0:T(8,128)(2,1)S(1)} %get-tuple-element.97), channel_id=1, source_target_pairs={{0,1},{1,2},{2,3},{3,0},{4,5},{5,6},{6,7},{7,4},{8,11},{9,8},{10,9... | collective-permute-start | bytes 983048 | tf_op jit(solution)/shard_map/ppermute | solution.py:51
  122.5 10.9 %collective-permute-start.28 = (bf16[1,32,5120]{2,1,0:T(8,128)(2,1)S(1)}, bf16[1,32,5120]{2,1,0:T(8,128)(2,1)S(1)}, u32[]{:S(2)}, u32[]{:S(2)}) collective-permute-start(bf16[1,32,5120]{2,1,0:T(8,128)(2,1)S(1)} %add_convert_fusion.1), channel_id=1, source_target_pairs={{0,3},{1,0},{2,1},{3,2},{4,7},{5,4},{6,5},{7,6},{8,9},{9,10},{10,1... | collective-permute-start | bytes 983048 | tf_op jit(solution)/shard_map/ppermute | solution.py:51
  129.5 8.4 %collective-permute-start.26 = (bf16[1,32,5120]{2,1,0:T(8,128)(2,1)S(1)}, bf16[1,32,5120]{2,1,0:T(8,128)(2,1)S(1)}, u32[]{:S(2)}, u32[]{:S(2)}) collective-permute-start(bf16[1,32,5120]{2,1,0:T(8,128)(2,1)S(1)} %add_convert_fusion.2), channel_id=1, source_target_pairs={{0,3},{1,0},{2,1},{3,2},{4,7},{5,4},{6,5},{7,6},{8,9},{9,10},{10,1... | collective-permute-start | bytes 983048 | tf_op jit(solution)/shard_map/ppermute | solution.py:51
  (9 other events, 79.4 us)

commit v6 on v5

--- a/solution.py
+++ b/solution.py
@@ -241,7 +241,7 @@
 
 
 def attend(q, frames, parts, own=None):
-    branches, blocks, chunk = q.shape[0], len(parts), 2048
+    branches, blocks, chunk = q.shape[0], len(parts), 4096
     state = pltpu.VMEM((branches, HERE, FRAME_TOK, HDIM), jnp.float32)
     return pl.pallas_call(
         functools.partial(attend_kernel, branches, chunk, blocks, own is not None),
@@ -324,7 +324,7 @@
 
 
 def project_out(core, a, b, wa, pieces):
-    branches, rows, width, block = a.shape[0], a.shape[1], wa.shape[1], 1280
+    branches, rows, width, block = a.shape[0], a.shape[1], wa.shape[1], 2560
     count = rows // 32
     return pl.pallas_call(
         out_kernel,

time: 140 us -> 149 us (1.064)
  starting transfers between devices: 33.8 us -> 48.5 us
  Pallas kernels: 54.8 us -> 50.7 us
  waiting for transfers between devices: 41.4 us -> 39.4 us
    ppermute x10, starting transfers between devices: 9.27 us -> 22.3 us  [along_branch(): return lax.ppermute(a, 'branch', perm)]
    pallas_call x4, Pallas kernels: 30.6 us -> 27.5 us  [attend(): pl.pallas_call(functools.partial(attend_kernel, branches, chunk, blocks,...]
    ppermute x14, waiting for transfers between devices: 36.9 us -> 34.6 us  [turned(): return lax.ppermute(a, ('branch', 'seq'), perm)]
    unnamed x29 -> x26, local copies, waits for them, and re-layouts: 6.64 us -> 6.58 us
  transfers between devices with their start and end apart: 31 -> 31, of which waited for: 13 -> 14; matrix products, arithmetic and copies ran while one was open for 1% -> 1% of each run, Pallas kernels for 34% -> 29%
where the time goes in v6:
time: 149 us; the launch traced here: 148 us
  Pallas kernels  50.7 us (34%)
  starting transfers between devices  48.5 us (33%)
  waiting for transfers between devices  39.4 us (26%)
  local copies, waits for them, and re-layouts  7 us (5%)
  other arithmetic  1.54 us (1%)
    ppermute x14, waiting for transfers between devices, turned(): return lax.ppermute(a, ('branch', 'seq'), perm)  34.6 us
    pallas_call x4, Pallas kernels, attend(): pl.pallas_call(functools.partial(attend_kernel, branches, chunk, blocks,...  27.5 us
    ppermute x10, starting transfers between devices, along_branch(): return lax.ppermute(a, 'branch', perm)  22.3 us
    ppermute x14, starting transfers between devices, turned(): return lax.ppermute(a, ('branch', 'seq'), perm)  16.6 us
    pallas_call x2, Pallas kernels, project_qkv(): pl.pallas_call(functools.partial(qkv_kernel, count), grid=(depth // block...  12.3 us
    unnamed x26, local copies, waits for them, and re-layouts  6.58 us
    ppermute x5, starting transfers between devices, along_seq(): return lax.ppermute(a, 'seq', perm)  5.62 us
    pallas_call x2, Pallas kernels, project_out(): pl.pallas_call(out_kernel, grid=(width // block,), out_shape=(jax.ShapeDt...  5.07 us
  transfers between devices with their start and end apart: 31, of which 14 were waited for; matrix products, arithmetic and copies ran while one was open for 1% of the time, Pallas kernels for 29%

profile of v6, /device:TPU:28, one launch (start us, length us, event | category | flops | bytes accessed | tf_op | source)
XLA Modules:
  0.0 147.7 jit_solution(7941773874369520904)
XLA Ops:
  0.0 4.6 %shard_map.73 = (bf16[2,32,5120]{2,1,0:T(8,128)(2,1)}, f32[2,1,5120]{2,1,0:T(1,128)}, bf16[96,5120]{1,0:T(8,128)(2,1)}, bf16[48,5120]{1,0:T(8,128)(2,1)}, bf16[48,5120]{1,0:T(8,128)(2,1)}) custom-call(s32[2]{0:T(128)} %actions.1, bf16[2,32,5120]{2,1,0:T(8,128)(2,1)} %x_hbm.1, bf16[3,16,5120]{2,1,0:T(8,128)(2,1)} %bitcast.24, bf16[384,5120]{1,0:T(8,128)(2,1)} %wa_ref.3), custom_call_target="tpu_custom_call" | custom-call | tf_op jit(solution)/shard_map/pallas_call | solution.py:106
  4.9 1.8 %collective-permute-start.1 = (bf16[2,32,5120]{2,1,0:T(8,128)(2,1)}, bf16[2,32,5120]{2,1,0:T(8,128)(2,1)S(1)}, u32[]{:S(2)}, u32[]{:S(2)}) collective-permute-start(bf16[2,32,5120]{2,1,0:T(8,128)(2,1)} %get-tuple-element.53.refs_0_), channel_id=1, source_target_pairs={{0,3},{1,0},{2,1},{3,2},{4,7},{5,4},{6,5},{7,6},{8,9},{9,10},{10,1... | collective-permute-start | bytes 1966088 | tf_op jit(solution)/shard_map/ppermute | solution.py:51
  6.7 1.2 collective-permute-start.8
  8.8 1.9 %collective-permute-start.2 = (bf16[2,32,5120]{2,1,0:T(8,128)(2,1)}, bf16[2,32,5120]{2,1,0:T(8,128)(2,1)S(1)}, u32[]{:S(2)}, u32[]{:S(2)}) collective-permute-start(bf16[2,32,5120]{2,1,0:T(8,128)(2,1)} %get-tuple-element.53.refs_0_), channel_id=1, source_target_pairs={{0,4},{1,5},{2,6},{3,7},{4,0},{5,1},{6,2},{7,3},{8,12},{9,13},{10,... | collective-permute-start | bytes 1966088 | tf_op jit(solution)/shard_map/ppermute | solution.py:27
  10.7 11.2 %collective-permute-done.refs_1_ = bf16[2,32,5120]{2,1,0:T(8,128)(2,1)S(1)} collective-permute-done((bf16[2,32,5120]{2,1,0:T(8,128)(2,1)}, bf16[2,32,5120]{2,1,0:T(8,128)(2,1)S(1)}, u32[]{:S(2)}, u32[]{:S(2)}) %collective-permute-start) | collective-permute-done | bytes 655392 | tf_op jit(solution)/shard_map/ppermute | solution.py:51
  22.6 4.0 %collective-permute-start.7 = (bf16[96,5120]{1,0:T(8,128)(2,1)}, bf16[96,5120]{1,0:T(8,128)(2,1)S(1)}, u32[]{:S(2)}, u32[]{:S(2)}) collective-permute-start(bf16[96,5120]{1,0:T(8,128)(2,1)} %get-tuple-element.55), channel_id=1, source_target_pairs={{0,68},{1,69},{2,70},{3,71},{4,64},{5,65},{6,66},{7,67},{8,76},{9,... | collective-permute-start | bytes 2949128 | tf_op jit(solution)/shard_map/ppermute | solution.py:59
  27.0 1.4 collective-permute-start.10
  28.4 1.1 collective-permute-start.4
  30.5 4.8 %collective-permute-done.3.refs_0_ = bf16[2,32,5120]{2,1,0:T(8,128)(2,1)S(1)} collective-permute-done((bf16[2,32,5120]{2,1,0:T(8,128)(2,1)S(1)}, bf16[2,32,5120]{2,1,0:T(8,128)(2,1)S(1)}, u32[]{:S(2)}, u32[]{:S(2)}) %collective-permute-start.3) | collective-permute-done | bytes 655392 | tf_op jit(solution)/shard_map/ppermute | solution.py:51
  35.3 1.9 %collective-permute-start.6 = (bf16[2,32,5120]{2,1,0:T(8,128)(2,1)S(1)}, bf16[2,32,5120]{2,1,0:T(8,128)(2,1)S(1)}, u32[]{:S(2)}, u32[]{:S(2)}) collective-permute-start(bf16[2,32,5120]{2,1,0:T(8,128)(2,1)S(1)} %collective-permute-done.3.refs_0_), channel_id=1, source_target_pairs={{0,4},{1,5},{2,6},{3,7},{4,0},{5,1},{6,2},{7,3},{8,12},{9,13},{10,... | collective-permute-start | bytes 1966088 | tf_op jit(solution)/shard_map/ppermute | solution.py:27
  37.3 4.3 %copy-done = bf16[5120,3,384]{2,0,1:T(8,128)(2,1)S(1)} copy-done((bf16[5120,3,384]{2,0,1:T(8,128)(2,1)S(1)}, bf16[5120,3,384]{2,0,1:T(8,128)(2,1)}, u32[]{:S(2)}) %copy-start) | copy-done | bytes 11796504
  41.7 1.1 copy-done.3
  42.8 6.1 %shard_map.74 = (bf16[2,128,384]{2,1,0:T(8,128)(2,1)S(1)}, bf16[2,128,384]{2,1,0:T(8,128)(2,1)S(1)}, bf16[2,128,384]{2,1,0:T(8,128)(2,1)S(1)}) custom-call(bf16[2,32,5120]{2,1,0:T(8,128)(2,1)S(1)} %copy-done.3, bf16[2,32,5120]{2,1,0:T(8,128)(2,1)S(1)} %collective-permute-done.refs_1_, bf16[2,32,5120]{2,1,0:T(8,128)(2,1)S(1)} %collective-permute-done.1.refs_2_, ...), custom_call_target="tpu_custom_call" | custom-call | flops 3019898880 | bytes 14417920 | tf_op jit(solution)/shard_map/pallas_call | solution.py:148
  50.4 6.1 %shard_map.75 = (bf16[2,128,384]{2,1,0:T(8,128)(2,1)S(1)}, bf16[2,128,384]{2,1,0:T(8,128)(2,1)S(1)}, bf16[2,128,384]{2,1,0:T(8,128)(2,1)S(1)}) custom-call(bf16[2,32,5120]{2,1,0:T(8,128)(2,1)S(1)} %collective-permute-done.3.refs_0_, bf16[2,32,5120]{2,1,0:T(8,128)(2,1)S(1)} %collective-permute-done.4.refs_1_, ...), custom_call_target="tpu_custom_call" | custom-call | flops 3019898880 | bytes 14417920 | tf_op jit(solution)/shard_map/pallas_call | solution.py:148
  56.8 3.7 %collective-permute-start.15 = (bf16[2,272,384]{2,1,0:T(8,128)(2,1)S(1)}, bf16[2,272,384]{2,1,0:T(8,128)(2,1)S(1)}, u32[]{:S(2)}, u32[]{:S(2)}) collective-permute-start(bf16[2,272,384]{2,1,0:T(8,128)(2,1)S(1)} %broadcast_dynamic-update-slice_fusion), channel_id=1, source_target_pairs={{0,64},{8,72},{16,80},{24,88},{32,96},{40,104},{48,112},{56,120},{... | collective-permute-start | bytes 1253384 | tf_op jit(solution)/shard_map/ppermute | solution.py:37
  62.3 6.8 %shard_map.76 = (f32[1,256,384]{2,1,0:T(8,128)S(1)}, bf16[1,256,128]{2,1,0:T(8,128)(2,1)S(1)}) custom-call(bf16[1,272,384]{2,1,0:T(8,128)(2,1)S(1)} %get-tuple-element.100.q_ref, f32[1,4096]{1,0:T(1,128)S(1)} %bitcast.20, bf16[1,256,384]{2,1,0:T(8,128)(2,1)S(1)} %get-tuple-element.107.rest_0_, bf16[1,256,384]{2,1,0:T(8,128)(2,1)S(1)} %get-tuple-element.104.rest_1_, ...), custom_call_target="tpu_custom_call" | custom-call | flops 3221225472 | bytes 6291456 | tf_op jit(solution)/shard_map/pallas_call | solution.py:246
  69.1 1.8 %collective-permute-done.15 = bf16[2,272,384]{2,1,0:T(8,128)(2,1)S(1)} collective-permute-done((bf16[2,272,384]{2,1,0:T(8,128)(2,1)S(1)}, bf16[2,272,384]{2,1,0:T(8,128)(2,1)S(1)}, u32[]{:S(2)}, u32[]{:S(2)}) %collective-permute-start.15) | collective-permute-done | bytes 417824 | tf_op jit(solution)/shard_map/ppermute | solution.py:37
  71.0 6.8 %shard_map.77 = bf16[1,256,512]{2,1,0:T(8,128)(2,1)S(1)} custom-call(bf16[1,272,384]{2,1,0:T(8,128)(2,1)S(1)} %get-tuple-element.101.q_ref, f32[1,4096]{1,0:T(1,128)S(1)} %bitcast.21, bf16[2,512,384]{2,1,0:T(8,128)(2,1)S(1)} %copy-done.4, bf16[2,512,384]{2,1,0:T(8,128)(2,1)} %collective-permute-done.8.rest_3_.rest_1_, ...), custom_call_target="tpu_custom_call" | custom-call | flops 3221225472 | bytes 6291456 | tf_op jit(solution)/shard_map/pallas_call | solution.py:246
  77.8 16.7 %collective-permute-start.16 = (bf16[1,256,512]{2,1,0:T(8,128)(2,1)S(1)}, bf16[1,256,512]{2,1,0:T(8,128)(2,1)S(1)}, u32[]{:S(2)}, u32[]{:S(2)}) collective-permute-start(bf16[1,256,512]{2,1,0:T(8,128)(2,1)S(1)} %shard_map.77), channel_id=1, source_target_pairs={{0,64},{8,72},{16,80},{24,88},{32,96},{40,104},{48,112},{56,120},{... | collective-permute-start | bytes 786440 | tf_op jit(solution)/shard_map/ppermute | solution.py:37
  94.5 6.9 %shard_map.78 = bf16[1,256,512]{2,1,0:T(8,128)(2,1)S(1)} custom-call(bf16[1,272,384]{2,1,0:T(8,128)(2,1)S(1)} %get-tuple-element.70.q_ref, f32[1,4096]{1,0:T(1,128)S(1)} %bitcast.22, bf16[2,512,384]{2,1,0:T(8,128)(2,1)S(1)} %copy-done.4, bf16[2,512,384]{2,1,0:T(8,128)(2,1)} %collective-permute-done.8.rest_3_.rest_1_, ...), custom_call_target="tpu_custom_call" | custom-call | flops 3221225472 | bytes 6291456 | tf_op jit(solution)/shard_map/pallas_call | solution.py:246
  103.0 7.0 %shard_map.80 = (f32[1,256,384]{2,1,0:T(8,128)S(1)}, bf16[1,256,128]{2,1,0:T(8,128)(2,1)S(1)}) custom-call(bf16[1,272,384]{2,1,0:T(8,128)(2,1)S(1)} %get-tuple-element.78.q_ref, f32[1,4096]{1,0:T(1,128)S(1)} %bitcast.23, bf16[1,256,384]{2,1,0:T(8,128)(2,1)S(1)} %get-tuple-element.108.rest_0_, bf16[1,256,384]{2,1,0:T(8,128)(2,1)S(1)} %get-tuple-element.103.rest_1_, ...), custom_call_target="tpu_custom_call" | custom-call | flops 3221225472 | bytes 6291456 | tf_op jit(solution)/shard_map/pallas_call | solution.py:246
  113.6 2.5 %shard_map.82 = (bf16[1,32,5120]{2,1,0:T(8,128)(2,1)S(1)}, bf16[1,32,5120]{2,1,0:T(8,128)(2,1)S(1)}, bf16[1,32,5120]{2,1,0:T(8,128)(2,1)S(1)}, bf16[1,32,5120]{2,1,0:T(8,128)(2,1)S(1)}) custom-call(s32[1]{0:T(128)} %bitcast.1.core, bf16[1,128,384]{2,1,0:T(8,128)(2,1)S(1)} %get-tuple-element.84.a_ref, bf16[1,128,384]{2,1,0:T(8,128)(2,1)S(1)} %collective-permute-done.20.b_ref, ...), custom_call_target="tpu_custom_call" | custom-call | flops 1006632960 | bytes 9175040 | tf_op jit(solution)/shard_map/pallas_call | solution.py:329
  117.0 2.5 %shard_map.83 = (bf16[1,32,5120]{2,1,0:T(8,128)(2,1)S(1)}, bf16[1,32,5120]{2,1,0:T(8,128)(2,1)S(1)}, bf16[1,32,5120]{2,1,0:T(8,128)(2,1)S(1)}, bf16[1,32,5120]{2,1,0:T(8,128)(2,1)S(1)}) custom-call(s32[1]{0:T(128)} %bitcast.1.core, bf16[1,128,384]{2,1,0:T(8,128)(2,1)S(1)} %get-tuple-element.90.a_ref, bf16[1,128,384]{2,1,0:T(8,128)(2,1)S(1)} %collective-permute-done.24.b_ref, ...), custom_call_target="tpu_custom_call" | custom-call | flops 1006632960 | bytes 9175040 | tf_op jit(solution)/shard_map/pallas_call | solution.py:329
  119.5 2.7 %collective-permute-start.27 = (bf16[1,32,5120]{2,1,0:T(8,128)(2,1)S(1)}, bf16[1,32,5120]{2,1,0:T(8,128)(2,1)S(1)}, u32[]{:S(2)}, u32[]{:S(2)}) collective-permute-start(bf16[1,32,5120]{2,1,0:T(8,128)(2,1)S(1)} %get-tuple-element.96), channel_id=1, source_target_pairs={{0,3},{1,0},{2,1},{3,2},{4,7},{5,4},{6,5},{7,6},{8,9},{9,10},{10,1... | collective-permute-start | bytes 983048 | tf_op jit(solution)/shard_map/ppermute | solution.py:51
  122.3 3.2 %collective-permute-start.30 = (bf16[1,32,5120]{2,1,0:T(8,128)(2,1)S(1)}, bf16[1,32,5120]{2,1,0:T(8,128)(2,1)S(1)}, u32[]{:S(2)}, u32[]{:S(2)}) collective-permute-start(bf16[1,32,5120]{2,1,0:T(8,128)(2,1)S(1)} %get-tuple-element.98), channel_id=1, source_target_pairs={{0,1},{1,2},{2,3},{3,0},{4,5},{5,6},{6,7},{7,4},{8,11},{9,8},{10,9... | collective-permute-start | bytes 983048 | tf_op jit(solution)/shard_map/ppermute | solution.py:51
  125.5 5.4 %collective-permute-done.27 = bf16[1,32,5120]{2,1,0:T(8,128)(2,1)S(1)} collective-permute-done((bf16[1,32,5120]{2,1,0:T(8,128)(2,1)S(1)}, bf16[1,32,5120]{2,1,0:T(8,128)(2,1)S(1)}, u32[]{:S(2)}, u32[]{:S(2)}) %collective-permute-start.27) | collective-permute-done | bytes 327712 | tf_op jit(solution)/shard_map/ppermute | solution.py:51
  131.0 2.1 %collective-permute-start.28 = (bf16[1,32,5120]{2,1,0:T(8,128)(2,1)S(1)}, bf16[1,32,5120]{2,1,0:T(8,128)(2,1)S(1)}, u32[]{:S(2)}, u32[]{:S(2)}) collective-permute-start(bf16[1,32,5120]{2,1,0:T(8,128)(2,1)S(1)} %add_convert_fusion.1), channel_id=1, source_target_pairs={{0,3},{1,0},{2,1},{3,2},{4,7},{5,4},{6,5},{7,6},{8,9},{9,10},{10,1... | collective-permute-start | bytes 983048 | tf_op jit(solution)/shard_map/ppermute | solution.py:51
  133.1 4.9 %collective-permute-done.25 = bf16[1,32,5120]{2,1,0:T(8,128)(2,1)S(1)} collective-permute-done((bf16[1,32,5120]{2,1,0:T(8,128)(2,1)S(1)}, bf16[1,32,5120]{2,1,0:T(8,128)(2,1)S(1)}, u32[]{:S(2)}, u32[]{:S(2)}) %collective-permute-start.25) | collective-permute-done | bytes 327712 | tf_op jit(solution)/shard_map/ppermute | solution.py:51
  138.6 2.0 %collective-permute-done.29 = bf16[1,32,5120]{2,1,0:T(8,128)(2,1)S(1)} collective-permute-done((bf16[1,32,5120]{2,1,0:T(8,128)(2,1)S(1)}, bf16[1,32,5120]{2,1,0:T(8,128)(2,1)S(1)}, u32[]{:S(2)}, u32[]{:S(2)}) %collective-permute-start.29) | collective-permute-done | bytes 327712 | tf_op jit(solution)/shard_map/ppermute | solution.py:51
  140.6 1.3 collective-permute-done.28
  141.9 4.4 %collective-permute-done.26 = bf16[1,32,5120]{2,1,0:T(8,128)(2,1)S(1)} collective-permute-done((bf16[1,32,5120]{2,1,0:T(8,128)(2,1)S(1)}, bf16[1,32,5120]{2,1,0:T(8,128)(2,1)S(1)}, u32[]{:S(2)}, u32[]{:S(2)}) %collective-permute-start.26) | collective-permute-done | bytes 327712 | tf_op jit(solution)/shard_map/ppermute | solution.py:51
  146.4 1.2 add_convert_fusion
  (89 shorter events, 13.8 us)
Async XLA Ops:
  0.0 28.4 %copy-start.9 = (s32[2]{0:T(128)S(1)}, s32[2]{0:T(128)}, u32[]{:S(2)}) copy-start(s32[2]{0:T(128)} %param.9) | copy-start | bytes 28
  4.6 17.2 %collective-permute-start = (bf16[2,32,5120]{2,1,0:T(8,128)(2,1)}, bf16[2,32,5120]{2,1,0:T(8,128)(2,1)S(1)}, u32[]{:S(2)}, u32[]{:S(2)}) collective-permute-start(bf16[2,32,5120]{2,1,0:T(8,128)(2,1)} %get-tuple-element.53.refs_0_), channel_id=1, source_target_pairs={{0,1},{1,2},{2,3},{3,0},{4,5},{5,6},{6,7},{7,4},{8,11},{9,8},{10,9... | collective-permute-start | bytes 1966088 | tf_op jit(solution)/shard_map/ppermute | solution.py:51
  4.9 17.7 %collective-permute-start.1 = (bf16[2,32,5120]{2,1,0:T(8,128)(2,1)}, bf16[2,32,5120]{2,1,0:T(8,128)(2,1)S(1)}, u32[]{:S(2)}, u32[]{:S(2)}) collective-permute-start(bf16[2,32,5120]{2,1,0:T(8,128)(2,1)} %get-tuple-element.53.refs_0_), channel_id=1, source_target_pairs={{0,3},{1,0},{2,1},{3,2},{4,7},{5,4},{6,5},{7,6},{8,9},{9,10},{10,1... | collective-permute-start | bytes 1966088 | tf_op jit(solution)/shard_map/ppermute | solution.py:51
  6.7 20.3 %collective-permute-start.8 = (bf16[2,512,384]{2,1,0:T(8,128)(2,1)S(1)}, bf16[2,512,384]{2,1,0:T(8,128)(2,1)}, u32[]{:S(2)}, u32[]{:S(2)}) collective-permute-start(bf16[2,512,384]{2,1,0:T(8,128)(2,1)S(1)} %copy-done.4), channel_id=1, source_target_pairs={{0,16},{1,17},{2,18},{3,19},{4,20},{5,21},{6,22},{7,23},{8,56},{9,... | collective-permute-start | bytes 2359304 | tf_op jit(solution)/shard_map/ppermute | solution.py:51
  7.9 21.6 %collective-permute-start.9 = (bf16[2,512,384]{2,1,0:T(8,128)(2,1)S(1)}, bf16[2,512,384]{2,1,0:T(8,128)(2,1)}, u32[]{:S(2)}, u32[]{:S(2)}) collective-permute-start(bf16[2,512,384]{2,1,0:T(8,128)(2,1)S(1)} %copy-done.4), channel_id=1, source_target_pairs={{0,48},{1,49},{2,50},{3,51},{4,52},{5,53},{6,54},{7,55},{8,24},{9,... | collective-permute-start | bytes 2359304 | tf_op jit(solution)/shard_map/ppermute | solution.py:51
  8.8 19.6 %collective-permute-start.2 = (bf16[2,32,5120]{2,1,0:T(8,128)(2,1)}, bf16[2,32,5120]{2,1,0:T(8,128)(2,1)S(1)}, u32[]{:S(2)}, u32[]{:S(2)}) collective-permute-start(bf16[2,32,5120]{2,1,0:T(8,128)(2,1)} %get-tuple-element.53.refs_0_), channel_id=1, source_target_pairs={{0,4},{1,5},{2,6},{3,7},{4,0},{5,1},{6,2},{7,3},{8,12},{9,13},{10,... | collective-permute-start | bytes 1966088 | tf_op jit(solution)/shard_map/ppermute | solution.py:27
  21.9 13.4 %collective-permute-start.3 = (bf16[2,32,5120]{2,1,0:T(8,128)(2,1)S(1)}, bf16[2,32,5120]{2,1,0:T(8,128)(2,1)S(1)}, u32[]{:S(2)}, u32[]{:S(2)}) collective-permute-start(bf16[2,32,5120]{2,1,0:T(8,128)(2,1)S(1)} %collective-permute-done.refs_1_), channel_id=1, source_target_pairs={{0,1},{1,2},{2,3},{3,0},{4,5},{5,6},{6,7},{7,4},{8,11},{9,8},{10,9... | collective-permute-start | bytes 1966088 | tf_op jit(solution)/shard_map/ppermute | solution.py:51
  22.6 26.5 %collective-permute-start.7 = (bf16[96,5120]{1,0:T(8,128)(2,1)}, bf16[96,5120]{1,0:T(8,128)(2,1)S(1)}, u32[]{:S(2)}, u32[]{:S(2)}) collective-permute-start(bf16[96,5120]{1,0:T(8,128)(2,1)} %get-tuple-element.55), channel_id=1, source_target_pairs={{0,68},{1,69},{2,70},{3,71},{4,64},{5,65},{6,66},{7,67},{8,76},{9,... | collective-permute-start | bytes 2949128 | tf_op jit(solution)/shard_map/ppermute | solution.py:59
  27.0 22.0 %collective-permute-start.10 = (bf16[2,512,384]{2,1,0:T(8,128)(2,1)}, bf16[2,512,384]{2,1,0:T(8,128)(2,1)S(1)}, u32[]{:S(2)}, u32[]{:S(2)}) collective-permute-start(bf16[2,512,384]{2,1,0:T(8,128)(2,1)} %collective-permute-done.8.rest_3_.rest_1_), channel_id=1, source_target_pairs={{0,16},{1,17},{2,18},{3,19},{4,20},{5,21},{6,22},{7,23},{8,56},{9,... | collective-permute-start | bytes 2359304 | tf_op jit(solution)/shard_map/ppermute | solution.py:51
  28.4 21.3 %collective-permute-start.4 = (bf16[2,32,5120]{2,1,0:T(8,128)(2,1)S(1)}, bf16[2,32,5120]{2,1,0:T(8,128)(2,1)S(1)}, u32[]{:S(2)}, u32[]{:S(2)}) collective-permute-start(bf16[2,32,5120]{2,1,0:T(8,128)(2,1)S(1)} %collective-permute-done.2.refs_3_), channel_id=1, source_target_pairs={{0,1},{1,2},{2,3},{3,0},{4,5},{5,6},{6,7},{7,4},{8,11},{9,8},{10,9... | collective-permute-start | bytes 1966088 | tf_op jit(solution)/shard_map/ppermute | solution.py:51
  29.5 20.9 %collective-permute-start.5 = (bf16[2,32,5120]{2,1,0:T(8,128)(2,1)S(1)}, bf16[2,32,5120]{2,1,0:T(8,128)(2,1)S(1)}, u32[]{:S(2)}, u32[]{:S(2)}) collective-permute-start(bf16[2,32,5120]{2,1,0:T(8,128)(2,1)S(1)} %collective-permute-done.2.refs_3_), channel_id=1, source_target_pairs={{0,3},{1,0},{2,1},{3,2},{4,7},{5,4},{6,5},{7,6},{8,9},{9,10},{10,1... | collective-permute-start | bytes 1966088 | tf_op jit(solution)/shard_map/ppermute | solution.py:51
  35.3 14.3 %collective-permute-start.6 = (bf16[2,32,5120]{2,1,0:T(8,128)(2,1)S(1)}, bf16[2,32,5120]{2,1,0:T(8,128)(2,1)S(1)}, u32[]{:S(2)}, u32[]{:S(2)}) collective-permute-start(bf16[2,32,5120]{2,1,0:T(8,128)(2,1)S(1)} %collective-permute-done.3.refs_0_), channel_id=1, source_target_pairs={{0,4},{1,5},{2,6},{3,7},{4,0},{5,1},{6,2},{7,3},{8,12},{9,13},{10,... | collective-permute-start | bytes 1966088 | tf_op jit(solution)/shard_map/ppermute | solution.py:27
  49.0 11.7 %collective-permute-start.11 = (bf16[2,512,384]{2,1,0:T(8,128)(2,1)S(1)}, bf16[2,512,384]{2,1,0:T(8,128)(2,1)S(1)}, u32[]{:S(2)}, u32[]{:S(2)}) collective-permute-start(bf16[2,512,384]{2,1,0:T(8,128)(2,1)S(1)} %copy-done.4), channel_id=1, source_target_pairs={{0,8},{8,0},{16,24},{24,16},{32,40},{40,32},{48,56},{56,48},{64,72... | collective-permute-start | bytes 2359304 | tf_op jit(solution)/shard_map/ppermute | solution.py:37
  49.1 12.4 %collective-permute-start.12 = (bf16[2,512,384]{2,1,0:T(8,128)(2,1)}, bf16[2,512,384]{2,1,0:T(8,128)(2,1)S(1)}, u32[]{:S(2)}, u32[]{:S(2)}) collective-permute-start(bf16[2,512,384]{2,1,0:T(8,128)(2,1)} %collective-permute-done.8.rest_3_.rest_1_), channel_id=1, source_target_pairs={{0,8},{8,0},{16,24},{24,16},{32,40},{40,32},{48,56},{56,48},{64,72... | collective-permute-start | bytes 2359304 | tf_op jit(solution)/shard_map/ppermute | solution.py:37
  49.6 12.6 %collective-permute-start.13 = (bf16[2,512,384]{2,1,0:T(8,128)(2,1)}, bf16[2,512,384]{2,1,0:T(8,128)(2,1)S(1)}, u32[]{:S(2)}, u32[]{:S(2)}) collective-permute-start(bf16[2,512,384]{2,1,0:T(8,128)(2,1)} %collective-permute-done.9.rest_4_.rest_2_), channel_id=1, source_target_pairs={{0,8},{8,0},{16,24},{24,16},{32,40},{40,32},{48,56},{56,48},{64,72... | collective-permute-start | bytes 2359304 | tf_op jit(solution)/shard_map/ppermute | solution.py:37
  49.7 12.5 %collective-permute-start.14 = (bf16[2,512,384]{2,1,0:T(8,128)(2,1)S(1)}, bf16[2,512,384]{2,1,0:T(8,128)(2,1)S(1)}, u32[]{:S(2)}, u32[]{:S(2)}) collective-permute-start(bf16[2,512,384]{2,1,0:T(8,128)(2,1)S(1)} %collective-permute-done.10.rest_5_.rest_3_), channel_id=1, source_target_pairs={{0,8},{8,0},{16,24},{24,16},{32,40},{40,32},{48,56},{56,48},{64,72... | collective-permute-start | bytes 2359304 | tf_op jit(solution)/shard_map/ppermute | solution.py:37
  56.8 14.1 %collective-permute-start.15 = (bf16[2,272,384]{2,1,0:T(8,128)(2,1)S(1)}, bf16[2,272,384]{2,1,0:T(8,128)(2,1)S(1)}, u32[]{:S(2)}, u32[]{:S(2)}) collective-permute-start(bf16[2,272,384]{2,1,0:T(8,128)(2,1)S(1)} %broadcast_dynamic-update-slice_fusion), channel_id=1, source_target_pairs={{0,64},{8,72},{16,80},{24,88},{32,96},{40,104},{48,112},{56,120},{... | collective-permute-start | bytes 1253384 | tf_op jit(solution)/shard_map/ppermute | solution.py:37
  61.6 48.4 %collective-permute-start.17 = (bf16[48,5120]{1,0:T(8,128)(2,1)S(1)}, bf16[48,5120]{1,0:T(8,128)(2,1)S(1)}, u32[]{:S(2)}, u32[]{:S(2)}) collective-permute-start(bf16[48,5120]{1,0:T(8,128)(2,1)S(1)} %copy-done.8), channel_id=1, source_target_pairs={{0,68},{1,69},{2,70},{3,71},{4,64},{5,65},{6,66},{7,67},{8,76},{9,... | collective-permute-start | bytes 1474568 | tf_op jit(solution)/shard_map/ppermute | solution.py:59
  61.7 48.2 %collective-permute-start.18 = (bf16[48,5120]{1,0:T(8,128)(2,1)S(1)}, bf16[48,5120]{1,0:T(8,128)(2,1)S(1)}, u32[]{:S(2)}, u32[]{:S(2)}) collective-permute-start(bf16[48,5120]{1,0:T(8,128)(2,1)S(1)} %copy-done.7), channel_id=1, source_target_pairs={{0,4},{1,5},{2,6},{3,7},{4,0},{5,1},{6,2},{7,3},{8,12},{9,13},{10,... | collective-permute-start | bytes 1474568 | tf_op jit(solution)/shard_map/ppermute | solution.py:27
  62.3 50.2 %collective-permute-start.21 = (bf16[96,5120]{1,0:T(8,128)(2,1)S(1)}, bf16[96,5120]{1,0:T(8,128)(2,1)S(1)}, u32[]{:S(2)}, u32[]{:S(2)}) collective-permute-start(bf16[96,5120]{1,0:T(8,128)(2,1)S(1)} %collective-permute-done.7.rest_0_), channel_id=1, source_target_pairs={{0,8},{8,0},{16,24},{24,16},{32,40},{40,32},{48,56},{56,48},{64,72... | collective-permute-start | bytes 2949128 | tf_op jit(solution)/shard_map/ppermute | solution.py:37
  77.8 23.6 %collective-permute-start.16 = (bf16[1,256,512]{2,1,0:T(8,128)(2,1)S(1)}, bf16[1,256,512]{2,1,0:T(8,128)(2,1)S(1)}, u32[]{:S(2)}, u32[]{:S(2)}) collective-permute-start(bf16[1,256,512]{2,1,0:T(8,128)(2,1)S(1)} %shard_map.77), channel_id=1, source_target_pairs={{0,64},{8,72},{16,80},{24,88},{32,96},{40,104},{48,112},{56,120},{... | collective-permute-start | bytes 786440 | tf_op jit(solution)/shard_map/ppermute | solution.py:37
  101.3 9.7 %collective-permute-start.19 = (bf16[1,256,512]{2,1,0:T(8,128)(2,1)S(1)}, bf16[1,256,512]{2,1,0:T(8,128)(2,1)S(1)}, u32[]{:S(2)}, u32[]{:S(2)}) collective-permute-start(bf16[1,256,512]{2,1,0:T(8,128)(2,1)S(1)} %shard_map.78), channel_id=1, source_target_pairs={{0,64},{8,72},{16,80},{24,88},{32,96},{40,104},{48,112},{56,120},{... | collective-permute-start | bytes 786440 | tf_op jit(solution)/shard_map/ppermute | solution.py:37
  102.1 9.0 %collective-permute-start.20 = (bf16[1,128,384]{2,1,0:T(8,128)(2,1)S(1)}, bf16[1,128,384]{2,1,0:T(8,128)(2,1)S(1)}, u32[]{:S(2)}, u32[]{:S(2)}) collective-permute-start(bf16[1,128,384]{2,1,0:T(8,128)(2,1)S(1)} %get-tuple-element.77), channel_id=1, source_target_pairs={{0,4},{1,5},{2,6},{3,7},{4,0},{5,1},{6,2},{7,3},{8,12},{9,13},{10,... | collective-permute-start | bytes 294920 | tf_op jit(solution)/shard_map/ppermute | solution.py:27
  111.0 1.9 %collective-permute-start.22 = (bf16[48,5120]{1,0:T(8,128)(2,1)S(1)}, bf16[48,5120]{1,0:T(8,128)(2,1)S(1)}, u32[]{:S(2)}, u32[]{:S(2)}) collective-permute-start(bf16[48,5120]{1,0:T(8,128)(2,1)S(1)} %collective-permute-done.17.rest_1_), channel_id=1, source_target_pairs={{0,8},{8,0},{16,24},{24,16},{32,40},{40,32},{48,56},{56,48},{64,72... | collective-permute-start | bytes 1474568 | tf_op jit(solution)/shard_map/ppermute | solution.py:37
  111.0 2.6 %collective-permute-start.23 = (bf16[48,5120]{1,0:T(8,128)(2,1)S(1)}, bf16[48,5120]{1,0:T(8,128)(2,1)S(1)}, u32[]{:S(2)}, u32[]{:S(2)}) collective-permute-start(bf16[48,5120]{1,0:T(8,128)(2,1)S(1)} %collective-permute-done.18.rest_2_), channel_id=1, source_target_pairs={{0,8},{8,0},{16,24},{24,16},{32,40},{40,32},{48,56},{56,48},{64,72... | collective-permute-start | bytes 1474568 | tf_op jit(solution)/shard_map/ppermute | solution.py:37
  112.2 4.8 %collective-permute-start.24 = (bf16[1,128,384]{2,1,0:T(8,128)(2,1)S(1)}, bf16[1,128,384]{2,1,0:T(8,128)(2,1)S(1)}, u32[]{:S(2)}, u32[]{:S(2)}) collective-permute-start(bf16[1,128,384]{2,1,0:T(8,128)(2,1)S(1)} %get-tuple-element.83), channel_id=1, source_target_pairs={{0,4},{1,5},{2,6},{3,7},{4,0},{5,1},{6,2},{7,3},{8,12},{9,13},{10,... | collective-permute-start | bytes 294920 | tf_op jit(solution)/shard_map/ppermute | solution.py:27
  119.5 11.3 %collective-permute-start.27 = (bf16[1,32,5120]{2,1,0:T(8,128)(2,1)S(1)}, bf16[1,32,5120]{2,1,0:T(8,128)(2,1)S(1)}, u32[]{:S(2)}, u32[]{:S(2)}) collective-permute-start(bf16[1,32,5120]{2,1,0:T(8,128)(2,1)S(1)} %get-tuple-element.96), channel_id=1, source_target_pairs={{0,3},{1,0},{2,1},{3,2},{4,7},{5,4},{6,5},{7,6},{8,9},{9,10},{10,1... | collective-permute-start | bytes 983048 | tf_op jit(solution)/shard_map/ppermute | solution.py:51
  122.3 15.7 %collective-permute-start.25 = (bf16[1,32,5120]{2,1,0:T(8,128)(2,1)S(1)}, bf16[1,32,5120]{2,1,0:T(8,128)(2,1)S(1)}, u32[]{:S(2)}, u32[]{:S(2)}) collective-permute-start(bf16[1,32,5120]{2,1,0:T(8,128)(2,1)S(1)} %get-tuple-element.94), channel_id=1, source_target_pairs={{0,3},{1,0},{2,1},{3,2},{4,7},{5,4},{6,5},{7,6},{8,9},{9,10},{10,1... | collective-permute-start | bytes 983048 | tf_op jit(solution)/shard_map/ppermute | solution.py:51
  122.3 16.3 %collective-permute-start.30 = (bf16[1,32,5120]{2,1,0:T(8,128)(2,1)S(1)}, bf16[1,32,5120]{2,1,0:T(8,128)(2,1)S(1)}, u32[]{:S(2)}, u32[]{:S(2)}) collective-permute-start(bf16[1,32,5120]{2,1,0:T(8,128)(2,1)S(1)} %get-tuple-element.98), channel_id=1, source_target_pairs={{0,1},{1,2},{2,3},{3,0},{4,5},{5,6},{6,7},{7,4},{8,11},{9,8},{10,9... | collective-permute-start | bytes 983048 | tf_op jit(solution)/shard_map/ppermute | solution.py:51
  125.5 15.2 %collective-permute-start.29 = (bf16[1,32,5120]{2,1,0:T(8,128)(2,1)S(1)}, bf16[1,32,5120]{2,1,0:T(8,128)(2,1)S(1)}, u32[]{:S(2)}, u32[]{:S(2)}) collective-permute-start(bf16[1,32,5120]{2,1,0:T(8,128)(2,1)S(1)} %get-tuple-element.97), channel_id=1, source_target_pairs={{0,1},{1,2},{2,3},{3,0},{4,5},{5,6},{6,7},{7,4},{8,11},{9,8},{10,9... | collective-permute-start | bytes 983048 | tf_op jit(solution)/shard_map/ppermute | solution.py:51
  131.0 11.0 %collective-permute-start.28 = (bf16[1,32,5120]{2,1,0:T(8,128)(2,1)S(1)}, bf16[1,32,5120]{2,1,0:T(8,128)(2,1)S(1)}, u32[]{:S(2)}, u32[]{:S(2)}) collective-permute-start(bf16[1,32,5120]{2,1,0:T(8,128)(2,1)S(1)} %add_convert_fusion.1), channel_id=1, source_target_pairs={{0,3},{1,0},{2,1},{3,2},{4,7},{5,4},{6,5},{7,6},{8,9},{9,10},{10,1... | collective-permute-start | bytes 983048 | tf_op jit(solution)/shard_map/ppermute | solution.py:51
  138.0 8.4 %collective-permute-start.26 = (bf16[1,32,5120]{2,1,0:T(8,128)(2,1)S(1)}, bf16[1,32,5120]{2,1,0:T(8,128)(2,1)S(1)}, u32[]{:S(2)}, u32[]{:S(2)}) collective-permute-start(bf16[1,32,5120]{2,1,0:T(8,128)(2,1)S(1)} %add_convert_fusion.2), channel_id=1, source_target_pairs={{0,3},{1,0},{2,1},{3,2},{4,7},{5,4},{6,5},{7,6},{8,9},{9,10},{10,1... | collective-permute-start | bytes 983048 | tf_op jit(solution)/shard_map/ppermute | solution.py:51
  (9 other events, 78.5 us)
